TPU v7x, 32 devices: a whole 2x2x4 slice. The times are simulated.
32 devices in a mesh: pipe: 4 (over z), tensor: 4 (over y, x), dp: 2 (over core).
Axes of the slice: x: 2, y: 2, z: 4, core: 2. Of those that a mesh axis runs over, the one named last changes fastest.
Arguments:
- entry_grads: float32 [2, 4, 64, 3584], P(None, 'pipe', ('dp', 'tensor')), may hold values from -6 to 6
- fresh_grads: float32 [2, 2, 64, 3584], P(None, None, ('dp', 'tensor')), may hold values from -6 to 6
- saved_inputs: bfloat16 [2, 3, 4, 64, 3584], P(None, None, 'pipe', 'dp'), may hold values from -6 to 6
- w_in: bfloat16 [2, 4, 3584, 2048], P(None, 'pipe', None, 'tensor'), may hold values from -0.09375 to 0.09375
- w_down: bfloat16 [2, 4, 1024, 3584], P(None, 'pipe', 'tensor'), may hold values from -0.1875 to 0.1875
Outputs:
- hand_offs: float32 [2, 3, 4, 64, 3584], P(None, None, 'pipe', ('dp', 'tensor'))
- grad_w_in: float32 [2, 4, 3584, 2048], P(None, 'pipe', 'dp', 'tensor')
- grad_w_down: float32 [2, 4, 1024, 3584], P(None, 'pipe', 'tensor', 'dp')
All inputs are finite; a program needn't handle non-finite values.
Results may differ from a plain program's by a relative error of at most 0.02.
Values may be sent and summed in bfloat16 or wider, within the bound.
No kernel may reach another device: no remote copies, remote signals or barrier semaphores. Data moves between devices by JAX's collectives and lax.ppermute only.
A program may use at most 128 MiB of HBM per device.

v0:
```python
import jax
import jax.numpy as jnp
from jax import lax
from jax.sharding import PartitionSpec as P


def extended_2(cells, sides, width):
    for axis, dim in sides:
        count = lax.axis_size(axis)
        ends = count - 1
        head = lax.slice_in_dim(cells, 0, width, axis=dim)
        tail = lax.slice_in_dim(cells, cells.shape[dim] - width, cells.shape[dim], axis=dim)
        cells = jnp.concatenate(
            [
                lax.ppermute(tail, axis, [(i, (i + 1) % count) for i in range(ends)]),
                cells,
                lax.ppermute(head, axis, [((i + 1) % count, i) for i in range(ends)]),
            ],
            axis=dim,
        )
    return cells


def block_local(inputs, dy_rows, w_in_local, w_down_local):
    hidden_width = w_down_local.shape[0]
    projected = jnp.dot(inputs, w_in_local, preferred_element_type=jnp.float32)
    gate_part = projected[:, :hidden_width]
    up_part = projected[:, hidden_width:]
    sigmoid_val = jax.nn.sigmoid(gate_part)
    activated = gate_part * sigmoid_val
    hidden = (activated * up_part).astype(jnp.bfloat16)
    hidden_grad = jnp.einsum("rd,hd->rh", dy_rows, w_down_local, preferred_element_type=jnp.float32)
    gate_grad = hidden_grad * up_part * sigmoid_val * (1.0 + gate_part * (1.0 - sigmoid_val))
    up_grad = hidden_grad * activated
    pre_grad = jnp.concatenate([gate_grad, up_grad], axis=1).astype(jnp.bfloat16)
    return (hidden, pre_grad)


def local(entry_grads, fresh_grads, saved_inputs, w_in, w_down):
    section_index = lax.axis_index("pipe")
    sections = lax.axis_size("pipe")
    tensor_count = lax.axis_size("tensor")
    w_in_local = w_in[:, 0]
    w_down_local = w_down[:, 0]
    saved_rows = saved_inputs[:, :, 0]
    window_steps = saved_rows.shape[1]
    batch_rows = saved_rows.shape[2]
    width = saved_rows.shape[3]
    shard_rows = batch_rows // tensor_count
    hidden_width = w_down_local.shape[1]
    at_upper = (section_index == sections - 1).astype(jnp.float32)
    at_lower = (section_index == 0).astype(jnp.float32)
    in_accum = jnp.zeros((2, width, 2 * hidden_width), jnp.float32)
    down_accum = jnp.zeros((2, width, hidden_width), jnp.float32)
    handed_list = []
    handed = None
    for window_step in range(window_steps):
        if window_step == 0:
            incoming = entry_grads[:, 0]
        else:
            extended = extended_2(handed.astype(jnp.bfloat16), (("pipe", 0),), 1).astype(
                handed.dtype
            )
            incoming = jnp.stack(
                [
                    extended[3] + at_upper * fresh_grads[0, window_step - 1],
                    extended[0] + at_lower * fresh_grads[1, window_step - 1],
                ]
            )
        dy_full = lax.all_gather(incoming.astype(jnp.bfloat16), "tensor", axis=1, tiled=True)
        hidden_first, pre_first = block_local(
            saved_rows[0, window_step], dy_full[0], w_in_local[0], w_down_local[0]
        )
        hidden_second, pre_second = block_local(
            saved_rows[1, window_step], dy_full[1], w_in_local[1], w_down_local[1]
        )
        hidden_pair = jnp.stack([hidden_first, hidden_second])
        pre_pair = jnp.stack([pre_first, pre_second])

        def term_rows(first_row, row_count, pre_pair=pre_pair):
            rows_first = pre_pair[0]
            rows_second = pre_pair[1]
            part_first = jnp.einsum(
                "rc,dc->rd", rows_first, w_in_local[0], preferred_element_type=jnp.float32
            )
            part_second = jnp.einsum(
                "rc,dc->rd", rows_second, w_in_local[1], preferred_element_type=jnp.float32
            )
            return jnp.concatenate([part_first, part_second], axis=1)

        summed = lax.psum_scatter(
            term_rows(jnp.int32(0), shard_rows * lax.axis_size("tensor")).astype(jnp.bfloat16),
            "tensor",
            scatter_dimension=0,
            tiled=True,
        ).astype(jnp.float32)
        summed = jnp.moveaxis(summed.reshape(shard_rows, 2, width), 1, 0)
        handed = incoming + summed
        handed_list.append(handed)
        in_accum = in_accum + jnp.einsum(
            "nrd,nrc->ndc", saved_rows[:, window_step], pre_pair, preferred_element_type=jnp.float32
        )
        down_accum = down_accum + jnp.einsum(
            "nrd,nrh->ndh", dy_full, hidden_pair, preferred_element_type=jnp.float32
        )
    combined = jnp.concatenate([in_accum, down_accum], axis=2)
    reduced = lax.psum_scatter(
        combined.astype(jnp.bfloat16), "dp", scatter_dimension=1, tiled=True
    ).astype(jnp.float32)
    grad_w_in = reduced[:, :, : 2 * hidden_width][:, None]
    grad_w_down = jnp.swapaxes(reduced[:, :, 2 * hidden_width :], 1, 2)[:, None]
    hand_offs = jnp.stack(handed_list, axis=1)[:, :, None]
    return (hand_offs, grad_w_in, grad_w_down)


def solution(mesh):
    placed = (
        P(None, "pipe", ("dp", "tensor"), None),
        P(None, None, ("dp", "tensor"), None),
        P(None, None, "pipe", "dp", None),
        P(None, "pipe", None, "tensor"),
        P(None, "pipe", "tensor", None),
    )
    return jax.shard_map(
        local,
        mesh=mesh,
        in_specs=placed,
        out_specs=(
            P(None, None, "pipe", ("dp", "tensor"), None),
            P(None, "pipe", "dp", "tensor"),
            P(None, "pipe", "tensor", "dp"),
        ),
        check_vma=False,
    )
```

profile of v0, /device:TPU:0, one launch (start us, length us, event | category | flops | bytes accessed | tf_op | source)
XLA Modules:
  0.0 272.8 jit_solution(10033028716409904416)
XLA Ops:
  7.2 1.4 copy.17
  8.7 3.3 %fusion.19 = f32[32,512]{1,0:T(8,128)S(1)} fusion(bf16[2,1,3584,512]{3,2,1,0:T(8,128)(2,1)} %param.8, bf16[2,3,32,3584]{3,2,0,1:T(8,128)(2,1)S(1)} %bitcast.211), kind=kOutput, calls=%fused_computation.30 | convolution fusion | flops 117440512 | bytes 3964928 | tf_op jit(solution)/shard_map/dot_general | solution.py:26
  12.0 3.4 %fusion.10 = f32[32,512]{1,0:T(8,128)S(1)} fusion(bf16[2,1,3584,512]{3,2,1,0:T(8,128)(2,1)} %param.8, bf16[2,3,32,3584]{3,2,0,1:T(8,128)(2,1)S(1)} %bitcast.212), kind=kOutput, calls=%fused_computation.21 | convolution fusion | flops 117440512 | bytes 3964928 | tf_op jit(solution)/shard_map/dot_general | solution.py:26
  15.5 11.2 %all_gather.9 = bf16[2,32,3584]{2,1,0:T(8,128)(2,1)S(1)} all-gather(bf16[2,8,3584]{2,1,0:T(8,128)(2,1)S(1)} %bitcast_convert_fusion), channel_id=1, replica_groups=mesh['pipe'=4,'tensor'=4,'dp'=2] {'tensor'}, dimensions={1}, use_global_device_ids=true | all-gather | bytes 573440 | tf_op jit(solution)/shard_map/all_gather | solution.py:70
  28.0 1.2 convolution_convert_fusion.5
  29.2 1.2 convolution_convert_fusion.4
  30.4 0.8 pad_maximum_fusion.1
  31.2 3.4 %fusion.16 = f32[32,512]{1,0:T(8,128)} fusion(bf16[2,1,3584,512]{3,2,1,0:T(8,128)(2,1)} %param.8, bf16[2,3,32,3584]{3,2,0,1:T(8,128)(2,1)S(1)} %bitcast.213), kind=kOutput, calls=%fused_computation.27 | convolution fusion | flops 117440512 | bytes 3964928 | tf_op jit(solution)/shard_map/dot_general | solution.py:26
  34.6 3.5 %fusion.7 = f32[32,512]{1,0:T(8,128)} fusion(bf16[2,1,3584,512]{3,2,1,0:T(8,128)(2,1)} %param.8, bf16[2,3,32,3584]{3,2,0,1:T(8,128)(2,1)S(1)} %bitcast.214), kind=kOutput, calls=%fused_computation.18 | convolution fusion | flops 117440512 | bytes 3964928 | tf_op jit(solution)/shard_map/dot_general | solution.py:26
  38.2 7.3 %fusion.52 = f32[2,512,3584]{2,1,0:T(8,128)} fusion(bf16[2,3,32,3584]{3,2,0,1:T(8,128)(2,1)S(1)} %bitcast.215, bf16[1,32,256]{2,1,0:T(8,128)(2,1)S(1)} %bitcast.234, bf16[1,32,256]{2,1,0:T(8,128)(2,1)S(1)} %bitcast.233, bf16[1,32,256]{2,1,0:T(8,128)(2,1)S(1)} %bitcast.228, bf16[1,32,256]{2,1,0:T(8,128)(2,1)S(1)} %bitcast.227), kind=kOutput, calls=%fused_computation.68 | convolution fusion | flops 235143168 | bytes 15204352 | tf_op jit(solution)/shard_map/nrd,nrc->ndc/dot_general | solution.py:100
  45.5 1.4 fusion.13
  48.1 4.1 %fusion.102 = f32[2,256,3584]{2,1,0:T(8,128)} fusion(bf16[2,32,3584]{2,1,0:T(8,128)(2,1)S(1)} %all_gather.9, bf16[1,32,256]{2,1,0:T(8,128)(2,1)S(1)} %get-tuple-element.36, bf16[1,32,256]{2,1,0:T(8,128)(2,1)S(1)} %get-tuple-element.35), kind=kOutput, calls=%fused_computation.147 | convolution fusion | flops 117456896 | bytes 7831552 | tf_op jit(solution)/shard_map/nrd,nrh->ndh/dot_general | solution.py:103
  52.2 24.1 %all-reduce.7.cloned.1.call-done = bf16[32,7168]{1,0:T(8,128)(2,1)} async-done(((bf16[32,7168]{1,0:T(8,128)(2,1)}), bf16[32,7168]{1,0:T(8,128)(2,1)}) %all-reduce.7.cloned.1.call-update) | async-done | bytes 458768
  76.3 0.9 constant_dynamic-slice_fusion.2
  77.2 0.7 fusion.60
  78.0 3.4 %collective-permute-start = (bf16[1,8,3584]{2,1,0:T(8,128)(2,1)S(1)}, bf16[1,8,3584]{2,1,0:T(8,128)(2,1)S(1)}, u32[]{:S(2)}, u32[]{:S(2)}) collective-permute-start(bf16[1,8,3584]{2,1,0:T(8,128)(2,1)S(1)} %get-tuple-element.19), channel_id=1, source_target_pairs={{0,8},{8,16},{16,24},{1,9},{9,17},{17,25},{2,10},{10,18},{18,26},{... | collective-permute-start | bytes 172040 | tf_op jit(solution)/shard_map/ppermute | solution.py:15
  81.4 1.3 collective-permute-start.1
  82.7 3.6 %fusion.4 = f32[32,512]{1,0:T(8,128)} fusion(bf16[2,1,3584,512]{3,2,1,0:T(8,128)(2,1)} %param.8, bf16[2,3,32,3584]{3,2,0,1:T(8,128)(2,1)} %bitcast.217), kind=kOutput, calls=%fused_computation.15 | convolution fusion | flops 117440512 | bytes 3964928 | tf_op jit(solution)/shard_map/dot_general | solution.py:26
  86.3 1.2 collective-permute-done.1
  87.5 1.0 convert_add_fusion.1
  88.5 10.0 %all_gather.10 = bf16[2,32,3584]{2,1,0:T(8,128)(2,1)S(1)} all-gather(bf16[2,8,3584]{2,1,0:T(8,128)(2,1)S(1)} %fusion.58), channel_id=1, replica_groups=mesh['pipe'=4,'tensor'=4,'dp'=2] {'tensor'}, dimensions={1}, use_global_device_ids=true | all-gather | bytes 573440 | tf_op jit(solution)/shard_map/all_gather | solution.py:70
  98.5 2.3 fusion.29
  100.9 1.5 multiply_convert_fusion.11
  102.3 3.2 %convolution_convert_fusion.3 = bf16[32,3584]{1,0:T(8,128)(2,1)S(1)} fusion(bf16[2,1,3584,512]{3,2,1,0:T(8,128)(2,1)} %param.8, bf16[32,256]{1,0:T(8,128)(2,1)S(1)} %get-tuple-element.40, bf16[32,256]{1,0:T(8,128)(2,1)S(1)} %get-tuple-element.41), kind=kOutput, calls=%fused_computation.10 | convolution fusion | flops 117620736 | bytes 3932160 | tf_op jit(solution)/shard_map/rc,dc->rd/dot_general | solution.py:83
  105.6 1.2 convolution_convert_fusion.2
  106.7 0.8 pad_maximum_fusion.2
  107.6 8.3 %fusion.51 = f32[2,512,3584]{2,1,0:T(8,128)} fusion(bf16[2,3,32,3584]{3,2,0,1:T(8,128)(2,1)} %bitcast.218, bf16[1,32,256]{2,1,0:T(8,128)(2,1)S(1)} %bitcast.230, bf16[1,32,256]{2,1,0:T(8,128)(2,1)S(1)} %bitcast.229, bf16[1,32,256]{2,1,0:T(8,128)(2,1)S(1)} %bitcast.231, bf16[1,32,256]{2,1,0:T(8,128)(2,1)S(1)} %bitcast.232), kind=kOutput, calls=%fused_computation.66 | convolution fusion | flops 235143168 | bytes 15204352 | tf_op jit(solution)/shard_map/nrd,nrc->ndc/dot_general | solution.py:100
  116.0 37.7 %all-reduce.9.cloned.1.call-done = bf16[32,7168]{1,0:T(8,128)(2,1)} async-done(((bf16[32,7168]{1,0:T(8,128)(2,1)}), bf16[32,7168]{1,0:T(8,128)(2,1)}) %all-reduce.9.cloned.1.call-update) | async-done | bytes 458768
  153.7 0.9 constant_dynamic-slice_fusion.1
  154.6 3.4 %collective-permute-start.2 = (bf16[1,8,3584]{2,1,0:T(8,128)(2,1)S(1)}, bf16[1,8,3584]{2,1,0:T(8,128)(2,1)S(1)}, u32[]{:S(2)}, u32[]{:S(2)}) collective-permute-start(bf16[1,8,3584]{2,1,0:T(8,128)(2,1)S(1)} %get-tuple-element.17), channel_id=1, source_target_pairs={{0,8},{8,16},{16,24},{1,9},{9,17},{17,25},{2,10},{10,18},{18,26},{... | collective-permute-start | bytes 172040 | tf_op jit(solution)/shard_map/ppermute | solution.py:15
  158.0 1.3 collective-permute-start.3
  159.4 4.9 %fusion.106 = f32[2,3584,256]{1,2,0:T(8,128)} fusion(bf16[2,32,3584]{2,1,0:T(8,128)(2,1)S(1)} %copy-done.2, bf16[1,32,256]{2,1,0:T(8,128)(2,1)S(1)} %get-tuple-element.38, bf16[1,32,256]{2,1,0:T(8,128)(2,1)S(1)} %get-tuple-element.39), kind=kOutput, calls=%fused_computation.151 | convolution fusion | flops 117456896 | bytes 7831552 | tf_op jit(solution)/shard_map/nrd,nrh->ndh/dot_general | solution.py:103
  164.3 10.8 %all_gather.11 = bf16[2,32,3584]{2,1,0:T(8,128)(2,1)S(1)} all-gather(bf16[2,8,3584]{2,1,0:T(8,128)(2,1)S(1)} %fusion.57), channel_id=1, replica_groups=mesh['pipe'=4,'tensor'=4,'dp'=2] {'tensor'}, dimensions={1}, use_global_device_ids=true | all-gather | bytes 573440 | tf_op jit(solution)/shard_map/all_gather | solution.py:70
  175.1 2.1 multiply_convert_fusion.9
  178.0 1.2 convolution_convert_fusion.1
  179.1 1.2 convolution_convert_fusion
  180.3 0.8 pad_maximum_fusion.3
  181.2 8.2 %fusion.1 = bf16[2,3584,256]{1,2,0:T(8,128)(2,1)} fusion(f32[2,3584,256]{1,2,0:T(8,128)} %fusion.106, f32[2,256,3584]{2,1,0:T(8,128)} %fusion.102, bf16[2,32,3584]{2,1,0:T(8,128)(2,1)S(1)} %all_gather.11, bf16[1,32,256]{2,1,0:T(8,128)(2,1)S(1)} %get-tuple-element.34, bf16[1,32,256]{2,1,0:T(8,128)(2,1)S(1)} %get-tuple-element.33), kind=kOutput, calls=%fused_computation.5 | convolution fusion | flops 122961920 | bytes 18841600 | tf_op jit(solution)/shard_map/nrd,nrh->ndh/dot_general | solution.py:103
  189.3 14.0 %fusion.2 = bf16[2,3584,512]{1,2,0:T(8,128)(2,1)} fusion(f32[2,512,3584]{2,1,0:T(8,128)} %fusion.52, f32[2,512,3584]{2,1,0:T(8,128)} %fusion.51, bf16[2,3,32,3584]{3,2,0,1:T(8,128)(2,1)} %bitcast.219, bf16[1,32,256]{2,1,0:T(8,128)(2,1)S(1)} %bitcast.226, bf16[1,32,256]{2,1,0:T(8,128)(2,1)S(1)} %bitcast.225, bf16[1,32,256]{2,1,0:T(8,128)(2,1)S(1)} %bitcast.224, ...), kind=kOutput, calls=%fused_computation.6 | convolution fusion | flops 246153216 | bytes 37224448 | tf_op jit(solution)/shard_map/nrd,nrc->ndc/dot_general | solution.py:100
  203.3 12.7 %pad_maximum_fusion = bf16[2,3584,768]{1,2,0:T(8,128)(2,1)} fusion(bf16[2,3584,256]{1,2,0:T(8,128)(2,1)} %fusion.1, bf16[2,3584,512]{1,2,0:T(8,128)(2,1)} %fusion.2), kind=kLoop, calls=%fused_computation.1 | loop fusion | flops 22020096 | bytes 22020096 | tf_op jit(solution)/shard_map/concatenate | solution.py:106
  216.0 11.2 %all-reduce.11.cloned.1.call-done = bf16[32,7168]{1,0:T(8,128)(2,1)} async-done(((bf16[32,7168]{1,0:T(8,128)(2,1)}), bf16[32,7168]{1,0:T(8,128)(2,1)}) %all-reduce.11.cloned.1.call-update) | async-done | bytes 458768
  227.1 0.9 constant_dynamic-slice_fusion
  228.1 0.9 copy.13
  229.0 20.0 %reduce-scatter.2.cloned.1.call-done = bf16[2,1792,768]{1,2,0:T(8,128)(2,1)} async-done(((bf16[2,3584,768]{1,2,0:T(8,128)(2,1)}), bf16[2,1792,768]{1,2,0:T(8,128)(2,1)}) %reduce-scatter.2.cloned.1.call-update) | async-done | bytes 5505040 | tf_op jit(solution)/shard_map/reduce_scatter | solution.py:107
  249.0 3.4 %convert_element_type.118 = f32[2,1792,768]{1,2,0:T(8,128)S(1)} convert(bf16[2,1792,768]{1,2,0:T(8,128)(2,1)} %reduce-scatter.2.cloned.1.call-done) | non-fusion elementwise | flops 2752512 | bytes 16515072 | tf_op jit(solution)/shard_map/convert_element_type | solution.py:109
  252.4 3.4 %slice_bitcast_fusion = f32[2,1,1792,512]{2,3,0,1:T(8,128)} fusion(f32[2,1792,768]{1,2,0:T(8,128)S(1)} %convert_element_type.118), kind=kLoop, calls=%fused_computation.2 | loop fusion | bytes 14680064 | tf_op jit(solution)/shard_map/broadcast_in_dim | solution.py:110
  255.8 2.1 slice_bitcast_fusion.1
  257.9 8.4 %copy.14 = f32[2,1,1792,512]{3,2,1,0:T(8,128)} copy(f32[2,1,1792,512]{2,3,0,1:T(8,128)} %slice_bitcast_fusion) | data formatting | bytes 14680064
  (68 shorter events, 3.1 us)
Async XLA Ops:
  7.2 69.2 %all-reduce.7.cloned.1.call-start = ((), (), s32[]{:S(2)}) async-start(), calls=%async_computation.2 | async-start | bytes 917504
  8.6 36.8 %copy-start = (bf16[2,3,1,32,3584]{4,3,0,1,2:T(8,128)(2,1)}, bf16[2,3,1,32,3584]{4,3,0,1,2:T(8,128)(2,1)S(1)}, u32[]{:S(2)}) copy-start(bf16[2,3,1,32,3584]{4,3,0,1,2:T(8,128)(2,1)S(1)} %copy.17) | copy-start | bytes 4128772
  8.7 6.8 %copy-start.3 = (f32[2,1,8,3584]{3,2,1,0:T(8,128)S(1)}, f32[2,1,8,3584]{3,2,1,0:T(8,128)}, u32[]{:S(2)}) copy-start(f32[2,1,8,3584]{3,2,1,0:T(8,128)} %param.5) | copy-start | bytes 688132
  8.7 18.0 %copy-start.6 = (bf16[2,1,256,3584]{3,2,1,0:T(8,128)(2,1)S(1)}, bf16[2,1,256,3584]{3,2,1,0:T(8,128)(2,1)}, u32[]{:S(2)}) copy-start(bf16[2,1,256,3584]{3,2,1,0:T(8,128)(2,1)} %param.9) | copy-start | bytes 11010052
  8.7 19.3 %slice-start = ((s8[7340032]{0:T(1024)(128)(4,1)}), s8[4194304]{0:T(1024)(128)(4,1)S(1)}, s32[]{:S(2)}) async-start(s8[7340032]{0:T(1024)(128)(4,1)} %bitcast.203), calls=%async_computation.5 | async-start | bytes 8388608
  12.0 16.0 %slice-start.1 = ((s8[7340032]{0:T(1024)(128)(4,1)}), s8[3145728]{0:T(1024)(128)(4,1)S(1)}, s32[]{:S(2)}) async-start(s8[7340032]{0:T(1024)(128)(4,1)} %bitcast.203), calls=%async_computation.6 | async-start | bytes 6291456
  31.2 122.5 %all-reduce.9.cloned.1.call-start = ((), (), s32[]{:S(2)}) async-start(), calls=%async_computation.3 | async-start | bytes 917504
  34.6 10.9 %slice-start.2 = ((s8[7340032]{0:T(1024)(128)(4,1)}), s8[4194304]{0:T(1024)(128)(4,1)S(1)}, s32[]{:S(2)}) async-start(s8[7340032]{0:T(1024)(128)(4,1)} %bitcast.205), calls=%async_computation.7 | async-start | bytes 8388608
  38.2 7.3 %slice-start.3 = ((s8[7340032]{0:T(1024)(128)(4,1)}), s8[3145728]{0:T(1024)(128)(4,1)S(1)}, s32[]{:S(2)}) async-start(s8[7340032]{0:T(1024)(128)(4,1)} %bitcast.205), calls=%async_computation.8 | async-start | bytes 6291456
  45.5 1.4 copy-start.9
  78.0 8.4 %collective-permute-start = (bf16[1,8,3584]{2,1,0:T(8,128)(2,1)S(1)}, bf16[1,8,3584]{2,1,0:T(8,128)(2,1)S(1)}, u32[]{:S(2)}, u32[]{:S(2)}) collective-permute-start(bf16[1,8,3584]{2,1,0:T(8,128)(2,1)S(1)} %get-tuple-element.19), channel_id=1, source_target_pairs={{0,8},{8,16},{16,24},{1,9},{9,17},{17,25},{2,10},{10,18},{18,26},{... | collective-permute-start | bytes 172040 | tf_op jit(solution)/shard_map/ppermute | solution.py:15
  81.4 6.2 %collective-permute-start.1 = (bf16[1,8,3584]{2,1,0:T(8,128)(2,1)S(1)}, bf16[1,8,3584]{2,1,0:T(8,128)(2,1)}, u32[]{:S(2)}, u32[]{:S(2)}) collective-permute-start(bf16[1,8,3584]{2,1,0:T(8,128)(2,1)S(1)} %get-tuple-element.20), channel_id=1, source_target_pairs={{8,0},{16,8},{24,16},{9,1},{17,9},{25,17},{10,2},{18,10},{26,18},{... | collective-permute-start | bytes 172040 | tf_op jit(solution)/shard_map/ppermute | solution.py:17
  82.7 22.9 %slice-start.4 = ((s8[7340032]{0:T(1024)(128)(4,1)}), s8[3145728]{0:T(1024)(128)(4,1)S(1)}, s32[]{:S(2)}) async-start(s8[7340032]{0:T(1024)(128)(4,1)} %bitcast.207), calls=%async_computation.9 | async-start | bytes 6291456
  86.3 14.6 %copy-start.7 = (bf16[2,1,256,3584]{3,2,1,0:T(8,128)(2,1)S(1)}, bf16[2,1,256,3584]{3,2,1,0:T(8,128)(2,1)}, u32[]{:S(2)}) copy-start(bf16[2,1,256,3584]{3,2,1,0:T(8,128)(2,1)} %param.9) | copy-start | bytes 11010052
  98.5 2.4 copy-start.1
  98.5 7.1 %slice-start.5 = ((s8[7340032]{0:T(1024)(128)(4,1)}), s8[4194304]{0:T(1024)(128)(4,1)S(1)}, s32[]{:S(2)}) async-start(s8[7340032]{0:T(1024)(128)(4,1)} %bitcast.207), calls=%async_computation.10 | async-start | bytes 8388608
  107.6 119.6 %all-reduce.11.cloned.1.call-start = ((), (), s32[]{:S(2)}) async-start(), calls=%async_computation.4 | async-start | bytes 917504
  107.6 51.7 %copy-start.2 = (bf16[2,32,3584]{2,1,0:T(8,128)(2,1)S(1)}, bf16[2,32,3584]{2,1,0:T(8,128)(2,1)}, u32[]{:S(2)}) copy-start(bf16[2,32,3584]{2,1,0:T(8,128)(2,1)} %copy-done.1) | copy-start | bytes 1376260
  154.6 9.6 %collective-permute-start.2 = (bf16[1,8,3584]{2,1,0:T(8,128)(2,1)S(1)}, bf16[1,8,3584]{2,1,0:T(8,128)(2,1)S(1)}, u32[]{:S(2)}, u32[]{:S(2)}) collective-permute-start(bf16[1,8,3584]{2,1,0:T(8,128)(2,1)S(1)} %get-tuple-element.17), channel_id=1, source_target_pairs={{0,8},{8,16},{16,24},{1,9},{9,17},{17,25},{2,10},{10,18},{18,26},{... | collective-permute-start | bytes 172040 | tf_op jit(solution)/shard_map/ppermute | solution.py:15
  158.0 6.2 %collective-permute-start.3 = (bf16[1,8,3584]{2,1,0:T(8,128)(2,1)S(1)}, bf16[1,8,3584]{2,1,0:T(8,128)(2,1)S(1)}, u32[]{:S(2)}, u32[]{:S(2)}) collective-permute-start(bf16[1,8,3584]{2,1,0:T(8,128)(2,1)S(1)} %get-tuple-element.18), channel_id=1, source_target_pairs={{8,0},{16,8},{24,16},{9,1},{17,9},{25,17},{10,2},{18,10},{26,18},{... | collective-permute-start | bytes 172040 | tf_op jit(solution)/shard_map/ppermute | solution.py:17
  159.3 18.6 %slice-start.6 = ((s8[7340032]{0:T(1024)(128)(4,1)}), s8[4194304]{0:T(1024)(128)(4,1)S(1)}, s32[]{:S(2)}) async-start(s8[7340032]{0:T(1024)(128)(4,1)} %bitcast.209), calls=%async_computation.11 | async-start | bytes 8388608
  159.3 4.9 %copy-start.5 = (f32[2,2,8,3584]{3,2,1,0:T(8,128)S(1)}, f32[2,2,8,3584]{3,2,1,0:T(8,128)}, u32[]{:S(2)}) copy-start(f32[2,2,8,3584]{3,2,1,0:T(8,128)} %param.6) | copy-start | bytes 1376260
  159.3 15.8 %copy-start.10 = (f32[32,512]{1,0:T(8,128)S(1)}, f32[32,512]{1,0:T(8,128)}, u32[]{:S(2)}) copy-start(f32[32,512]{1,0:T(8,128)} %fusion.13) | copy-start | bytes 196612
  159.3 18.6 %slice-start.7 = ((s8[7340032]{0:T(1024)(128)(4,1)}), s8[3145728]{0:T(1024)(128)(4,1)S(1)}, s32[]{:S(2)}) async-start(s8[7340032]{0:T(1024)(128)(4,1)} %bitcast.209), calls=%async_computation.12 | async-start | bytes 6291456
  164.2 13.0 %copy-start.8 = (bf16[2,1,256,3584]{3,2,1,0:T(8,128)(2,1)S(1)}, bf16[2,1,256,3584]{3,2,1,0:T(8,128)(2,1)}, u32[]{:S(2)}) copy-start(bf16[2,1,256,3584]{3,2,1,0:T(8,128)(2,1)} %param.9) | copy-start | bytes 11010052
  164.2 13.0 %copy-start.11 = (f32[32,512]{1,0:T(8,128)S(1)}, f32[32,512]{1,0:T(8,128)}, u32[]{:S(2)}) copy-start(f32[32,512]{1,0:T(8,128)} %fusion.4) | copy-start | bytes 196612
  181.1 67.9 %reduce-scatter.2.cloned.1.call-start = ((), (), s32[]{:S(2)}) async-start(), calls=%async_computation.1 | async-start | bytes 16515072 | tf_op jit(solution)/shard_map/reduce_scatter | solution.py:107
  215.9 12.1 %copy-start.4 = (f32[2,1,8,3584]{3,2,0,1:T(8,128)S(1)}, f32[2,1,8,3584]{3,2,0,1:T(8,128)}, u32[]{:S(2)}) copy-start(f32[2,1,8,3584]{3,2,0,1:T(8,128)} %get-tuple-element.13) | copy-start | bytes 688132
Sparse Core Ops, SparseCore 0:
  31.3 44.9 all-reduce.6
  107.7 45.9 all-reduce.8
  181.3 45.8 all-reduce.10
  229.4 19.5 reduce-scatter.1
where the time goes:
time: 274 us; the launch traced here: 273 us
  waiting for transfers between devices  94.2 us (34%)
  matrix products  82.3 us (30%)
  blocking collectives  32 us (12%)
  other arithmetic  20.4 us (7%)
  local copies, waits for them, and re-layouts  19.6 us (7%)
  between operations  14.8 us (5%)
  starting transfers between devices  9.53 us (3%)
    unnamed x7, waiting for transfers between devices  73 us
    all_gather x3, blocking collectives, local(): lax.all_gather(incoming.astype(jnp.bfloat16), 'tensor', axis=1, tiled=True)  32 us
    dot_general x3, matrix products, local(): jnp.einsum('nrd,nrc->ndc', saved_rows[:, window_step], pre_pair, preferre...  29.6 us
    reduce_scatter x1, waiting for transfers between devices, local(): lax.psum_scatter(combined.astype(jnp.bfloat16), 'dp', scatter_dimension=1...  20 us
    dot_general x6, matrix products, block_local(): projected = jnp.dot(inputs, w_in_local, preferred_element_type=jnp.float32)  18.7 us
    dot_general x3, matrix products, local(): jnp.einsum('nrd,nrh->ndh', dy_full, hidden_pair, preferred_element_type=j...  17.2 us
    unnamed x48, local copies, waits for them, and re-layouts  16.2 us
    concatenate x1, other arithmetic, local(): combined = jnp.concatenate([in_accum, down_accum], axis=2)  12.7 us
  transfers between devices with their start and end apart: 8, of which 5 were waited for; matrix products, arithmetic and copies ran while one was open for 27% of the time, Pallas kernels for 0%

commit v1 on v0

v1 whole, which is shorter than its diff:
```python
import jax
import jax.numpy as jnp
from jax import lax
from jax.sharding import PartitionSpec as P

AXES = ("pipe", "tensor", "dp")
BF16 = jnp.bfloat16
F32 = jnp.float32


def ring_pairs(sections, tensor_count, replicas, shift):
    pairs = []
    for p in range(sections):
        for t in range(tensor_count):
            to = (t + shift) % tensor_count
            for q in range(replicas):
                step = 1 if q % 2 else -1
                if 0 <= p + step < sections:
                    target = ((p + step) * tensor_count + to) * replicas + q
                else:
                    target = (p * tensor_count + to) * replicas + (q ^ 1)
                pairs.append(((p * tensor_count + t) * replicas + q, target))
    return pairs


def local(entry_grads, fresh_grads, saved_inputs, w_in, w_down):
    section = lax.axis_index("pipe")
    sections = lax.axis_size("pipe")
    place = lax.axis_index("tensor")
    tensor_count = lax.axis_size("tensor")
    replica = lax.axis_index("dp")
    replicas = lax.axis_size("dp")
    core = lax.rem(replica, 2)
    steps, _, batch_rows, width = saved_inputs.shape[1:]
    shard_rows = batch_rows // tensor_count
    hidden_width = w_down.shape[2]
    part_width = width // replicas

    def mine(x):
        return lax.dynamic_index_in_dim(x, core, 0, keepdims=False)

    def theirs(x):
        return lax.dynamic_index_in_dim(x, 1 - core, 0, keepdims=False)

    def to_core(x, offset=1):
        return lax.ppermute(x, "dp", [(i, i ^ offset) for i in range(replicas)])

    def rotate(x, shift):
        return lax.ppermute(x, "tensor", [(i, (i + shift) % tensor_count) for i in range(tensor_count)])

    entry = entry_grads[:, 0]
    entry_other = to_core(theirs(entry).astype(BF16))
    payload = jnp.concatenate([mine(entry).astype(BF16), entry_other])
    blocks = [payload] + [rotate(payload, s) for s in range(1, tensor_count)]
    incoming = jnp.concatenate([mine(entry), entry_other.astype(F32)])

    fresh_own = theirs(fresh_grads).astype(BF16)
    fresh_other = to_core(mine(fresh_grads).astype(BF16))
    fresh_pair = jnp.concatenate([fresh_other, fresh_own], axis=1)
    at_end = section == jnp.where(core == 0, 0, sections - 1)

    saved = saved_inputs[:, :, 0]
    saved_own = mine(saved)
    saved_other = to_core(theirs(saved))
    ordered = []
    for s in range(tensor_count):
        start = lax.rem(place - s + tensor_count, tensor_count) * shard_rows
        ordered.append(lax.dynamic_slice_in_dim(saved_own, start, shard_rows, axis=1))
        ordered.append(lax.dynamic_slice_in_dim(saved_other, start, shard_rows, axis=1))
    rows = jnp.concatenate(ordered, axis=1)

    w_in_dir = mine(w_in[:, 0])
    w_down_dir = mine(w_down[:, 0])
    projected = jnp.einsum("krd,dc->krc", rows, w_in_dir, preferred_element_type=F32)
    gate = projected[:, :, :hidden_width]
    up = projected[:, :, hidden_width:]
    sigmoid_val = jax.nn.sigmoid(gate)
    activated = gate * sigmoid_val
    hidden = (activated * up).astype(BF16)
    gate_factor = up * sigmoid_val * (1.0 + gate * (1.0 - sigmoid_val))

    block_rows = 2 * shard_rows
    own_hand, other_hand, all_dy, all_pre = [], [], [], []
    for k in range(steps):
        dy = jnp.concatenate(blocks)
        dh = jnp.einsum("rd,hd->rh", dy, w_down_dir, preferred_element_type=F32)
        pre_grad = jnp.concatenate([dh * gate_factor[k], dh * activated[k]], axis=1).astype(BF16)
        part = jnp.einsum("rc,dc->rd", pre_grad, w_in_dir, preferred_element_type=F32).astype(BF16)
        summed = part[:block_rows].astype(F32)
        for s in range(1, tensor_count):
            summed = summed + rotate(part[s * block_rows:(s + 1) * block_rows], -s).astype(F32)
        handed = incoming + summed
        if k + 1 < steps:
            payload = jnp.where(at_end, fresh_pair[k], handed.astype(BF16))
            blocks = [lax.ppermute(payload, AXES, ring_pairs(sections, tensor_count, replicas, s))
                      for s in range(tensor_count)]
        own_hand.append(handed[:shard_rows])
        if k == 0:
            other_hand.append(theirs(entry) + to_core(summed[shard_rows:]))
        else:
            other_hand.append(to_core(handed[shard_rows:]))
        incoming = blocks[0].astype(F32)
        all_dy.append(dy)
        all_pre.append(pre_grad)
    dy_rows = jnp.stack(all_dy)
    pre_rows = jnp.stack(all_pre)

    def columns(x, owner):
        return lax.dynamic_slice_in_dim(x, owner * part_width, part_width, axis=2)

    in_terms = [0.0, 0.0]
    down_terms = [0.0, 0.0]
    for offset in range(replicas):
        owner = jnp.bitwise_xor(replica, offset)
        pieces = [columns(rows, owner), pre_rows, hidden, columns(dy_rows, owner)]
        if offset:
            pieces = [to_core(x, offset) for x in pieces]
        rows_part, pre_part, hidden_part, dy_part = pieces
        which = offset % 2
        in_terms[which] = in_terms[which] + jnp.einsum("krd,krc->dc", rows_part, pre_part, preferred_element_type=F32)
        down_terms[which] = down_terms[which] + jnp.einsum("krh,krd->hd", hidden_part, dy_part, preferred_element_type=F32)

    def by_direction(own, other):
        return jnp.where(core == 0, jnp.stack([own, other]), jnp.stack([other, own]))

    hand_offs = by_direction(jnp.stack(own_hand), jnp.stack(other_hand))[:, :, None]
    grad_w_in = by_direction(*in_terms)[:, None]
    grad_w_down = by_direction(*down_terms)[:, None]
    return (hand_offs, grad_w_in, grad_w_down)


def solution(mesh):
    placed = (
        P(None, "pipe", ("dp", "tensor"), None),
        P(None, None, ("dp", "tensor"), None),
        P(None, None, "pipe", "dp", None),
        P(None, "pipe", None, "tensor"),
        P(None, "pipe", "tensor", None),
    )
    return jax.shard_map(
        local,
        mesh=mesh,
        in_specs=placed,
        out_specs=(
            P(None, None, "pipe", ("dp", "tensor"), None),
            P(None, "pipe", "dp", "tensor"),
            P(None, "pipe", "tensor", "dp"),
        ),
        check_vma=False,
    )
```

time: 274 us -> 89.3 us (0.33)
  matrix products: 82.3 us -> 11.7 us
  waiting for transfers between devices: 94.2 us -> 29.7 us
  blocking collectives: 32 us -> 0 us
  starting transfers between devices: 9.53 us -> 25.8 us
  between operations: 14.8 us -> 0.96 us
  other arithmetic: 20.4 us -> 10.4 us
  local copies, waits for them, and re-layouts: 19.6 us -> 10.5 us
    unnamed x7 -> x0, waiting for transfers between devices: 73 us -> none
    dot_general x24 -> x11, matrix products: 82.3 us -> 11.7 us  [the longest x1 3.72 us: local(): jnp.einsum('krd,dc->krc', rows, w_in_dir, preferred_element_type=F32)]
    all_gather x3 -> x0, blocking collectives: 32 us -> none  [local(): lax.all_gather(incoming.astype(jnp.bfloat16), 'tensor', axis=1, tiled=True)]
    ppermute x4 -> x30, waiting for transfers between devices: 1.22 us -> 29.7 us  [the longest x8 15.4 us: local(): lax.ppermute(payload, AXES, ring_pairs(sections, tensor_count, replicas, s))]
    reduce_scatter x1 -> x0, waiting for transfers between devices: 20 us -> none  [local(): lax.psum_scatter(combined.astype(jnp.bfloat16), 'dp', scatter_dimension=1...]
    ppermute x4 -> x30, starting transfers between devices: 9.37 us -> 25.8 us  [the longest x12 18.6 us: rotate(): lax.ppermute(x, 'tensor', [(i, (i + shift) % tensor_count) for i in range...]
    concatenate x4 -> x1, other arithmetic: 15.1 us -> 0.86 us  [local(): payload = jnp.concatenate([mine(entry).astype(BF16), entry_other])]
    unnamed x48 -> x27, local copies, waits for them, and re-layouts: 16.2 us -> 5.05 us
  transfers between devices with their start and end apart: 8 -> 30, of which waited for: 5 -> 20; matrix products, arithmetic and copies ran while one was open for 27% -> 32% of each run, Pallas kernels for 0% -> 0%
where the time goes in v1:
time: 89.3 us; the launch traced here: 88.9 us
  waiting for transfers between devices  29.7 us (33%)
  starting transfers between devices  25.8 us (29%)
  matrix products  11.7 us (13%)
  local copies, waits for them, and re-layouts  10.5 us (12%)
  other arithmetic  10.4 us (12%)
  between operations  0.96 us (1%)
    ppermute x12, starting transfers between devices, rotate(): lax.ppermute(x, 'tensor', [(i, (i + shift) % tensor_count) for i in range...  18.6 us
    ppermute x8, waiting for transfers between devices, local(): lax.ppermute(payload, AXES, ring_pairs(sections, tensor_count, replicas, s))  15.4 us
    ppermute x12, waiting for transfers between devices, rotate(): lax.ppermute(x, 'tensor', [(i, (i + shift) % tensor_count) for i in range...  13.6 us
    select_n x2, other arithmetic, by_direction(): jnp.where(core == 0, jnp.stack([own, other]), jnp.stack([other, own]))  5.58 us
    unnamed x27, local copies, waits for them, and re-layouts  5.05 us
    ppermute x8, starting transfers between devices, local(): lax.ppermute(payload, AXES, ring_pairs(sections, tensor_count, replicas, s))  5 us
    dot_general x1, matrix products, local(): jnp.einsum('krd,dc->krc', rows, w_in_dir, preferred_element_type=F32)  3.72 us
    dot_general x3, matrix products, local(): jnp.einsum('rc,dc->rd', pre_grad, w_in_dir, preferred_element_type=F32)  3.68 us
  transfers between devices with their start and end apart: 30, of which 20 were waited for; matrix products, arithmetic and copies ran while one was open for 32% of the time, Pallas kernels for 0%

profile of v1, /device:TPU:0, one launch (start us, length us, event | category | flops | bytes accessed | tf_op | source)
XLA Modules:
  0.0 88.9 jit_solution(11006662159529608464)
XLA Ops:
  0.6 1.3 %dynamic-slice_bitcast_fusion = bf16[3,32,3584]{2,1,0:T(8,128)(2,1)S(1)} fusion(bf16[2,3,1,32,3584]{4,3,2,1,0:T(8,128)(2,1)} %param.7, s32[]{:T(128)S(6)} %select_n.116), kind=kLoop, calls=%fused_computation.32 | loop fusion | bytes 1376260 | tf_op jit(solution)/shard_map/jit(dynamic_index_in_dim)/squeeze | solution.py:43
  2.4 1.7 %fusion.22 = (bf16[2,8,3584]{2,1,0:T(8,128)(2,1)}, bf16[2,8,3584]{2,1,0:T(8,128)(2,1)S(1)}) fusion(f32[2,2,8,3584]{3,2,1,0:T(8,128)} %param.6, s32[]{:T(128)S(6)} %select_n.115, s32[]{:T(128)S(6)} %select_n.116), kind=kLoop, calls=%fused_computation.56 | loop fusion | bytes 458760 | tf_op jit(solution)/shard_map/convert_element_type | solution.py:58
  4.2 1.5 %bitcast_convert_fusion = bf16[8,3584]{1,0:T(8,128)(2,1)} fusion(f32[2,1,8,3584]{3,2,1,0:T(8,128)} %param.5, s32[]{:T(128)S(6)} %select_n.116), kind=kLoop, calls=%fused_computation.69 | loop fusion | bytes 114692 | tf_op jit(solution)/shard_map/convert_element_type | solution.py:52
  6.2 1.5 %constant_dynamic-update-slice_fusion.4 = (bf16[64,3584]{1,0:T(8,128)(2,1)S(1)}, bf16[8,3584]{1,0:T(8,128)(2,1)}, f32[8,3584]{1,0:T(8,128)S(1)}) fusion(f32[2,1,8,3584]{3,2,1,0:T(8,128)} %param.5, s32[]{:T(128)S(6)} %select_n.115), kind=kLoop, calls=%fused_computation.103 | loop fusion | flops 28671 | bytes 344068
  7.7 0.7 bitcast_dynamic-update-slice_fusion.3
  8.4 0.9 pad_maximum_fusion.2
  9.3 2.6 %collective-permute-start.1 = (bf16[16,3584]{1,0:T(8,128)(2,1)S(1)}, bf16[16,3584]{1,0:T(8,128)(2,1)S(1)}, u32[]{:S(2)}, u32[]{:S(2)}) collective-permute-start(bf16[16,3584]{1,0:T(8,128)(2,1)S(1)} %pad_maximum_fusion.2), channel_id=1, source_target_pairs={{0,2},{2,4},{4,6},{6,0},{1,3},{3,5},{5,7},{7,1},{8,10},{10,12},{12... | collective-permute-start | bytes 344072 | tf_op jit(solution)/shard_map/ppermute | solution.py:49
  11.9 1.5 %collective-permute-start.2 = (bf16[16,3584]{1,0:T(8,128)(2,1)S(1)}, bf16[16,3584]{1,0:T(8,128)(2,1)S(1)}, u32[]{:S(2)}, u32[]{:S(2)}) collective-permute-start(bf16[16,3584]{1,0:T(8,128)(2,1)S(1)} %pad_maximum_fusion.2), channel_id=1, source_target_pairs={{0,4},{2,6},{4,0},{6,2},{1,5},{3,7},{5,1},{7,3},{8,12},{10,14},{12... | collective-permute-start | bytes 344072 | tf_op jit(solution)/shard_map/ppermute | solution.py:49
  13.4 1.4 %collective-permute-start.3 = (bf16[16,3584]{1,0:T(8,128)(2,1)S(1)}, bf16[16,3584]{1,0:T(8,128)(2,1)S(1)}, u32[]{:S(2)}, u32[]{:S(2)}) collective-permute-start(bf16[16,3584]{1,0:T(8,128)(2,1)S(1)} %pad_maximum_fusion.2), channel_id=1, source_target_pairs={{0,6},{2,0},{4,2},{6,4},{1,7},{3,1},{5,3},{7,5},{8,14},{10,8},{12,... | collective-permute-start | bytes 344072 | tf_op jit(solution)/shard_map/ppermute | solution.py:49
  14.8 0.9 %constant_dynamic-update-slice_fusion.3 = (bf16[64,3584]{1,0:T(8,128)(2,1)S(1)}, f32[8,3584]{1,0:T(8,128)S(1)}) fusion(bf16[64,3584]{1,0:T(8,128)(2,1)S(1)} %get-tuple-element.11, bf16[8,3584]{1,0:T(8,128)(2,1)} %collective-permute-done), kind=kLoop, calls=%fused_computation.102 | loop fusion | flops 28672 | bytes 229376
  15.7 1.1 %collective-permute-done.1 = bf16[16,3584]{1,0:T(8,128)(2,1)S(1)} collective-permute-done((bf16[16,3584]{1,0:T(8,128)(2,1)S(1)}, bf16[16,3584]{1,0:T(8,128)(2,1)S(1)}, u32[]{:S(2)}, u32[]{:S(2)}) %collective-permute-start.1) | collective-permute-done | bytes 114720 | tf_op jit(solution)/shard_map/ppermute | solution.py:49
  16.9 2.2 %collective-permute-done.2 = bf16[16,3584]{1,0:T(8,128)(2,1)S(1)} collective-permute-done((bf16[16,3584]{1,0:T(8,128)(2,1)S(1)}, bf16[16,3584]{1,0:T(8,128)(2,1)S(1)}, u32[]{:S(2)}, u32[]{:S(2)}) %collective-permute-start.2) | collective-permute-done | bytes 114720 | tf_op jit(solution)/shard_map/ppermute | solution.py:49
  19.4 0.7 dynamic-slice_dynamic-update-slice_fusion.3
  20.1 0.7 bitcast_dynamic-update-slice_fusion.2
  21.5 0.7 bitcast_dynamic-update-slice_fusion.1
  22.9 0.7 bitcast_dynamic-update-slice_fusion
  24.3 3.7 %fusion = f32[3,64,512]{2,1,0:T(8,128)S(1)} fusion(bf16[3,64,3584]{2,1,0:T(8,128)(2,1)} %dynamic-slice_dynamic-update-slice_fusion, bf16[2,1,3584,512]{3,2,1,0:T(8,128)(2,1)} %param.8, s32[]{:T(128)S(6)} %select_n.115), kind=kOutput, calls=%fused_computation.5 | convolution fusion | flops 704643072 | bytes 5439492 | tf_op jit(solution)/shard_map/krd,dc->krc/dot_general | solution.py:74
  28.1 0.7 fusion.41
  28.8 1.2 %convolution_convert_fusion.2 = bf16[64,3584]{1,0:T(8,128)(2,1)S(1)} fusion(bf16[2,1,3584,512]{3,2,1,0:T(8,128)(2,1)S(1)} %bitcast.141, s32[]{:T(128)S(6)} %select_n.115, bf16[64,256]{1,0:T(8,128)(2,1)S(1)} %get-tuple-element.37, bf16[64,256]{1,0:T(8,128)(2,1)S(1)} %get-tuple-element.36), kind=kOutput, calls=%fused_computation.3 | convolution fusion | flops 235241472 | bytes 4194308 | tf_op jit(solution)/shard_map/rc,dc->rd/dot_general | solution.py:88
  30.1 1.8 %collective-permute-start.7 = (bf16[16,3584]{1,0:T(8,128)(2,1)S(1)}, bf16[16,3584]{1,0:T(8,128)(2,1)S(1)}, u32[]{:S(2)}, u32[]{:S(2)}) collective-permute-start(bf16[16,3584]{1,0:T(8,128)(2,1)S(1)} %get-tuple-element.21), channel_id=1, source_target_pairs={{0,2},{2,4},{4,6},{6,0},{1,3},{3,5},{5,7},{7,1},{8,10},{10,12},{12... | collective-permute-start | bytes 344072 | tf_op jit(solution)/shard_map/ppermute | solution.py:49
  32.3 2.3 %collective-permute-start.5 = (bf16[16,3584]{1,0:T(8,128)(2,1)S(1)}, bf16[16,3584]{1,0:T(8,128)(2,1)S(1)}, u32[]{:S(2)}, u32[]{:S(2)}) collective-permute-start(bf16[16,3584]{1,0:T(8,128)(2,1)S(1)} %get-tuple-element.20), channel_id=1, source_target_pairs={{0,6},{2,0},{4,2},{6,4},{1,7},{3,1},{5,3},{7,5},{8,14},{10,8},{12,... | collective-permute-start | bytes 344072 | tf_op jit(solution)/shard_map/ppermute | solution.py:49
  35.2 1.8 %collective-permute-done.7 = bf16[16,3584]{1,0:T(8,128)(2,1)S(1)} collective-permute-done((bf16[16,3584]{1,0:T(8,128)(2,1)S(1)}, bf16[16,3584]{1,0:T(8,128)(2,1)S(1)}, u32[]{:S(2)}, u32[]{:S(2)}) %collective-permute-start.7) | collective-permute-done | bytes 114720 | tf_op jit(solution)/shard_map/ppermute | solution.py:49
  37.0 1.4 %collective-permute-done.6 = bf16[16,3584]{1,0:T(8,128)(2,1)S(1)} collective-permute-done((bf16[16,3584]{1,0:T(8,128)(2,1)S(1)}, bf16[16,3584]{1,0:T(8,128)(2,1)S(1)}, u32[]{:S(2)}, u32[]{:S(2)}) %collective-permute-start.6) | collective-permute-done | bytes 114720 | tf_op jit(solution)/shard_map/ppermute | solution.py:49
  38.9 2.2 %collective-permute-start.11 = (bf16[16,3584]{1,0:T(8,128)(2,1)S(1)}, bf16[16,3584]{1,0:T(8,128)(2,1)S(1)}, u32[]{:S(2)}, u32[]{:S(2)}) collective-permute-start(bf16[16,3584]{1,0:T(8,128)(2,1)S(1)} %get-tuple-element.8), channel_id=1, source_target_pairs={{0,5},{1,13},{2,7},{3,15},{4,1},{5,9},{6,3},{7,11},{8,4},{9,21},{1... | collective-permute-start | bytes 344072 | tf_op jit(solution)/shard_map/ppermute | solution.py:95
  41.1 2.5 %collective-permute-done.9 = bf16[16,3584]{1,0:T(8,128)(2,1)S(1)} collective-permute-done((bf16[16,3584]{1,0:T(8,128)(2,1)S(1)}, bf16[16,3584]{1,0:T(8,128)(2,1)S(1)}, u32[]{:S(2)}, u32[]{:S(2)}) %collective-permute-start.9) | collective-permute-done | bytes 114720 | tf_op jit(solution)/shard_map/ppermute | solution.py:95
  43.8 3.4 %collective-permute-done.10 = bf16[16,3584]{1,0:T(8,128)(2,1)S(1)} collective-permute-done((bf16[16,3584]{1,0:T(8,128)(2,1)S(1)}, bf16[16,3584]{1,0:T(8,128)(2,1)S(1)}, u32[]{:S(2)}, u32[]{:S(2)}) %collective-permute-start.10) | collective-permute-done | bytes 114720 | tf_op jit(solution)/shard_map/ppermute | solution.py:95
  47.6 1.6 %collective-permute-done.12 = bf16[16,3584]{1,0:T(8,128)(2,1)S(1)} collective-permute-done((bf16[16,3584]{1,0:T(8,128)(2,1)S(1)}, bf16[16,3584]{1,0:T(8,128)(2,1)S(1)}, u32[]{:S(2)}, u32[]{:S(2)}) %collective-permute-start.12) | collective-permute-done | bytes 114720 | tf_op jit(solution)/shard_map/ppermute | solution.py:95
  50.0 1.2 %convolution_convert_fusion.1 = bf16[64,3584]{1,0:T(8,128)(2,1)S(1)} fusion(bf16[2,1,3584,512]{3,2,1,0:T(8,128)(2,1)S(1)} %bitcast.141, s32[]{:T(128)S(6)} %select_n.115, bf16[64,256]{1,0:T(8,128)(2,1)S(1)} %get-tuple-element.35, bf16[64,256]{1,0:T(8,128)(2,1)S(1)} %get-tuple-element.34), kind=kOutput, calls=%fused_computation.2 | convolution fusion | flops 235241472 | bytes 4194308 | tf_op jit(solution)/shard_map/rc,dc->rd/dot_general | solution.py:88
  51.2 2.6 %collective-permute-start.15 = (bf16[16,3584]{1,0:T(8,128)(2,1)S(1)}, bf16[16,3584]{1,0:T(8,128)(2,1)S(1)}, u32[]{:S(2)}, u32[]{:S(2)}) collective-permute-start(bf16[16,3584]{1,0:T(8,128)(2,1)S(1)} %get-tuple-element.18), channel_id=1, source_target_pairs={{0,2},{2,4},{4,6},{6,0},{1,3},{3,5},{5,7},{7,1},{8,10},{10,12},{12... | collective-permute-start | bytes 344072 | tf_op jit(solution)/shard_map/ppermute | solution.py:49
  54.4 1.0 %collective-permute-start.13 = (bf16[16,3584]{1,0:T(8,128)(2,1)S(1)}, bf16[16,3584]{1,0:T(8,128)(2,1)S(1)}, u32[]{:S(2)}, u32[]{:S(2)}) collective-permute-start(bf16[16,3584]{1,0:T(8,128)(2,1)S(1)} %get-tuple-element.17), channel_id=1, source_target_pairs={{0,6},{2,0},{4,2},{6,4},{1,7},{3,1},{5,3},{7,5},{8,14},{10,8},{12,... | collective-permute-start | bytes 344072 | tf_op jit(solution)/shard_map/ppermute | solution.py:49
  55.5 2.7 %collective-permute-done.15 = bf16[16,3584]{1,0:T(8,128)(2,1)S(1)} collective-permute-done((bf16[16,3584]{1,0:T(8,128)(2,1)S(1)}, bf16[16,3584]{1,0:T(8,128)(2,1)S(1)}, u32[]{:S(2)}, u32[]{:S(2)}) %collective-permute-start.15) | collective-permute-done | bytes 114720 | tf_op jit(solution)/shard_map/ppermute | solution.py:49
  58.2 0.9 %collective-permute-done.14 = bf16[16,3584]{1,0:T(8,128)(2,1)S(1)} collective-permute-done((bf16[16,3584]{1,0:T(8,128)(2,1)S(1)}, bf16[16,3584]{1,0:T(8,128)(2,1)S(1)}, u32[]{:S(2)}, u32[]{:S(2)}) %collective-permute-start.14) | collective-permute-done | bytes 114720 | tf_op jit(solution)/shard_map/ppermute | solution.py:49
  59.3 0.9 %collective-permute-start.17 = (bf16[16,3584]{1,0:T(8,128)(2,1)S(1)}, bf16[16,3584]{1,0:T(8,128)(2,1)S(1)}, u32[]{:S(2)}, u32[]{:S(2)}) collective-permute-start(bf16[16,3584]{1,0:T(8,128)(2,1)S(1)} %get-tuple-element.6), channel_id=1, source_target_pairs={{0,3},{1,11},{2,5},{3,13},{4,7},{5,15},{6,1},{7,9},{8,2},{9,19},{1... | collective-permute-start | bytes 344072 | tf_op jit(solution)/shard_map/ppermute | solution.py:95
  60.3 1.5 %collective-permute-start.18 = (bf16[16,3584]{1,0:T(8,128)(2,1)S(1)}, bf16[16,3584]{1,0:T(8,128)(2,1)S(1)}, u32[]{:S(2)}, u32[]{:S(2)}) collective-permute-start(bf16[16,3584]{1,0:T(8,128)(2,1)S(1)} %get-tuple-element.6), channel_id=1, source_target_pairs={{0,5},{1,13},{2,7},{3,15},{4,1},{5,9},{6,3},{7,11},{8,4},{9,21},{1... | collective-permute-start | bytes 344072 | tf_op jit(solution)/shard_map/ppermute | solution.py:95
  61.8 2.3 %collective-permute-done.16 = bf16[16,3584]{1,0:T(8,128)(2,1)S(1)} collective-permute-done((bf16[16,3584]{1,0:T(8,128)(2,1)S(1)}, bf16[16,3584]{1,0:T(8,128)(2,1)S(1)}, u32[]{:S(2)}, u32[]{:S(2)}) %collective-permute-start.16) | collective-permute-done | bytes 114720 | tf_op jit(solution)/shard_map/ppermute | solution.py:95
  64.1 4.0 %collective-permute-done.17 = bf16[16,3584]{1,0:T(8,128)(2,1)S(1)} collective-permute-done((bf16[16,3584]{1,0:T(8,128)(2,1)S(1)}, bf16[16,3584]{1,0:T(8,128)(2,1)S(1)}, u32[]{:S(2)}, u32[]{:S(2)}) %collective-permute-start.17) | collective-permute-done | bytes 114720 | tf_op jit(solution)/shard_map/ppermute | solution.py:95
  68.5 1.3 %collective-permute-done.19 = bf16[16,3584]{1,0:T(8,128)(2,1)S(1)} collective-permute-done((bf16[16,3584]{1,0:T(8,128)(2,1)S(1)}, bf16[16,3584]{1,0:T(8,128)(2,1)S(1)}, u32[]{:S(2)}, u32[]{:S(2)}) %collective-permute-start.19) | collective-permute-done | bytes 114720 | tf_op jit(solution)/shard_map/ppermute | solution.py:95
  70.5 1.2 %convolution_convert_fusion = bf16[64,3584]{1,0:T(8,128)(2,1)S(1)} fusion(bf16[2,1,3584,512]{3,2,1,0:T(8,128)(2,1)S(1)} %bitcast.141, s32[]{:T(128)S(6)} %select_n.115, bf16[64,256]{1,0:T(8,128)(2,1)S(1)} %get-tuple-element.33, bf16[64,256]{1,0:T(8,128)(2,1)S(1)} %get-tuple-element.32), kind=kOutput, calls=%fused_computation.1 | convolution fusion | flops 235241472 | bytes 4194308 | tf_op jit(solution)/shard_map/rc,dc->rd/dot_general | solution.py:88
  71.8 2.5 %collective-permute-start.22 = (bf16[16,3584]{1,0:T(8,128)(2,1)S(1)}, bf16[16,3584]{1,0:T(8,128)(2,1)S(1)}, u32[]{:S(2)}, u32[]{:S(2)}) collective-permute-start(bf16[16,3584]{1,0:T(8,128)(2,1)S(1)} %get-tuple-element.15), channel_id=1, source_target_pairs={{0,2},{2,4},{4,6},{6,0},{1,3},{3,5},{5,7},{7,1},{8,10},{10,12},{12... | collective-permute-start | bytes 344072 | tf_op jit(solution)/shard_map/ppermute | solution.py:49
  74.3 1.4 %collective-permute-start.21 = (bf16[16,3584]{1,0:T(8,128)(2,1)S(1)}, bf16[16,3584]{1,0:T(8,128)(2,1)S(1)}, u32[]{:S(2)}, u32[]{:S(2)}) collective-permute-start(bf16[16,3584]{1,0:T(8,128)(2,1)S(1)} %get-tuple-element.16), channel_id=1, source_target_pairs={{0,4},{2,6},{4,0},{6,2},{1,5},{3,7},{5,1},{7,3},{8,12},{10,14},{12... | collective-permute-start | bytes 344072 | tf_op jit(solution)/shard_map/ppermute | solution.py:49
  76.9 0.7 convolution_bitcast_fusion.1
  77.6 1.2 %collective-permute-done.22 = bf16[16,3584]{1,0:T(8,128)(2,1)S(1)} collective-permute-done((bf16[16,3584]{1,0:T(8,128)(2,1)S(1)}, bf16[16,3584]{1,0:T(8,128)(2,1)S(1)}, u32[]{:S(2)}, u32[]{:S(2)}) %collective-permute-start.22) | collective-permute-done | bytes 114720 | tf_op jit(solution)/shard_map/ppermute | solution.py:49
  78.8 0.9 %collective-permute-done.21 = bf16[16,3584]{1,0:T(8,128)(2,1)S(1)} collective-permute-done((bf16[16,3584]{1,0:T(8,128)(2,1)S(1)}, bf16[16,3584]{1,0:T(8,128)(2,1)S(1)}, u32[]{:S(2)}, u32[]{:S(2)}) %collective-permute-start.21) | collective-permute-done | bytes 114720 | tf_op jit(solution)/shard_map/ppermute | solution.py:49
  79.7 0.7 collective-permute-done.20
  81.3 0.7 convolution_bitcast_fusion
  82.0 3.5 %maximum_select_fusion = f32[2,1,1792,512]{3,2,1,0:T(8,128)} fusion(f32[1,1,1792,512]{3,2,1,0:T(8,128)S(1)} %convolution_bitcast_fusion, f32[1,1,1792,512]{3,2,1,0:T(8,128)S(1)} %convolution_bitcast_fusion.1, pred[]{:T(512)S(6)} %eq.4), kind=kLoop, calls=%fused_computation | loop fusion | flops 5505024 | bytes 14680065 | tf_op jit(solution)/shard_map/jit(_where)/select_n | solution.py:124
  85.5 0.9 %fusion.18 = f32[2,3,1,8,3584]{4,3,2,1,0:T(8,128)} fusion(f32[1,3,1,8,3584]{4,3,1,2,0:T(8,128)S(1)} %maximum_bitcast_fusion.1, f32[1,3,1,8,3584]{4,3,1,2,0:T(8,128)S(1)} %maximum_bitcast_fusion, pred[]{:T(512)S(6)} %eq.4), kind=kLoop, calls=%fused_computation.29 | loop fusion | flops 516096 | bytes 1376257
  86.9 2.1 %maximum_select_fusion.1 = f32[2,1,256,1792]{3,2,1,0:T(8,128)} fusion(f32[1,1,256,1792]{3,2,1,0:T(8,128)S(1)} %convolution_bitcast_fusion.2, f32[1,1,256,1792]{3,2,1,0:T(8,128)S(1)} %convolution_bitcast_fusion.3, pred[]{:T(512)S(6)} %eq.4), kind=kLoop, calls=%fused_computation.4 | loop fusion | flops 2752512 | bytes 7340033 | tf_op jit(solution)/shard_map/jit(_where)/select_n | solution.py:124
  (82 shorter events, 10.8 us)
Async XLA Ops:
  0.6 7.1 %copy-start.1 = (bf16[2,3,1,32,3584]{4,3,2,1,0:T(8,128)(2,1)S(1)}, bf16[2,3,1,32,3584]{4,3,2,1,0:T(8,128)(2,1)}, u32[]{:S(2)}) copy-start(bf16[2,3,1,32,3584]{4,3,2,1,0:T(8,128)(2,1)} %param.7) | copy-start | bytes 4128772
  1.9 17.5 %collective-permute-start.4 = (bf16[3,32,3584]{2,1,0:T(8,128)(2,1)S(1)}, bf16[3,32,3584]{2,1,0:T(8,128)(2,1)S(1)}, u32[]{:S(2)}, u32[]{:S(2)}) collective-permute-start(bf16[3,32,3584]{2,1,0:T(8,128)(2,1)S(1)} %dynamic-slice_bitcast_fusion), channel_id=1, source_target_pairs={{0,1},{1,0},{2,3},{3,2},{4,5},{5,4},{6,7},{7,6},{8,9},{9,8},{10,11... | collective-permute-start | bytes 2064392 | tf_op jit(solution)/shard_map/ppermute | solution.py:46
  4.1 30.6 %collective-permute-start.8 = (bf16[2,8,3584]{2,1,0:T(8,128)(2,1)}, bf16[2,8,3584]{2,1,0:T(8,128)(2,1)S(1)}, u32[]{:S(2)}, u32[]{:S(2)}) collective-permute-start(bf16[2,8,3584]{2,1,0:T(8,128)(2,1)} %get-tuple-element.23), channel_id=1, source_target_pairs={{0,1},{1,0},{2,3},{3,2},{4,5},{5,4},{6,7},{7,6},{8,9},{9,8},{10,11... | collective-permute-start | bytes 344072 | tf_op jit(solution)/shard_map/ppermute | solution.py:46
  5.7 2.7 %collective-permute-start = (bf16[8,3584]{1,0:T(8,128)(2,1)}, bf16[8,3584]{1,0:T(8,128)(2,1)}, u32[]{:S(2)}, u32[]{:S(2)}) collective-permute-start(bf16[8,3584]{1,0:T(8,128)(2,1)} %bitcast_convert_fusion), channel_id=1, source_target_pairs={{0,1},{1,0},{2,3},{3,2},{4,5},{5,4},{6,7},{7,6},{8,9},{9,8},{10,11... | collective-permute-start | bytes 172040 | tf_op jit(solution)/shard_map/ppermute | solution.py:46
  9.3 7.5 %collective-permute-start.1 = (bf16[16,3584]{1,0:T(8,128)(2,1)S(1)}, bf16[16,3584]{1,0:T(8,128)(2,1)S(1)}, u32[]{:S(2)}, u32[]{:S(2)}) collective-permute-start(bf16[16,3584]{1,0:T(8,128)(2,1)S(1)} %pad_maximum_fusion.2), channel_id=1, source_target_pairs={{0,2},{2,4},{4,6},{6,0},{1,3},{3,5},{5,7},{7,1},{8,10},{10,12},{12... | collective-permute-start | bytes 344072 | tf_op jit(solution)/shard_map/ppermute | solution.py:49
  11.9 7.2 %collective-permute-start.2 = (bf16[16,3584]{1,0:T(8,128)(2,1)S(1)}, bf16[16,3584]{1,0:T(8,128)(2,1)S(1)}, u32[]{:S(2)}, u32[]{:S(2)}) collective-permute-start(bf16[16,3584]{1,0:T(8,128)(2,1)S(1)} %pad_maximum_fusion.2), channel_id=1, source_target_pairs={{0,4},{2,6},{4,0},{6,2},{1,5},{3,7},{5,1},{7,3},{8,12},{10,14},{12... | collective-permute-start | bytes 344072 | tf_op jit(solution)/shard_map/ppermute | solution.py:49
  13.4 6.0 %collective-permute-start.3 = (bf16[16,3584]{1,0:T(8,128)(2,1)S(1)}, bf16[16,3584]{1,0:T(8,128)(2,1)S(1)}, u32[]{:S(2)}, u32[]{:S(2)}) collective-permute-start(bf16[16,3584]{1,0:T(8,128)(2,1)S(1)} %pad_maximum_fusion.2), channel_id=1, source_target_pairs={{0,6},{2,0},{4,2},{6,4},{1,7},{3,1},{5,3},{7,5},{8,14},{10,8},{12,... | collective-permute-start | bytes 344072 | tf_op jit(solution)/shard_map/ppermute | solution.py:49
  19.3 9.5 %slice-start = ((s8[7340032]{0:T(1024)(128)(4,1)}), s8[4194304]{0:T(1024)(128)(4,1)S(1)}, s32[]{:S(2)}) async-start(s8[7340032]{0:T(1024)(128)(4,1)} %bitcast.140), calls=%async_computation | async-start | bytes 8388608
  23.6 4.5 %copy-start = (bf16[2,1,256,3584]{3,2,1,0:T(8,128)(2,1)S(1)}, bf16[2,1,256,3584]{3,2,1,0:T(8,128)(2,1)}, u32[]{:S(2)}) copy-start(bf16[2,1,256,3584]{3,2,1,0:T(8,128)(2,1)} %param.9) | copy-start | bytes 11010052
  24.3 4.5 %slice-start.1 = ((s8[7340032]{0:T(1024)(128)(4,1)}), s8[3145728]{0:T(1024)(128)(4,1)S(1)}, s32[]{:S(2)}) async-start(s8[7340032]{0:T(1024)(128)(4,1)} %bitcast.140), calls=%async_computation.1 | async-start | bytes 6291456
  28.8 5.7 %copy-start.2 = (bf16[3,64,3584]{2,1,0:T(8,128)(2,1)S(1)}, bf16[3,64,3584]{2,1,0:T(8,128)(2,1)}, u32[]{:S(2)}) copy-start(bf16[3,64,3584]{2,1,0:T(8,128)(2,1)} %dynamic-slice_dynamic-update-slice_fusion) | copy-start | bytes 4128772
  30.1 6.8 %collective-permute-start.7 = (bf16[16,3584]{1,0:T(8,128)(2,1)S(1)}, bf16[16,3584]{1,0:T(8,128)(2,1)S(1)}, u32[]{:S(2)}, u32[]{:S(2)}) collective-permute-start(bf16[16,3584]{1,0:T(8,128)(2,1)S(1)} %get-tuple-element.21), channel_id=1, source_target_pairs={{0,2},{2,4},{4,6},{6,0},{1,3},{3,5},{5,7},{7,1},{8,10},{10,12},{12... | collective-permute-start | bytes 344072 | tf_op jit(solution)/shard_map/ppermute | solution.py:49
  31.9 6.5 %collective-permute-start.6 = (bf16[16,3584]{1,0:T(8,128)(2,1)S(1)}, bf16[16,3584]{1,0:T(8,128)(2,1)S(1)}, u32[]{:S(2)}, u32[]{:S(2)}) collective-permute-start(bf16[16,3584]{1,0:T(8,128)(2,1)S(1)} %get-tuple-element.22), channel_id=1, source_target_pairs={{0,4},{2,6},{4,0},{6,2},{1,5},{3,7},{5,1},{7,3},{8,12},{10,14},{12... | collective-permute-start | bytes 344072 | tf_op jit(solution)/shard_map/ppermute | solution.py:49
  32.3 6.4 %collective-permute-start.5 = (bf16[16,3584]{1,0:T(8,128)(2,1)S(1)}, bf16[16,3584]{1,0:T(8,128)(2,1)S(1)}, u32[]{:S(2)}, u32[]{:S(2)}) collective-permute-start(bf16[16,3584]{1,0:T(8,128)(2,1)S(1)} %get-tuple-element.20), channel_id=1, source_target_pairs={{0,6},{2,0},{4,2},{6,4},{1,7},{3,1},{5,3},{7,5},{8,14},{10,8},{12,... | collective-permute-start | bytes 344072 | tf_op jit(solution)/shard_map/ppermute | solution.py:49
  34.6 46.7 %collective-permute-start.26 = (bf16[3,64,1792]{2,1,0:T(8,128)(2,1)S(1)}, bf16[3,64,1792]{2,1,0:T(8,128)(2,1)S(1)}, u32[]{:S(2)}, u32[]{:S(2)}) collective-permute-start(bf16[3,64,1792]{2,1,0:T(8,128)(2,1)S(1)} %constant_dynamic-slice_fusion.1), channel_id=1, source_target_pairs={{0,1},{1,0},{2,3},{3,2},{4,5},{5,4},{6,7},{7,6},{8,9},{9,8},{10,11... | collective-permute-start | bytes 2064392 | tf_op jit(solution)/shard_map/ppermute | solution.py:46
  34.7 51.7 %collective-permute-start.28 = (bf16[3,64,256]{2,1,0:T(8,128)(2,1)S(1)}, bf16[3,64,256]{2,1,0:T(8,128)(2,1)S(1)}, u32[]{:S(2)}, u32[]{:S(2)}) collective-permute-start(bf16[3,64,256]{2,1,0:T(8,128)(2,1)S(1)} %get-tuple-element.25), channel_id=1, source_target_pairs={{0,1},{1,0},{2,3},{3,2},{4,5},{5,4},{6,7},{7,6},{8,9},{9,8},{10,11... | collective-permute-start | bytes 294920 | tf_op jit(solution)/shard_map/ppermute | solution.py:46
  38.8 4.8 %collective-permute-start.9 = (bf16[16,3584]{1,0:T(8,128)(2,1)S(1)}, bf16[16,3584]{1,0:T(8,128)(2,1)S(1)}, u32[]{:S(2)}, u32[]{:S(2)}) collective-permute-start(bf16[16,3584]{1,0:T(8,128)(2,1)S(1)} %get-tuple-element.8), channel_id=1, source_target_pairs={{0,1},{1,9},{2,3},{3,11},{4,5},{5,13},{6,7},{7,15},{8,0},{9,17},{1... | collective-permute-start | bytes 344072 | tf_op jit(solution)/shard_map/ppermute | solution.py:95
  38.8 8.4 %collective-permute-start.10 = (bf16[16,3584]{1,0:T(8,128)(2,1)S(1)}, bf16[16,3584]{1,0:T(8,128)(2,1)S(1)}, u32[]{:S(2)}, u32[]{:S(2)}) collective-permute-start(bf16[16,3584]{1,0:T(8,128)(2,1)S(1)} %get-tuple-element.8), channel_id=1, source_target_pairs={{0,3},{1,11},{2,5},{3,13},{4,7},{5,15},{6,1},{7,9},{8,2},{9,19},{1... | collective-permute-start | bytes 344072 | tf_op jit(solution)/shard_map/ppermute | solution.py:95
  38.9 8.8 %collective-permute-start.11 = (bf16[16,3584]{1,0:T(8,128)(2,1)S(1)}, bf16[16,3584]{1,0:T(8,128)(2,1)S(1)}, u32[]{:S(2)}, u32[]{:S(2)}) collective-permute-start(bf16[16,3584]{1,0:T(8,128)(2,1)S(1)} %get-tuple-element.8), channel_id=1, source_target_pairs={{0,5},{1,13},{2,7},{3,15},{4,1},{5,9},{6,3},{7,11},{8,4},{9,21},{1... | collective-permute-start | bytes 344072 | tf_op jit(solution)/shard_map/ppermute | solution.py:95
  43.6 5.7 %collective-permute-start.12 = (bf16[16,3584]{1,0:T(8,128)(2,1)S(1)}, bf16[16,3584]{1,0:T(8,128)(2,1)S(1)}, u32[]{:S(2)}, u32[]{:S(2)}) collective-permute-start(bf16[16,3584]{1,0:T(8,128)(2,1)S(1)} %get-tuple-element.8), channel_id=1, source_target_pairs={{0,7},{1,15},{2,1},{3,9},{4,3},{5,11},{6,5},{7,13},{8,6},{9,23},{1... | collective-permute-start | bytes 344072 | tf_op jit(solution)/shard_map/ppermute | solution.py:95
  47.2 7.2 %collective-permute-start.23 = (f32[8,3584]{1,0:T(8,128)S(1)}, f32[8,3584]{1,0:T(8,128)S(1)}, u32[]{:S(2)}, u32[]{:S(2)}) collective-permute-start(f32[8,3584]{1,0:T(8,128)S(1)} %slice.137), channel_id=1, source_target_pairs={{0,1},{1,0},{2,3},{3,2},{4,5},{5,4},{6,7},{7,6},{8,9},{9,8},{10,11... | collective-permute-start | bytes 344072 | tf_op jit(solution)/shard_map/ppermute | solution.py:46
  50.0 5.5 %copy-start.3 = (f32[2,1,8,3584]{3,2,1,0:T(8,128)S(1)}, f32[2,1,8,3584]{3,2,1,0:T(8,128)}, u32[]{:S(2)}) copy-start(f32[2,1,8,3584]{3,2,1,0:T(8,128)} %param.5) | copy-start | bytes 688132
  51.2 6.9 %collective-permute-start.15 = (bf16[16,3584]{1,0:T(8,128)(2,1)S(1)}, bf16[16,3584]{1,0:T(8,128)(2,1)S(1)}, u32[]{:S(2)}, u32[]{:S(2)}) collective-permute-start(bf16[16,3584]{1,0:T(8,128)(2,1)S(1)} %get-tuple-element.18), channel_id=1, source_target_pairs={{0,2},{2,4},{4,6},{6,0},{1,3},{3,5},{5,7},{7,1},{8,10},{10,12},{12... | collective-permute-start | bytes 344072 | tf_op jit(solution)/shard_map/ppermute | solution.py:49
  53.9 5.2 %collective-permute-start.14 = (bf16[16,3584]{1,0:T(8,128)(2,1)S(1)}, bf16[16,3584]{1,0:T(8,128)(2,1)S(1)}, u32[]{:S(2)}, u32[]{:S(2)}) collective-permute-start(bf16[16,3584]{1,0:T(8,128)(2,1)S(1)} %get-tuple-element.19), channel_id=1, source_target_pairs={{0,4},{2,6},{4,0},{6,2},{1,5},{3,7},{5,1},{7,3},{8,12},{10,14},{12... | collective-permute-start | bytes 344072 | tf_op jit(solution)/shard_map/ppermute | solution.py:49
  54.4 4.8 %collective-permute-start.13 = (bf16[16,3584]{1,0:T(8,128)(2,1)S(1)}, bf16[16,3584]{1,0:T(8,128)(2,1)S(1)}, u32[]{:S(2)}, u32[]{:S(2)}) collective-permute-start(bf16[16,3584]{1,0:T(8,128)(2,1)S(1)} %get-tuple-element.17), channel_id=1, source_target_pairs={{0,6},{2,0},{4,2},{6,4},{1,7},{3,1},{5,3},{7,5},{8,14},{10,8},{12,... | collective-permute-start | bytes 344072 | tf_op jit(solution)/shard_map/ppermute | solution.py:49
  59.3 4.8 %collective-permute-start.16 = (bf16[16,3584]{1,0:T(8,128)(2,1)S(1)}, bf16[16,3584]{1,0:T(8,128)(2,1)S(1)}, u32[]{:S(2)}, u32[]{:S(2)}) collective-permute-start(bf16[16,3584]{1,0:T(8,128)(2,1)S(1)} %get-tuple-element.6), channel_id=1, source_target_pairs={{0,1},{1,9},{2,3},{3,11},{4,5},{5,13},{6,7},{7,15},{8,0},{9,17},{1... | collective-permute-start | bytes 344072 | tf_op jit(solution)/shard_map/ppermute | solution.py:95
  59.3 8.8 %collective-permute-start.17 = (bf16[16,3584]{1,0:T(8,128)(2,1)S(1)}, bf16[16,3584]{1,0:T(8,128)(2,1)S(1)}, u32[]{:S(2)}, u32[]{:S(2)}) collective-permute-start(bf16[16,3584]{1,0:T(8,128)(2,1)S(1)} %get-tuple-element.6), channel_id=1, source_target_pairs={{0,3},{1,11},{2,5},{3,13},{4,7},{5,15},{6,1},{7,9},{8,2},{9,19},{1... | collective-permute-start | bytes 344072 | tf_op jit(solution)/shard_map/ppermute | solution.py:95
  60.3 8.2 %collective-permute-start.18 = (bf16[16,3584]{1,0:T(8,128)(2,1)S(1)}, bf16[16,3584]{1,0:T(8,128)(2,1)S(1)}, u32[]{:S(2)}, u32[]{:S(2)}) collective-permute-start(bf16[16,3584]{1,0:T(8,128)(2,1)S(1)} %get-tuple-element.6), channel_id=1, source_target_pairs={{0,5},{1,13},{2,7},{3,15},{4,1},{5,9},{6,3},{7,11},{8,4},{9,21},{1... | collective-permute-start | bytes 344072 | tf_op jit(solution)/shard_map/ppermute | solution.py:95
  64.1 5.7 %collective-permute-start.19 = (bf16[16,3584]{1,0:T(8,128)(2,1)S(1)}, bf16[16,3584]{1,0:T(8,128)(2,1)S(1)}, u32[]{:S(2)}, u32[]{:S(2)}) collective-permute-start(bf16[16,3584]{1,0:T(8,128)(2,1)S(1)} %get-tuple-element.6), channel_id=1, source_target_pairs={{0,7},{1,15},{2,1},{3,9},{4,3},{5,11},{6,5},{7,13},{8,6},{9,23},{1... | collective-permute-start | bytes 344072 | tf_op jit(solution)/shard_map/ppermute | solution.py:95
  71.8 7.0 %collective-permute-start.22 = (bf16[16,3584]{1,0:T(8,128)(2,1)S(1)}, bf16[16,3584]{1,0:T(8,128)(2,1)S(1)}, u32[]{:S(2)}, u32[]{:S(2)}) collective-permute-start(bf16[16,3584]{1,0:T(8,128)(2,1)S(1)} %get-tuple-element.15), channel_id=1, source_target_pairs={{0,2},{2,4},{4,6},{6,0},{1,3},{3,5},{5,7},{7,1},{8,10},{10,12},{12... | collective-permute-start | bytes 344072 | tf_op jit(solution)/shard_map/ppermute | solution.py:49
  74.3 5.5 %collective-permute-start.21 = (bf16[16,3584]{1,0:T(8,128)(2,1)S(1)}, bf16[16,3584]{1,0:T(8,128)(2,1)S(1)}, u32[]{:S(2)}, u32[]{:S(2)}) collective-permute-start(bf16[16,3584]{1,0:T(8,128)(2,1)S(1)} %get-tuple-element.16), channel_id=1, source_target_pairs={{0,4},{2,6},{4,0},{6,2},{1,5},{3,7},{5,1},{7,3},{8,12},{10,14},{12... | collective-permute-start | bytes 344072 | tf_op jit(solution)/shard_map/ppermute | solution.py:49
  75.7 4.8 %collective-permute-start.20 = (bf16[16,3584]{1,0:T(8,128)(2,1)S(1)}, bf16[16,3584]{1,0:T(8,128)(2,1)S(1)}, u32[]{:S(2)}, u32[]{:S(2)}) collective-permute-start(bf16[16,3584]{1,0:T(8,128)(2,1)S(1)} %get-tuple-element.14), channel_id=1, source_target_pairs={{0,6},{2,0},{4,2},{6,4},{1,7},{3,1},{5,3},{7,5},{8,14},{10,8},{12,... | collective-permute-start | bytes 344072 | tf_op jit(solution)/shard_map/ppermute | solution.py:49
  78.8 6.7 %collective-permute-start.24 = (f32[8,3584]{1,0:T(8,128)S(1)}, f32[8,3584]{1,0:T(8,128)S(1)}, u32[]{:S(2)}, u32[]{:S(2)}) collective-permute-start(f32[8,3584]{1,0:T(8,128)S(1)} %get-tuple-element.29), channel_id=1, source_target_pairs={{0,1},{1,0},{2,3},{3,2},{4,5},{5,4},{6,7},{7,6},{8,9},{9,8},{10,11... | collective-permute-start | bytes 344072 | tf_op jit(solution)/shard_map/ppermute | solution.py:46
  79.7 1.4 %collective-permute-start.27 = (bf16[3,64,512]{2,1,0:T(8,128)(2,1)S(1)}, bf16[3,64,512]{2,1,0:T(8,128)(2,1)S(1)}, u32[]{:S(2)}, u32[]{:S(2)}) collective-permute-start(bf16[3,64,512]{2,1,0:T(8,128)(2,1)S(1)} %maximum_maximum_fusion), channel_id=1, source_target_pairs={{0,1},{1,0},{2,3},{3,2},{4,5},{5,4},{6,7},{7,6},{8,9},{9,8},{10,11... | collective-permute-start | bytes 589832 | tf_op jit(solution)/shard_map/ppermute | solution.py:46
  80.5 6.0 %collective-permute-start.29 = (bf16[3,64,1792]{2,1,0:T(8,128)(2,1)S(1)}, bf16[3,64,1792]{2,1,0:T(8,128)(2,1)S(1)}, u32[]{:S(2)}, u32[]{:S(2)}) collective-permute-start(bf16[3,64,1792]{2,1,0:T(8,128)(2,1)S(1)} %constant_dynamic-slice_fusion), channel_id=1, source_target_pairs={{0,1},{1,0},{2,3},{3,2},{4,5},{5,4},{6,7},{7,6},{8,9},{9,8},{10,11... | collective-permute-start | bytes 2064392 | tf_op jit(solution)/shard_map/ppermute | solution.py:46
  81.2 4.3 %collective-permute-start.25 = (f32[8,3584]{1,0:T(8,128)S(1)}, f32[8,3584]{1,0:T(8,128)S(1)}, u32[]{:S(2)}, u32[]{:S(2)}) collective-permute-start(f32[8,3584]{1,0:T(8,128)S(1)} %get-tuple-element.31), channel_id=1, source_target_pairs={{0,1},{1,0},{2,3},{3,2},{4,5},{5,4},{6,7},{7,6},{8,9},{9,8},{10,11... | collective-permute-start | bytes 344072 | tf_op jit(solution)/shard_map/ppermute | solution.py:46

commit v2 on v1

v2 whole, which is shorter than its diff:
```python
import functools

import jax
import jax.numpy as jnp
from jax import lax
from jax.experimental import pallas as pl
from jax.experimental.pallas import tpu as pltpu
from jax.sharding import PartitionSpec as P

AXES = ("pipe", "tensor", "dp")
BF16 = jnp.bfloat16
F32 = jnp.float32


def ring_pairs(sections, tensor_count, replicas, shift):
    pairs = []
    for p in range(sections):
        for t in range(tensor_count):
            to = (t + shift) % tensor_count
            for q in range(replicas):
                step = 1 if q % 2 else -1
                if 0 <= p + step < sections:
                    target = ((p + step) * tensor_count + to) * replicas + q
                else:
                    target = (p * tensor_count + to) * replicas + (q ^ 1)
                pairs.append(((p * tensor_count + t) * replicas + q, target))
    return pairs


def lane_block(width, most):
    best = 128
    for size in range(128, most + 1, 128):
        if width % size == 0:
            best = size
    return best


def factors_kernel(places, _, own_ref, peer_ref, w_ref, payload_ref, gate_ref, up_ref, hidden_ref, total, mixed):
    steps, batch_rows, depth = own_ref.shape[1], own_ref.shape[3], own_ref.shape[4]
    shard_rows = batch_rows // places
    hidden_width = hidden_ref.shape[2]
    count = steps * batch_rows
    step = pl.program_id(0)
    rows = jnp.concatenate(
        [own_ref[...].reshape(count, depth), peer_ref[...].reshape(count, depth)], axis=0
    )
    product = jnp.dot(rows, w_ref[0, 0], preferred_element_type=F32)

    @pl.when(step == 0)
    def _():
        total[...] = product

    @pl.when(step > 0)
    def _():
        total[...] += product

    @pl.when(step == pl.num_programs(0) - 1)
    def _():
        for k in range(steps):
            for j in range(places):
                for r in range(2):
                    source = (r * steps + k) * batch_rows + j * shard_rows
                    target = (2 * j + r) * shard_rows
                    mixed[k, target:target + shard_rows] = total[source:source + shard_rows]
        gate = mixed[:, :, :hidden_width]
        up = mixed[:, :, hidden_width:]
        sigmoid_val = jax.nn.sigmoid(gate)
        activated = gate * sigmoid_val
        gate_ref[...] = up * sigmoid_val * (1.0 + gate * (1.0 - sigmoid_val))
        up_ref[...] = activated
        hidden_ref[...] = (activated * up).astype(BF16)


def weight_grads_kernel(steps, replicas, places, _, *refs):
    saved = refs[:replicas]
    pre = refs[replicas:replicas + replicas * steps]
    hidden = refs[replicas + replicas * steps:2 * replicas + replicas * steps]
    dy = refs[2 * replicas + replicas * steps:2 * replicas + 2 * replicas * steps]
    in_ref, down_ref, pre_rows, hidden_rows = refs[-4:]
    batch_rows, block = saved[0].shape[3], saved[0].shape[4]
    pair_rows = 2 * batch_rows
    shard_rows = batch_rows // places
    count = steps * batch_rows

    def columns_of(parity):
        return jnp.concatenate(
            [dy[offset * steps + k][...] for offset in range(parity, replicas, 2) for k in range(steps)], axis=0
        )

    for parity in range(2):

        @pl.when(pl.program_id(0) == parity)
        def _(parity=parity):
            @pl.when(pl.program_id(1) == 0)
            def _():
                for pair in range(replicas // 2):
                    offset = 2 * pair + parity
                    hidden_rows[pair * 2 * count:(pair + 1) * 2 * count] = hidden[offset][...].reshape(
                        2 * count, hidden[offset].shape[2]
                    )
                    for k in range(steps):
                        values = pre[offset * steps + k][...].astype(F32)
                        for r in range(2):
                            half = jnp.concatenate(
                                [
                                    values[(2 * j + r) * shard_rows:(2 * j + r + 1) * shard_rows]
                                    for j in range(places)
                                ],
                                axis=0,
                            )
                            start = ((2 * pair + (r ^ parity)) * steps + k) * batch_rows
                            pre_rows[start:start + batch_rows] = half.astype(BF16)

            down_ref[0, 0] = lax.dot_general(
                hidden_rows[...], columns_of(parity), (((0,), (0,)), ((), ())), preferred_element_type=F32
            )

    inputs = jnp.concatenate([x[...].reshape(count, block) for x in saved], axis=0)
    in_ref[0, 0] = lax.dot_general(
        inputs, pre_rows[...], (((0,), (0,)), ((), ())), preferred_element_type=F32
    )


def local(entry_grads, fresh_grads, saved_inputs, w_in, w_down):
    section = lax.axis_index("pipe")
    sections = lax.axis_size("pipe")
    place = lax.axis_index("tensor")
    tensor_count = lax.axis_size("tensor")
    replica = lax.axis_index("dp")
    replicas = lax.axis_size("dp")
    core = lax.rem(replica, 2)
    steps, _, batch_rows, width = saved_inputs.shape[1:]
    shard_rows = batch_rows // tensor_count
    block_rows = 2 * shard_rows
    pair_rows = 2 * batch_rows
    hidden_width = w_down.shape[2]
    part_width = width // replicas

    def mine(x):
        return jnp.where(core == 0, x[0], x[1])

    def theirs(x):
        return jnp.where(core == 0, x[1], x[0])

    def indexed(x):
        return lax.dynamic_index_in_dim(x, core, 0, keepdims=False)

    def by_direction(own, other):
        return jnp.where(core == 0, jnp.stack([own, other]), jnp.stack([other, own]))

    def to_core(x, offset=1):
        return lax.ppermute(x, "dp", [(i, i ^ offset) for i in range(replicas)])

    def rotate(x, shift):
        return lax.ppermute(x, "tensor", [(i, (i + shift) % tensor_count) for i in range(tensor_count)])

    def placed(blocks):
        rows = []
        for source in range(tensor_count):
            shift = lax.rem(place - source + tensor_count, tensor_count)
            block = blocks[0]
            for i in range(1, tensor_count):
                block = jnp.where(shift == i, blocks[i], block)
            rows.append(block)
        return jnp.concatenate(rows)

    entry = entry_grads[:, 0]
    entry_peer = to_core(entry_grads)[:, 0]
    incoming = jnp.concatenate([mine(entry), mine(entry_peer)])
    payload = incoming.astype(BF16)
    blocks = [payload] + [rotate(payload, s) for s in range(1, tensor_count)]
    saved = [saved_inputs] + [to_core(saved_inputs, offset) for offset in range(1, replicas)]
    which = jnp.stack([core, replica]).astype(jnp.int32)
    depth = lane_block(width, 512)
    gate_factor, activated, hidden = pl.pallas_call(
        functools.partial(factors_kernel, tensor_count),
        grid_spec=pltpu.PrefetchScalarGridSpec(
            num_scalar_prefetch=1,
            grid=(width // depth,),
            in_specs=[
                pl.BlockSpec((1, steps, 1, batch_rows, depth), lambda i, at: (at[0], 0, 0, 0, i)),
                pl.BlockSpec((1, steps, 1, batch_rows, depth), lambda i, at: (at[0], 0, 0, 0, i)),
                pl.BlockSpec((1, 1, depth, 2 * hidden_width), lambda i, at: (at[0], 0, i, 0)),
                pl.BlockSpec(memory_space=pl.ANY),
            ],
            out_specs=[pl.BlockSpec((steps, pair_rows, hidden_width), lambda i, at: (0, 0, 0))] * 3,
            scratch_shapes=[
                pltpu.VMEM((2 * steps * batch_rows, 2 * hidden_width), F32),
                pltpu.VMEM((steps, pair_rows, 2 * hidden_width), F32),
            ],
        ),
        out_shape=[
            jax.ShapeDtypeStruct((steps, pair_rows, hidden_width), F32),
            jax.ShapeDtypeStruct((steps, pair_rows, hidden_width), F32),
            jax.ShapeDtypeStruct((steps, pair_rows, hidden_width), BF16),
        ],
        compiler_params=pltpu.CompilerParams(vmem_limit_bytes=16 << 20),
        cost_estimate=pl.CostEstimate(flops=0, bytes_accessed=0, transcendentals=0),
        name="factors",
    )(which, saved[0], saved[1], w_in, payload)

    fresh_pair = jnp.concatenate(
        [to_core(mine(fresh_grads).astype(BF16)), theirs(fresh_grads).astype(BF16)], axis=1
    )
    at_end = section == jnp.where(core == 0, 0, sections - 1)
    w_in_dir = indexed(w_in[:, 0])
    w_down_dir = indexed(w_down[:, 0])

    blocks, gate_factor, activated = lax.optimization_barrier((blocks, gate_factor, activated))

    def weight_grads():
        hidden_all = [to_core(hidden, o) if o else hidden for o in range(replicas)]
        block = lane_block(part_width, 1024)
        blocks_each = part_width // block
        return pl.pallas_call(
            functools.partial(weight_grads_kernel, steps, replicas, tensor_count),
            grid_spec=pltpu.PrefetchScalarGridSpec(
                num_scalar_prefetch=1,
                grid=(2, blocks_each),
                in_specs=[
                    pl.BlockSpec(
                        (1, steps, 1, batch_rows, block),
                        lambda i, j, at: (at[0] ^ i, 0, 0, 0, at[1] * blocks_each + j),
                    )
                ] * replicas
                + [pl.BlockSpec((pair_rows, 2 * hidden_width), lambda i, j, at: (0, 0))] * (replicas * steps)
                + [pl.BlockSpec((steps, pair_rows, hidden_width), lambda i, j, at: (0, 0, 0))] * replicas
                + [pl.BlockSpec((pair_rows, block), lambda i, j, at: (0, at[1] * blocks_each + j))] * (replicas * steps),
                out_specs=[
                    pl.BlockSpec((1, 1, block, 2 * hidden_width), lambda i, j, at: (at[0] ^ i, 0, j, 0)),
                    pl.BlockSpec((1, 1, hidden_width, block), lambda i, j, at: (at[0] ^ i, 0, 0, j)),
                ],
                scratch_shapes=[
                    pltpu.VMEM((replicas * steps * batch_rows, 2 * hidden_width), BF16),
                    pltpu.VMEM((replicas * steps * batch_rows, hidden_width), BF16),
                ],
            ),
            out_shape=[
                jax.ShapeDtypeStruct((2, 1, part_width, 2 * hidden_width), F32),
                jax.ShapeDtypeStruct((2, 1, hidden_width, part_width), F32),
            ],
            compiler_params=pltpu.CompilerParams(vmem_limit_bytes=24 << 20),
            cost_estimate=pl.CostEstimate(flops=0, bytes_accessed=0, transcendentals=0),
            name="weight_grads",
        )(
            which,
            *saved,
            *[pre_all[k][o] for o in range(replicas) for k in range(steps)],
            *hidden_all,
            *[dy_all[k][o] for o in range(replicas) for k in range(steps)],
        )

    hand_offs = jnp.zeros((2, steps, shard_rows, width), F32)
    dy_all, pre_all = [], []
    for k in range(steps):
        dy = placed(blocks)
        dh = jnp.einsum("rd,hd->rh", dy, w_down_dir, preferred_element_type=F32)
        pre_grad = jnp.concatenate([dh * gate_factor[k], dh * activated[k]], axis=1).astype(BF16)
        part = jnp.einsum("rc,dc->rd", pre_grad, w_in_dir, preferred_element_type=F32).astype(BF16)
        part = part.reshape(tensor_count, block_rows, width)

        def part_for(target):
            return lax.dynamic_index_in_dim(part, target, 0, keepdims=False)

        own_part = part_for(place)
        parts = []
        for s in range(1, tensor_count):
            parts.append(rotate(part_for(lax.rem(place + s, tensor_count)), s))
        dy_all.append([to_core(dy, o) if o else dy for o in range(replicas)])
        pre_all.append([to_core(pre_grad, o) if o else pre_grad for o in range(replicas)])
        if k + 1 == steps:
            parts, grads = lax.optimization_barrier((parts, weight_grads()))
        summed = own_part.astype(F32)
        for x in parts:
            summed = summed + x.astype(F32)
        handed = incoming + summed
        if k + 1 < steps:
            payload = jnp.where(at_end, fresh_pair[k], handed.astype(BF16))
            blocks = [
                lax.ppermute(payload, AXES, ring_pairs(sections, tensor_count, replicas, s))
                for s in range(tensor_count)
            ]
        if k == 0:
            other = theirs(entry) + to_core(summed[shard_rows:])
        else:
            other = to_core(handed[shard_rows:])
        hand_offs = hand_offs.at[:, k].set(by_direction(handed[:shard_rows], other))
        incoming = blocks[0].astype(F32)
    return (hand_offs[:, :, None], *grads)


def solution(mesh):
    placed = (
        P(None, "pipe", ("dp", "tensor"), None),
        P(None, None, ("dp", "tensor"), None),
        P(None, None, "pipe", "dp", None),
        P(None, "pipe", None, "tensor"),
        P(None, "pipe", "tensor", None),
    )
    return jax.shard_map(
        local,
        mesh=mesh,
        in_specs=placed,
        out_specs=(
            P(None, None, "pipe", ("dp", "tensor"), None),
            P(None, "pipe", "dp", "tensor"),
            P(None, "pipe", "tensor", "dp"),
        ),
        check_vma=False,
    )
```

time: 89.3 us -> 74.8 us (0.84)
  Pallas kernels: 0 us -> 9.04 us
  waiting for transfers between devices: 29.7 us -> 21.1 us
  other arithmetic: 10.4 us -> 2.81 us
  matrix products: 11.7 us -> 5.72 us
  local copies, waits for them, and re-layouts: 10.5 us -> 5.79 us
  starting transfers between devices: 25.8 us -> 28.4 us
    pallas_call x0 -> x2, Pallas kernels: none -> 9.04 us  [the longest x1 5.97 us: weight_grads(): pl.pallas_call(functools.partial(weight_grads_kernel, steps, replicas, te...]
    ppermute x12, waiting for transfers between devices: 13.6 us -> 7.51 us  [rotate(): lax.ppermute(x, 'tensor', [(i, (i + shift) % tensor_count) for i in range...]
    dot_general x5 -> x0, matrix products: 5.98 us -> none  [the longest x1 3.72 us: local(): jnp.einsum('krd,dc->krc', rows, w_in_dir, preferred_element_type=F32)]
    select_n x2 -> x1, other arithmetic: 5.58 us -> 0.02 us  [by_direction(): jnp.where(core == 0, jnp.stack([own, other]), jnp.stack([other, own]))]
    unnamed x4 -> x0, other arithmetic: 3.34 us -> none
    convert_element_type x2 -> x0, local copies, waits for them, and re-layouts: 3.24 us -> none  [the longest x1 1.72 us: local(): fresh_other = to_core(mine(fresh_grads).astype(BF16))]
    ppermute x8, starting transfers between devices: 5 us -> 8.04 us  [local(): lax.ppermute(payload, AXES, ring_pairs(sections, tensor_count, replicas, s))]
    ppermute x8, waiting for transfers between devices: 15.4 us -> 12.6 us  [local(): lax.ppermute(payload, AXES, ring_pairs(sections, tensor_count, replicas, s))]
  transfers between devices with their start and end apart: 30 -> 33, of which waited for: 20 -> 13; matrix products, arithmetic and copies ran while one was open for 32% -> 12% of each run, Pallas kernels for 0% -> 12%
where the time goes in v2:
time: 74.8 us; the launch traced here: 73.8 us
  starting transfers between devices  28.4 us (38%)
  waiting for transfers between devices  21.1 us (28%)
  Pallas kernels  9.04 us (12%)
  local copies, waits for them, and re-layouts  5.79 us (8%)
  matrix products  5.72 us (8%)
  other arithmetic  2.81 us (4%)
  between operations  1 us (1%)
    ppermute x12, starting transfers between devices, rotate(): lax.ppermute(x, 'tensor', [(i, (i + shift) % tensor_count) for i in range...  16.6 us
    ppermute x8, waiting for transfers between devices, local(): lax.ppermute(payload, AXES, ring_pairs(sections, tensor_count, replicas, s))  12.6 us
    ppermute x8, starting transfers between devices, local(): lax.ppermute(payload, AXES, ring_pairs(sections, tensor_count, replicas, s))  8.04 us
    ppermute x12, waiting for transfers between devices, rotate(): lax.ppermute(x, 'tensor', [(i, (i + shift) % tensor_count) for i in range...  7.51 us
    pallas_call x1, Pallas kernels, weight_grads(): pl.pallas_call(functools.partial(weight_grads_kernel, steps, replicas, te...  5.97 us
    unnamed x14, local copies, waits for them, and re-layouts  5.59 us
    ppermute x13, starting transfers between devices, to_core(): return lax.ppermute(x, 'dp', [(i, i ^ offset) for i in range(replicas)])  3.72 us
    dot_general x3, matrix products, local(): jnp.einsum('rc,dc->rd', pre_grad, w_in_dir, preferred_element_type=F32)  3.67 us
  transfers between devices with their start and end apart: 33, of which 13 were waited for; matrix products, arithmetic and copies ran while one was open for 12% of the time, Pallas kernels for 12%

profile of v2, /device:TPU:0, one launch (start us, length us, event | category | flops | bytes accessed | tf_op | source)
XLA Modules:
  0.0 73.8 jit_solution(17293575705011432416)
XLA Ops:
  0.6 0.5 collective-permute-start
  1.2 1.1 %fusion.28 = (bf16[2,8,3584]{2,1,0:T(8,128)(2,1)S(1)}, bf16[2,8,3584]{2,1,0:T(8,128)(2,1)S(1)}) fusion(f32[2,2,8,3584]{3,2,1,0:T(8,128)} %param.12, pred[]{:T(512)S(6)} %eq.28), kind=kLoop, calls=%fused_computation.46 | loop fusion | flops 114688 | bytes 458753 | tf_op jit(solution)/shard_map/convert_element_type | solution.py:203
  2.3 0.5 collective-permute-start.9
  2.8 1.0 %select_bitcast_fusion = f32[8,3584]{1,0:T(8,128)S(1)} fusion(f32[2,1,8,3584]{3,2,1,0:T(8,128)} %param.11, pred[]{:T(512)S(6)} %eq.28), kind=kLoop, calls=%fused_computation.81 | loop fusion | flops 28672 | bytes 344065 | tf_op jit(solution)/shard_map/jit(_where)/select_n | solution.py:140
  3.8 2.6 %collective-permute-start.1 = (bf16[16,3584]{1,0:T(8,128)(2,1)S(1)}, bf16[16,3584]{1,0:T(8,128)(2,1)S(1)}, u32[]{:S(2)}, u32[]{:S(2)}) collective-permute-start(bf16[16,3584]{1,0:T(8,128)(2,1)S(1)} %fusion.26.payload_ref), channel_id=1, source_target_pairs={{0,2},{2,4},{4,6},{6,0},{1,3},{3,5},{5,7},{7,1},{8,10},{10,12},{12... | collective-permute-start | bytes 344072 | tf_op jit(solution)/shard_map/ppermute | solution.py:155
  6.5 1.5 %collective-permute-start.2 = (bf16[16,3584]{1,0:T(8,128)(2,1)S(1)}, bf16[16,3584]{1,0:T(8,128)(2,1)S(1)}, u32[]{:S(2)}, u32[]{:S(2)}) collective-permute-start(bf16[16,3584]{1,0:T(8,128)(2,1)S(1)} %fusion.26.payload_ref), channel_id=1, source_target_pairs={{0,4},{2,6},{4,0},{6,2},{1,5},{3,7},{5,1},{7,3},{8,12},{10,14},{12... | collective-permute-start | bytes 344072 | tf_op jit(solution)/shard_map/ppermute | solution.py:155
  8.0 1.4 %collective-permute-start.3 = (bf16[16,3584]{1,0:T(8,128)(2,1)S(1)}, bf16[16,3584]{1,0:T(8,128)(2,1)S(1)}, u32[]{:S(2)}, u32[]{:S(2)}) collective-permute-start(bf16[16,3584]{1,0:T(8,128)(2,1)S(1)} %fusion.26.payload_ref), channel_id=1, source_target_pairs={{0,6},{2,0},{4,2},{6,4},{1,7},{3,1},{5,3},{7,5},{8,14},{10,8},{12,... | collective-permute-start | bytes 344072 | tf_op jit(solution)/shard_map/ppermute | solution.py:155
  9.5 3.1 %copy-done = bf16[2,1,3584,512]{3,2,1,0:T(8,128)(2,1)S(1)} copy-done((bf16[2,1,3584,512]{3,2,1,0:T(8,128)(2,1)S(1)}, bf16[2,1,3584,512]{3,2,1,0:T(8,128)(2,1)}, u32[]{:S(2)}) %copy-start) | copy-done | bytes 7340056
  12.6 1.3 %copy-done.2 = bf16[2,3,1,32,3584]{4,3,2,1,0:T(8,128)(2,1)S(1)} copy-done((bf16[2,3,1,32,3584]{4,3,2,1,0:T(8,128)(2,1)S(1)}, bf16[2,3,1,32,3584]{4,3,2,1,0:T(8,128)(2,1)}, u32[]{:S(2)}) %copy-start.2) | copy-done | bytes 1376280
  13.9 3.1 %factors.1 = (f32[3,64,256]{2,1,0:T(8,128)S(1)}, f32[3,64,256]{2,1,0:T(8,128)S(1)}, bf16[3,64,256]{2,1,0:T(8,128)(2,1)S(1)}) custom-call(s32[2]{0:T(128)S(1)} %pad_add_fusion._, bf16[2,3,1,32,3584]{4,3,2,1,0:T(8,128)(2,1)S(1)} %copy-done.2, bf16[2,3,1,32,3584]{4,3,2,1,0:T(8,128)(2,1)S(1)} %collective-permute-done.4.peer_ref.refs_1_, ...), custom_call_target="tpu_custom_call" | custom-call | tf_op jit(solution)/shard_map/factors/pallas_call | solution.py:175
  17.1 0.7 fusion.41
  17.8 0.3 copy-done.1
  18.1 1.2 %convolution_convert_fusion.2 = bf16[64,3584]{1,0:T(8,128)(2,1)S(1)} fusion(bf16[2,1,3584,512]{3,2,1,0:T(8,128)(2,1)S(1)} %copy-done.1, s32[]{:T(128)S(6)} %select_n.307, bf16[64,256]{1,0:T(8,128)(2,1)S(1)} %get-tuple-element.111, bf16[64,256]{1,0:T(8,128)(2,1)S(1)} %get-tuple-element.110), kind=kOutput, calls=%fused_computation.2 | convolution fusion | flops 235241472 | bytes 4194308 | tf_op jit(solution)/shard_map/rc,dc->rd/dot_general | solution.py:259
  19.4 0.6 collective-permute-start.5
  20.0 0.5 collective-permute-start.6
  20.5 1.9 %collective-permute-start.7 = (bf16[16,3584]{1,0:T(8,128)(2,1)S(1)}, bf16[16,3584]{1,0:T(8,128)(2,1)S(1)}, u32[]{:S(2)}, u32[]{:S(2)}) collective-permute-start(bf16[16,3584]{1,0:T(8,128)(2,1)S(1)} %get-tuple-element.94), channel_id=1, source_target_pairs={{0,6},{2,0},{4,2},{6,4},{1,7},{3,1},{5,3},{7,5},{8,14},{10,8},{12,... | collective-permute-start | bytes 344072 | tf_op jit(solution)/shard_map/ppermute | solution.py:155
  22.6 3.7 %collective-permute-done.5 = bf16[16,3584]{1,0:T(8,128)(2,1)S(1)} collective-permute-done((bf16[16,3584]{1,0:T(8,128)(2,1)S(1)}, bf16[16,3584]{1,0:T(8,128)(2,1)S(1)}, u32[]{:S(2)}, u32[]{:S(2)}) %collective-permute-start.5) | collective-permute-done | bytes 114720 | tf_op jit(solution)/shard_map/ppermute | solution.py:155
  26.3 0.6 collective-permute-done.6
  27.0 0.8 %collective-permute-start.11 = (bf16[16,3584]{1,0:T(8,128)(2,1)S(1)}, bf16[16,3584]{1,0:T(8,128)(2,1)S(1)}, u32[]{:S(2)}, u32[]{:S(2)}) collective-permute-start(bf16[16,3584]{1,0:T(8,128)(2,1)S(1)} %get-tuple-element.76), channel_id=1, source_target_pairs={{0,7},{1,15},{2,1},{3,9},{4,3},{5,11},{6,5},{7,13},{8,6},{9,23},{1... | collective-permute-start | bytes 344072 | tf_op jit(solution)/shard_map/ppermute | solution.py:280
  27.8 2.0 %collective-permute-start.12 = (bf16[16,3584]{1,0:T(8,128)(2,1)S(1)}, bf16[16,3584]{1,0:T(8,128)(2,1)S(1)}, u32[]{:S(2)}, u32[]{:S(2)}) collective-permute-start(bf16[16,3584]{1,0:T(8,128)(2,1)S(1)} %get-tuple-element.76), channel_id=1, source_target_pairs={{0,5},{1,13},{2,7},{3,15},{4,1},{5,9},{6,3},{7,11},{8,4},{9,21},{1... | collective-permute-start | bytes 344072 | tf_op jit(solution)/shard_map/ppermute | solution.py:280
  29.8 1.5 %collective-permute-start.13 = (bf16[16,3584]{1,0:T(8,128)(2,1)S(1)}, bf16[16,3584]{1,0:T(8,128)(2,1)S(1)}, u32[]{:S(2)}, u32[]{:S(2)}) collective-permute-start(bf16[16,3584]{1,0:T(8,128)(2,1)S(1)} %get-tuple-element.76), channel_id=1, source_target_pairs={{0,3},{1,11},{2,5},{3,13},{4,7},{5,15},{6,1},{7,9},{8,2},{9,19},{1... | collective-permute-start | bytes 344072 | tf_op jit(solution)/shard_map/ppermute | solution.py:280
  31.3 0.4 collective-permute-done.10
  31.8 1.2 %collective-permute-start.8 = (f32[8,3584]{1,0:T(8,128)S(1)}, f32[8,3584]{1,0:T(8,128)S(1)}, u32[]{:S(2)}, u32[]{:S(2)}) collective-permute-start(f32[8,3584]{1,0:T(8,128)S(1)} %slice.165), channel_id=1, source_target_pairs={{0,1},{1,0},{2,3},{3,2},{4,5},{5,4},{6,7},{7,6},{8,9},{9,8},{10,11... | collective-permute-start | bytes 344072 | tf_op jit(solution)/shard_map/ppermute | solution.py:152
  33.0 1.2 %collective-permute-done.11 = bf16[16,3584]{1,0:T(8,128)(2,1)S(1)} collective-permute-done((bf16[16,3584]{1,0:T(8,128)(2,1)S(1)}, bf16[16,3584]{1,0:T(8,128)(2,1)S(1)}, u32[]{:S(2)}, u32[]{:S(2)}) %collective-permute-start.11) | collective-permute-done | bytes 114720 | tf_op jit(solution)/shard_map/ppermute | solution.py:280
  34.2 1.1 %collective-permute-done.12 = bf16[16,3584]{1,0:T(8,128)(2,1)S(1)} collective-permute-done((bf16[16,3584]{1,0:T(8,128)(2,1)S(1)}, bf16[16,3584]{1,0:T(8,128)(2,1)S(1)}, u32[]{:S(2)}, u32[]{:S(2)}) %collective-permute-start.12) | collective-permute-done | bytes 114720 | tf_op jit(solution)/shard_map/ppermute | solution.py:280
  35.3 2.2 %collective-permute-done.13 = bf16[16,3584]{1,0:T(8,128)(2,1)S(1)} collective-permute-done((bf16[16,3584]{1,0:T(8,128)(2,1)S(1)}, bf16[16,3584]{1,0:T(8,128)(2,1)S(1)}, u32[]{:S(2)}, u32[]{:S(2)}) %collective-permute-start.13) | collective-permute-done | bytes 114720 | tf_op jit(solution)/shard_map/ppermute | solution.py:280
  37.6 0.7 fusion.39
  38.3 1.2 %convolution_convert_fusion.1 = bf16[64,3584]{1,0:T(8,128)(2,1)S(1)} fusion(bf16[2,1,3584,512]{3,2,1,0:T(8,128)(2,1)S(1)} %copy-done.1, s32[]{:T(128)S(6)} %select_n.307, bf16[64,256]{1,0:T(8,128)(2,1)S(1)} %get-tuple-element.109, bf16[64,256]{1,0:T(8,128)(2,1)S(1)} %get-tuple-element.108), kind=kOutput, calls=%fused_computation.1 | convolution fusion | flops 235241472 | bytes 4194308 | tf_op jit(solution)/shard_map/rc,dc->rd/dot_general | solution.py:259
  39.6 0.1 collective-permute-start.14
  39.7 1.3 %collective-permute-start.15 = (bf16[16,3584]{1,0:T(8,128)(2,1)S(1)}, bf16[16,3584]{1,0:T(8,128)(2,1)S(1)}, u32[]{:S(2)}, u32[]{:S(2)}) collective-permute-start(bf16[16,3584]{1,0:T(8,128)(2,1)S(1)} %get-tuple-element.88), channel_id=1, source_target_pairs={{0,4},{2,6},{4,0},{6,2},{1,5},{3,7},{5,1},{7,3},{8,12},{10,14},{12... | collective-permute-start | bytes 344072 | tf_op jit(solution)/shard_map/ppermute | solution.py:155
  41.0 2.8 %collective-permute-start.16 = (bf16[16,3584]{1,0:T(8,128)(2,1)S(1)}, bf16[16,3584]{1,0:T(8,128)(2,1)S(1)}, u32[]{:S(2)}, u32[]{:S(2)}) collective-permute-start(bf16[16,3584]{1,0:T(8,128)(2,1)S(1)} %get-tuple-element.87), channel_id=1, source_target_pairs={{0,6},{2,0},{4,2},{6,4},{1,7},{3,1},{5,3},{7,5},{8,14},{10,8},{12,... | collective-permute-start | bytes 344072 | tf_op jit(solution)/shard_map/ppermute | solution.py:155
  44.0 2.6 %collective-permute-done.14 = bf16[16,3584]{1,0:T(8,128)(2,1)S(1)} collective-permute-done((bf16[16,3584]{1,0:T(8,128)(2,1)S(1)}, bf16[16,3584]{1,0:T(8,128)(2,1)S(1)}, u32[]{:S(2)}, u32[]{:S(2)}) %collective-permute-start.14) | collective-permute-done | bytes 114720 | tf_op jit(solution)/shard_map/ppermute | solution.py:155
  46.6 0.6 collective-permute-done.15
  47.3 2.4 %collective-permute-start.19 = (bf16[16,3584]{1,0:T(8,128)(2,1)S(1)}, bf16[16,3584]{1,0:T(8,128)(2,1)S(1)}, u32[]{:S(2)}, u32[]{:S(2)}) collective-permute-start(bf16[16,3584]{1,0:T(8,128)(2,1)S(1)} %get-tuple-element.74), channel_id=1, source_target_pairs={{0,7},{1,15},{2,1},{3,9},{4,3},{5,11},{6,5},{7,13},{8,6},{9,23},{1... | collective-permute-start | bytes 344072 | tf_op jit(solution)/shard_map/ppermute | solution.py:280
  49.8 1.3 %collective-permute-start.20 = (bf16[16,3584]{1,0:T(8,128)(2,1)S(1)}, bf16[16,3584]{1,0:T(8,128)(2,1)S(1)}, u32[]{:S(2)}, u32[]{:S(2)}) collective-permute-start(bf16[16,3584]{1,0:T(8,128)(2,1)S(1)} %get-tuple-element.74), channel_id=1, source_target_pairs={{0,5},{1,13},{2,7},{3,15},{4,1},{5,9},{6,3},{7,11},{8,4},{9,21},{1... | collective-permute-start | bytes 344072 | tf_op jit(solution)/shard_map/ppermute | solution.py:280
  51.1 1.9 %collective-permute-done.18 = bf16[16,3584]{1,0:T(8,128)(2,1)S(1)} collective-permute-done((bf16[16,3584]{1,0:T(8,128)(2,1)S(1)}, bf16[16,3584]{1,0:T(8,128)(2,1)S(1)}, u32[]{:S(2)}, u32[]{:S(2)}) %collective-permute-start.18) | collective-permute-done | bytes 114720 | tf_op jit(solution)/shard_map/ppermute | solution.py:280
  53.0 2.5 %collective-permute-done.19 = bf16[16,3584]{1,0:T(8,128)(2,1)S(1)} collective-permute-done((bf16[16,3584]{1,0:T(8,128)(2,1)S(1)}, bf16[16,3584]{1,0:T(8,128)(2,1)S(1)}, u32[]{:S(2)}, u32[]{:S(2)}) %collective-permute-start.19) | collective-permute-done | bytes 114720 | tf_op jit(solution)/shard_map/ppermute | solution.py:280
  55.5 0.9 %collective-permute-done.20 = bf16[16,3584]{1,0:T(8,128)(2,1)S(1)} collective-permute-done((bf16[16,3584]{1,0:T(8,128)(2,1)S(1)}, bf16[16,3584]{1,0:T(8,128)(2,1)S(1)}, u32[]{:S(2)}, u32[]{:S(2)}) %collective-permute-start.20) | collective-permute-done | bytes 114720 | tf_op jit(solution)/shard_map/ppermute | solution.py:280
  56.4 2.4 %collective-permute-done.21 = bf16[16,3584]{1,0:T(8,128)(2,1)S(1)} collective-permute-done((bf16[16,3584]{1,0:T(8,128)(2,1)S(1)}, bf16[16,3584]{1,0:T(8,128)(2,1)S(1)}, u32[]{:S(2)}, u32[]{:S(2)}) %collective-permute-start.21) | collective-permute-done | bytes 114720 | tf_op jit(solution)/shard_map/ppermute | solution.py:280
  58.9 0.7 fusion.37
  59.6 1.2 %convolution_convert_fusion = bf16[64,3584]{1,0:T(8,128)(2,1)S(1)} fusion(bf16[2,1,3584,512]{3,2,1,0:T(8,128)(2,1)S(1)} %copy-done.1, s32[]{:T(128)S(6)} %select_n.307, bf16[64,256]{1,0:T(8,128)(2,1)S(1)} %get-tuple-element.107, bf16[64,256]{1,0:T(8,128)(2,1)S(1)} %get-tuple-element.106), kind=kOutput, calls=%fused_computation | convolution fusion | flops 235241472 | bytes 4194308 | tf_op jit(solution)/shard_map/rc,dc->rd/dot_general | solution.py:259
  61.0 0.5 collective-permute-start.30
  61.6 0.9 %collective-permute-start.23 = (bf16[16,3584]{1,0:T(8,128)(2,1)S(1)}, bf16[16,3584]{1,0:T(8,128)(2,1)S(1)}, u32[]{:S(2)}, u32[]{:S(2)}) collective-permute-start(bf16[16,3584]{1,0:T(8,128)(2,1)S(1)} %get-tuple-element.80), channel_id=1, source_target_pairs={{0,4},{2,6},{4,0},{6,2},{1,5},{3,7},{5,1},{7,3},{8,12},{10,14},{12... | collective-permute-start | bytes 344072 | tf_op jit(solution)/shard_map/ppermute | solution.py:155
  62.5 2.7 %collective-permute-start.24 = (bf16[16,3584]{1,0:T(8,128)(2,1)S(1)}, bf16[16,3584]{1,0:T(8,128)(2,1)S(1)}, u32[]{:S(2)}, u32[]{:S(2)}) collective-permute-start(bf16[16,3584]{1,0:T(8,128)(2,1)S(1)} %get-tuple-element.79), channel_id=1, source_target_pairs={{0,6},{2,0},{4,2},{6,4},{1,7},{3,1},{5,3},{7,5},{8,14},{10,8},{12,... | collective-permute-start | bytes 344072 | tf_op jit(solution)/shard_map/ppermute | solution.py:155
  65.4 6.0 %weight_grads.1 = (f32[2,1,1792,512]{3,2,1,0:T(8,128)}, f32[2,1,256,1792]{3,2,1,0:T(8,128)}) custom-call(s32[2]{0:T(128)S(1)} %pad_add_fusion._, bf16[2,3,1,32,3584]{4,3,2,1,0:T(8,128)(2,1)S(1)} %copy-done.3, bf16[2,3,1,32,3584]{4,3,2,1,0:T(8,128)(2,1)S(1)} %collective-permute-done.4.peer_ref.refs_1_, bf16[64,512]{1,0:T(8,128)(2,1)S(1)} %pad_maximum_fusion.5.refs_2_, ...), custom_call_target="tpu_custom_call" | custom-call | tf_op jit(solution)/shard_map/weight_grads/pallas_call | solution.py:215
  71.5 0.5 collective-permute-start.32
  72.0 0.9 %collective-permute-done.32 = f32[8,3584]{1,0:T(8,128)S(1)} collective-permute-done((f32[8,3584]{1,0:T(8,128)S(1)}, f32[8,3584]{1,0:T(8,128)S(1)}, u32[]{:S(2)}, u32[]{:S(2)}) %collective-permute-start.32) | collective-permute-done | bytes 114720 | tf_op jit(solution)/shard_map/ppermute | solution.py:152
  73.0 0.8 %copy-done.5 = f32[2,3,1,8,3584]{4,3,1,0,2:T(8,128)} copy-done((f32[2,3,1,8,3584]{4,3,1,0,2:T(8,128)}, f32[2,3,1,8,3584]{4,3,1,0,2:T(8,128)S(1)}, u32[]{:S(2)}) %copy-start.5) | copy-done | bytes 688152
  (69 shorter events, 1.5 us)
Async XLA Ops:
  0.6 3.2 %collective-permute-start = (f32[2,1,8,3584]{3,2,1,0:T(8,128)}, f32[2,1,8,3584]{3,2,1,0:T(8,128)S(1)}, u32[]{:S(2)}, u32[]{:S(2)}) collective-permute-start(f32[2,1,8,3584]{3,2,1,0:T(8,128)} %param.11), channel_id=1, source_target_pairs={{0,1},{1,0},{2,3},{3,2},{4,5},{5,4},{6,7},{7,6},{8,9},{9,8},{10,11... | collective-permute-start | bytes 688136 | tf_op jit(solution)/shard_map/ppermute | solution.py:152
  1.1 8.3 %collective-permute-start.4 = (bf16[2,3,1,32,3584]{4,3,2,1,0:T(8,128)(2,1)}, bf16[2,3,1,32,3584]{4,3,2,1,0:T(8,128)(2,1)S(1)}, u32[]{:S(2)}, u32[]{:S(2)}) collective-permute-start(bf16[2,3,1,32,3584]{4,3,2,1,0:T(8,128)(2,1)} %refs_0_.1), channel_id=1, source_target_pairs={{0,1},{1,0},{2,3},{3,2},{4,5},{5,4},{6,7},{7,6},{8,9},{9,8},{10,11... | collective-permute-start | bytes 4128776 | tf_op jit(solution)/shard_map/ppermute | solution.py:152
  2.3 20.3 %collective-permute-start.9 = (bf16[2,8,3584]{2,1,0:T(8,128)(2,1)S(1)}, bf16[2,8,3584]{2,1,0:T(8,128)(2,1)S(1)}, u32[]{:S(2)}, u32[]{:S(2)}) collective-permute-start(bf16[2,8,3584]{2,1,0:T(8,128)(2,1)S(1)} %get-tuple-element.101), channel_id=1, source_target_pairs={{0,1},{1,0},{2,3},{3,2},{4,5},{5,4},{6,7},{7,6},{8,9},{9,8},{10,11... | collective-permute-start | bytes 344072 | tf_op jit(solution)/shard_map/ppermute | solution.py:152
  3.8 13.2 %collective-permute-start.1 = (bf16[16,3584]{1,0:T(8,128)(2,1)S(1)}, bf16[16,3584]{1,0:T(8,128)(2,1)S(1)}, u32[]{:S(2)}, u32[]{:S(2)}) collective-permute-start(bf16[16,3584]{1,0:T(8,128)(2,1)S(1)} %fusion.26.payload_ref), channel_id=1, source_target_pairs={{0,2},{2,4},{4,6},{6,0},{1,3},{3,5},{5,7},{7,1},{8,10},{10,12},{12... | collective-permute-start | bytes 344072 | tf_op jit(solution)/shard_map/ppermute | solution.py:155
  6.5 10.6 %collective-permute-start.2 = (bf16[16,3584]{1,0:T(8,128)(2,1)S(1)}, bf16[16,3584]{1,0:T(8,128)(2,1)S(1)}, u32[]{:S(2)}, u32[]{:S(2)}) collective-permute-start(bf16[16,3584]{1,0:T(8,128)(2,1)S(1)} %fusion.26.payload_ref), channel_id=1, source_target_pairs={{0,4},{2,6},{4,0},{6,2},{1,5},{3,7},{5,1},{7,3},{8,12},{10,14},{12... | collective-permute-start | bytes 344072 | tf_op jit(solution)/shard_map/ppermute | solution.py:155
  8.0 9.1 %collective-permute-start.3 = (bf16[16,3584]{1,0:T(8,128)(2,1)S(1)}, bf16[16,3584]{1,0:T(8,128)(2,1)S(1)}, u32[]{:S(2)}, u32[]{:S(2)}) collective-permute-start(bf16[16,3584]{1,0:T(8,128)(2,1)S(1)} %fusion.26.payload_ref), channel_id=1, source_target_pairs={{0,6},{2,0},{4,2},{6,4},{1,7},{3,1},{5,3},{7,5},{8,14},{10,8},{12,... | collective-permute-start | bytes 344072 | tf_op jit(solution)/shard_map/ppermute | solution.py:155
  9.5 3.1 %copy-start = (bf16[2,1,3584,512]{3,2,1,0:T(8,128)(2,1)S(1)}, bf16[2,1,3584,512]{3,2,1,0:T(8,128)(2,1)}, u32[]{:S(2)}) copy-start(bf16[2,1,3584,512]{3,2,1,0:T(8,128)(2,1)} %w_ref.1) | copy-start | bytes 22020100
  12.6 1.3 %copy-start.2 = (bf16[2,3,1,32,3584]{4,3,2,1,0:T(8,128)(2,1)S(1)}, bf16[2,3,1,32,3584]{4,3,2,1,0:T(8,128)(2,1)}, u32[]{:S(2)}) copy-start(bf16[2,3,1,32,3584]{4,3,2,1,0:T(8,128)(2,1)} %refs_0_.1) | copy-start | bytes 4128772
  13.9 3.2 %copy-start.6 = (bf16[2,1,256,3584]{3,2,1,0:T(8,128)(2,1)S(1)}, bf16[2,1,256,3584]{3,2,1,0:T(8,128)(2,1)}, u32[]{:S(2)}) copy-start(bf16[2,1,256,3584]{3,2,1,0:T(8,128)(2,1)} %param.15) | copy-start | bytes 11010052
  13.9 4.2 %copy-start.1 = (bf16[2,1,3584,512]{3,2,1,0:T(8,128)(2,1)S(1)}, bf16[2,1,3584,512]{3,2,1,0:T(8,128)(2,1)}, u32[]{:S(2)}) copy-start(bf16[2,1,3584,512]{3,2,1,0:T(8,128)(2,1)} %w_ref.1) | copy-start | bytes 22020100
  19.4 6.9 %collective-permute-start.5 = (bf16[16,3584]{1,0:T(8,128)(2,1)S(1)}, bf16[16,3584]{1,0:T(8,128)(2,1)S(1)}, u32[]{:S(2)}, u32[]{:S(2)}) collective-permute-start(bf16[16,3584]{1,0:T(8,128)(2,1)S(1)} %get-tuple-element.93), channel_id=1, source_target_pairs={{0,2},{2,4},{4,6},{6,0},{1,3},{3,5},{5,7},{7,1},{8,10},{10,12},{12... | collective-permute-start | bytes 344072 | tf_op jit(solution)/shard_map/ppermute | solution.py:155
  20.0 6.8 %collective-permute-start.6 = (bf16[16,3584]{1,0:T(8,128)(2,1)S(1)}, bf16[16,3584]{1,0:T(8,128)(2,1)S(1)}, u32[]{:S(2)}, u32[]{:S(2)}) collective-permute-start(bf16[16,3584]{1,0:T(8,128)(2,1)S(1)} %get-tuple-element.95), channel_id=1, source_target_pairs={{0,4},{2,6},{4,0},{6,2},{1,5},{3,7},{5,1},{7,3},{8,12},{10,14},{12... | collective-permute-start | bytes 344072 | tf_op jit(solution)/shard_map/ppermute | solution.py:155
  20.5 6.3 %collective-permute-start.7 = (bf16[16,3584]{1,0:T(8,128)(2,1)S(1)}, bf16[16,3584]{1,0:T(8,128)(2,1)S(1)}, u32[]{:S(2)}, u32[]{:S(2)}) collective-permute-start(bf16[16,3584]{1,0:T(8,128)(2,1)S(1)} %get-tuple-element.94), channel_id=1, source_target_pairs={{0,6},{2,0},{4,2},{6,4},{1,7},{3,1},{5,3},{7,5},{8,14},{10,8},{12,... | collective-permute-start | bytes 344072 | tf_op jit(solution)/shard_map/ppermute | solution.py:155
  22.5 39.1 %collective-permute-start.29 = (bf16[64,3584]{1,0:T(8,128)(2,1)S(1)}, bf16[64,3584]{1,0:T(8,128)(2,1)S(1)}, u32[]{:S(2)}, u32[]{:S(2)}) collective-permute-start(bf16[64,3584]{1,0:T(8,128)(2,1)S(1)} %pad_maximum_fusion.refs_10_), channel_id=1, source_target_pairs={{0,1},{1,0},{2,3},{3,2},{4,5},{5,4},{6,7},{7,6},{8,9},{9,8},{10,11... | collective-permute-start | bytes 1376264 | tf_op jit(solution)/shard_map/ppermute | solution.py:152
  27.0 4.8 %collective-permute-start.10 = (bf16[16,3584]{1,0:T(8,128)(2,1)S(1)}, bf16[16,3584]{1,0:T(8,128)(2,1)S(1)}, u32[]{:S(2)}, u32[]{:S(2)}) collective-permute-start(bf16[16,3584]{1,0:T(8,128)(2,1)S(1)} %get-tuple-element.76), channel_id=1, source_target_pairs={{0,1},{1,9},{2,3},{3,11},{4,5},{5,13},{6,7},{7,15},{8,0},{9,17},{1... | collective-permute-start | bytes 344072 | tf_op jit(solution)/shard_map/ppermute | solution.py:280
  27.0 7.2 %collective-permute-start.11 = (bf16[16,3584]{1,0:T(8,128)(2,1)S(1)}, bf16[16,3584]{1,0:T(8,128)(2,1)S(1)}, u32[]{:S(2)}, u32[]{:S(2)}) collective-permute-start(bf16[16,3584]{1,0:T(8,128)(2,1)S(1)} %get-tuple-element.76), channel_id=1, source_target_pairs={{0,7},{1,15},{2,1},{3,9},{4,3},{5,11},{6,5},{7,13},{8,6},{9,23},{1... | collective-permute-start | bytes 344072 | tf_op jit(solution)/shard_map/ppermute | solution.py:280
  27.8 7.4 %collective-permute-start.12 = (bf16[16,3584]{1,0:T(8,128)(2,1)S(1)}, bf16[16,3584]{1,0:T(8,128)(2,1)S(1)}, u32[]{:S(2)}, u32[]{:S(2)}) collective-permute-start(bf16[16,3584]{1,0:T(8,128)(2,1)S(1)} %get-tuple-element.76), channel_id=1, source_target_pairs={{0,5},{1,13},{2,7},{3,15},{4,1},{5,9},{6,3},{7,11},{8,4},{9,21},{1... | collective-permute-start | bytes 344072 | tf_op jit(solution)/shard_map/ppermute | solution.py:280
  29.8 7.7 %collective-permute-start.13 = (bf16[16,3584]{1,0:T(8,128)(2,1)S(1)}, bf16[16,3584]{1,0:T(8,128)(2,1)S(1)}, u32[]{:S(2)}, u32[]{:S(2)}) collective-permute-start(bf16[16,3584]{1,0:T(8,128)(2,1)S(1)} %get-tuple-element.76), channel_id=1, source_target_pairs={{0,3},{1,11},{2,5},{3,13},{4,7},{5,15},{6,1},{7,9},{8,2},{9,19},{1... | collective-permute-start | bytes 344072 | tf_op jit(solution)/shard_map/ppermute | solution.py:280
  31.8 12.1 %collective-permute-start.8 = (f32[8,3584]{1,0:T(8,128)S(1)}, f32[8,3584]{1,0:T(8,128)S(1)}, u32[]{:S(2)}, u32[]{:S(2)}) collective-permute-start(f32[8,3584]{1,0:T(8,128)S(1)} %slice.165), channel_id=1, source_target_pairs={{0,1},{1,0},{2,3},{3,2},{4,5},{5,4},{6,7},{7,6},{8,9},{9,8},{10,11... | collective-permute-start | bytes 344072 | tf_op jit(solution)/shard_map/ppermute | solution.py:152
  37.6 6.3 %copy-start.4 = (f32[2,1,8,3584]{3,2,1,0:T(8,128)S(1)}, f32[2,1,8,3584]{3,2,1,0:T(8,128)}, u32[]{:S(2)}) copy-start(f32[2,1,8,3584]{3,2,1,0:T(8,128)} %param.11) | copy-start | bytes 688132
  39.6 7.0 %collective-permute-start.14 = (bf16[16,3584]{1,0:T(8,128)(2,1)S(1)}, bf16[16,3584]{1,0:T(8,128)(2,1)S(1)}, u32[]{:S(2)}, u32[]{:S(2)}) collective-permute-start(bf16[16,3584]{1,0:T(8,128)(2,1)S(1)} %get-tuple-element.86), channel_id=1, source_target_pairs={{0,2},{2,4},{4,6},{6,0},{1,3},{3,5},{5,7},{7,1},{8,10},{10,12},{12... | collective-permute-start | bytes 344072 | tf_op jit(solution)/shard_map/ppermute | solution.py:155
  39.7 7.5 %collective-permute-start.15 = (bf16[16,3584]{1,0:T(8,128)(2,1)S(1)}, bf16[16,3584]{1,0:T(8,128)(2,1)S(1)}, u32[]{:S(2)}, u32[]{:S(2)}) collective-permute-start(bf16[16,3584]{1,0:T(8,128)(2,1)S(1)} %get-tuple-element.88), channel_id=1, source_target_pairs={{0,4},{2,6},{4,0},{6,2},{1,5},{3,7},{5,1},{7,3},{8,12},{10,14},{12... | collective-permute-start | bytes 344072 | tf_op jit(solution)/shard_map/ppermute | solution.py:155
  41.0 6.2 %collective-permute-start.16 = (bf16[16,3584]{1,0:T(8,128)(2,1)S(1)}, bf16[16,3584]{1,0:T(8,128)(2,1)S(1)}, u32[]{:S(2)}, u32[]{:S(2)}) collective-permute-start(bf16[16,3584]{1,0:T(8,128)(2,1)S(1)} %get-tuple-element.87), channel_id=1, source_target_pairs={{0,6},{2,0},{4,2},{6,4},{1,7},{3,1},{5,3},{7,5},{8,14},{10,8},{12,... | collective-permute-start | bytes 344072 | tf_op jit(solution)/shard_map/ppermute | solution.py:155
  47.3 5.7 %collective-permute-start.18 = (bf16[16,3584]{1,0:T(8,128)(2,1)S(1)}, bf16[16,3584]{1,0:T(8,128)(2,1)S(1)}, u32[]{:S(2)}, u32[]{:S(2)}) collective-permute-start(bf16[16,3584]{1,0:T(8,128)(2,1)S(1)} %get-tuple-element.74), channel_id=1, source_target_pairs={{0,1},{1,9},{2,3},{3,11},{4,5},{5,13},{6,7},{7,15},{8,0},{9,17},{1... | collective-permute-start | bytes 344072 | tf_op jit(solution)/shard_map/ppermute | solution.py:280
  47.3 8.1 %collective-permute-start.19 = (bf16[16,3584]{1,0:T(8,128)(2,1)S(1)}, bf16[16,3584]{1,0:T(8,128)(2,1)S(1)}, u32[]{:S(2)}, u32[]{:S(2)}) collective-permute-start(bf16[16,3584]{1,0:T(8,128)(2,1)S(1)} %get-tuple-element.74), channel_id=1, source_target_pairs={{0,7},{1,15},{2,1},{3,9},{4,3},{5,11},{6,5},{7,13},{8,6},{9,23},{1... | collective-permute-start | bytes 344072 | tf_op jit(solution)/shard_map/ppermute | solution.py:280
  49.8 6.7 %collective-permute-start.20 = (bf16[16,3584]{1,0:T(8,128)(2,1)S(1)}, bf16[16,3584]{1,0:T(8,128)(2,1)S(1)}, u32[]{:S(2)}, u32[]{:S(2)}) collective-permute-start(bf16[16,3584]{1,0:T(8,128)(2,1)S(1)} %get-tuple-element.74), channel_id=1, source_target_pairs={{0,5},{1,13},{2,7},{3,15},{4,1},{5,9},{6,3},{7,11},{8,4},{9,21},{1... | collective-permute-start | bytes 344072 | tf_op jit(solution)/shard_map/ppermute | solution.py:280
  51.0 7.8 %collective-permute-start.21 = (bf16[16,3584]{1,0:T(8,128)(2,1)S(1)}, bf16[16,3584]{1,0:T(8,128)(2,1)S(1)}, u32[]{:S(2)}, u32[]{:S(2)}) collective-permute-start(bf16[16,3584]{1,0:T(8,128)(2,1)S(1)} %get-tuple-element.74), channel_id=1, source_target_pairs={{0,3},{1,11},{2,5},{3,13},{4,7},{5,15},{6,1},{7,9},{8,2},{9,19},{1... | collective-permute-start | bytes 344072 | tf_op jit(solution)/shard_map/ppermute | solution.py:280
  53.0 7.9 %collective-permute-start.25 = (bf16[64,512]{1,0:T(8,128)(2,1)S(1)}, bf16[64,512]{1,0:T(8,128)(2,1)S(1)}, u32[]{:S(2)}, u32[]{:S(2)}) collective-permute-start(bf16[64,512]{1,0:T(8,128)(2,1)S(1)} %pad_maximum_fusion.5.refs_2_), channel_id=1, source_target_pairs={{0,1},{1,0},{2,3},{3,2},{4,5},{5,4},{6,7},{7,6},{8,9},{9,8},{10,11... | collective-permute-start | bytes 196616 | tf_op jit(solution)/shard_map/ppermute | solution.py:152
  55.5 6.0 %collective-permute-start.28 = (bf16[3,64,256]{2,1,0:T(8,128)(2,1)S(1)}, bf16[3,64,256]{2,1,0:T(8,128)(2,1)S(1)}, u32[]{:S(2)}, u32[]{:S(2)}) collective-permute-start(bf16[3,64,256]{2,1,0:T(8,128)(2,1)S(1)} %get-tuple-element.63.refs_8_), channel_id=1, source_target_pairs={{0,1},{1,0},{2,3},{3,2},{4,5},{5,4},{6,7},{7,6},{8,9},{9,8},{10,11... | collective-permute-start | bytes 294920 | tf_op jit(solution)/shard_map/ppermute | solution.py:152
  56.4 5.2 %collective-permute-start.26 = (bf16[64,512]{1,0:T(8,128)(2,1)S(1)}, bf16[64,512]{1,0:T(8,128)(2,1)S(1)}, u32[]{:S(2)}, u32[]{:S(2)}) collective-permute-start(bf16[64,512]{1,0:T(8,128)(2,1)S(1)} %pad_maximum_fusion.6.refs_3_), channel_id=1, source_target_pairs={{0,1},{1,0},{2,3},{3,2},{4,5},{5,4},{6,7},{7,6},{8,9},{9,8},{10,11... | collective-permute-start | bytes 196616 | tf_op jit(solution)/shard_map/ppermute | solution.py:152
  58.9 6.5 %copy-start.3 = (bf16[2,3,1,32,3584]{4,3,2,1,0:T(8,128)(2,1)S(1)}, bf16[2,3,1,32,3584]{4,3,2,1,0:T(8,128)(2,1)}, u32[]{:S(2)}) copy-start(bf16[2,3,1,32,3584]{4,3,2,1,0:T(8,128)(2,1)} %refs_0_.1) | copy-start | bytes 4128772
  60.8 1.7 %collective-permute-start.27 = (bf16[64,512]{1,0:T(8,128)(2,1)S(1)}, bf16[64,512]{1,0:T(8,128)(2,1)S(1)}, u32[]{:S(2)}, u32[]{:S(2)}) collective-permute-start(bf16[64,512]{1,0:T(8,128)(2,1)S(1)} %pad_maximum_fusion.7.refs_4_), channel_id=1, source_target_pairs={{0,1},{1,0},{2,3},{3,2},{4,5},{5,4},{6,7},{7,6},{8,9},{9,8},{10,11... | collective-permute-start | bytes 196616 | tf_op jit(solution)/shard_map/ppermute | solution.py:152
  61.0 4.3 %collective-permute-start.30 = (bf16[64,3584]{1,0:T(8,128)(2,1)S(1)}, bf16[64,3584]{1,0:T(8,128)(2,1)S(1)}, u32[]{:S(2)}, u32[]{:S(2)}) collective-permute-start(bf16[64,3584]{1,0:T(8,128)(2,1)S(1)} %pad_maximum_fusion.1.refs_11_), channel_id=1, source_target_pairs={{0,1},{1,0},{2,3},{3,2},{4,5},{5,4},{6,7},{7,6},{8,9},{9,8},{10,11... | collective-permute-start | bytes 1376264 | tf_op jit(solution)/shard_map/ppermute | solution.py:152
  61.5 3.9 %collective-permute-start.31 = (bf16[64,3584]{1,0:T(8,128)(2,1)S(1)}, bf16[64,3584]{1,0:T(8,128)(2,1)S(1)}, u32[]{:S(2)}, u32[]{:S(2)}) collective-permute-start(bf16[64,3584]{1,0:T(8,128)(2,1)S(1)} %pad_maximum_fusion.2.refs_12_), channel_id=1, source_target_pairs={{0,1},{1,0},{2,3},{3,2},{4,5},{5,4},{6,7},{7,6},{8,9},{9,8},{10,11... | collective-permute-start | bytes 1376264 | tf_op jit(solution)/shard_map/ppermute | solution.py:152
  61.6 9.7 %collective-permute-start.22 = (bf16[16,3584]{1,0:T(8,128)(2,1)S(1)}, bf16[16,3584]{1,0:T(8,128)(2,1)S(1)}, u32[]{:S(2)}, u32[]{:S(2)}) collective-permute-start(bf16[16,3584]{1,0:T(8,128)(2,1)S(1)} %get-tuple-element.81), channel_id=1, source_target_pairs={{0,2},{2,4},{4,6},{6,0},{1,3},{3,5},{5,7},{7,1},{8,10},{10,12},{12... | collective-permute-start | bytes 344072 | tf_op jit(solution)/shard_map/ppermute | solution.py:155
  61.6 9.7 %collective-permute-start.23 = (bf16[16,3584]{1,0:T(8,128)(2,1)S(1)}, bf16[16,3584]{1,0:T(8,128)(2,1)S(1)}, u32[]{:S(2)}, u32[]{:S(2)}) collective-permute-start(bf16[16,3584]{1,0:T(8,128)(2,1)S(1)} %get-tuple-element.80), channel_id=1, source_target_pairs={{0,4},{2,6},{4,0},{6,2},{1,5},{3,7},{5,1},{7,3},{8,12},{10,14},{12... | collective-permute-start | bytes 344072 | tf_op jit(solution)/shard_map/ppermute | solution.py:155
  62.5 8.8 %collective-permute-start.24 = (bf16[16,3584]{1,0:T(8,128)(2,1)S(1)}, bf16[16,3584]{1,0:T(8,128)(2,1)S(1)}, u32[]{:S(2)}, u32[]{:S(2)}) collective-permute-start(bf16[16,3584]{1,0:T(8,128)(2,1)S(1)} %get-tuple-element.79), channel_id=1, source_target_pairs={{0,6},{2,0},{4,2},{6,4},{1,7},{3,1},{5,3},{7,5},{8,14},{10,8},{12,... | collective-permute-start | bytes 344072 | tf_op jit(solution)/shard_map/ppermute | solution.py:155
  65.3 6.7 %collective-permute-start.17 = (f32[8,3584]{1,0:T(8,128)S(1)}, f32[8,3584]{1,0:T(8,128)S(1)}, u32[]{:S(2)}, u32[]{:S(2)}) collective-permute-start(f32[8,3584]{1,0:T(8,128)S(1)} %get-tuple-element.105), channel_id=1, source_target_pairs={{0,1},{1,0},{2,3},{3,2},{4,5},{5,4},{6,7},{7,6},{8,9},{9,8},{10,11... | collective-permute-start | bytes 344072 | tf_op jit(solution)/shard_map/ppermute | solution.py:152
  71.5 1.5 %collective-permute-start.32 = (f32[8,3584]{1,0:T(8,128)S(1)}, f32[8,3584]{1,0:T(8,128)S(1)}, u32[]{:S(2)}, u32[]{:S(2)}) collective-permute-start(f32[8,3584]{1,0:T(8,128)S(1)} %get-tuple-element.103), channel_id=1, source_target_pairs={{0,1},{1,0},{2,3},{3,2},{4,5},{5,4},{6,7},{7,6},{8,9},{9,8},{10,11... | collective-permute-start | bytes 344072 | tf_op jit(solution)/shard_map/ppermute | solution.py:152
  73.0 0.9 %copy-start.5 = (f32[2,3,1,8,3584]{4,3,1,0,2:T(8,128)}, f32[2,3,1,8,3584]{4,3,1,0,2:T(8,128)S(1)}, u32[]{:S(2)}) copy-start(f32[2,3,1,8,3584]{4,3,1,0,2:T(8,128)S(1)} %fusion.16) | copy-start | bytes 2064388

commit v3 on v2

--- a/solution.py
+++ b/solution.py
@@ -35,7 +35,10 @@
     return best
 
 
-def factors_kernel(places, _, own_ref, peer_ref, w_ref, payload_ref, gate_ref, up_ref, hidden_ref, total, mixed):
+def factors_kernel(
+    places, at, own_ref, peer_ref, w_ref, down_ref, fresh_ref, _,
+    gate_ref, up_ref, hidden_ref, send_ref, keep_ref, w_copy, down_copy, total, mixed
+):
     steps, batch_rows, depth = own_ref.shape[1], own_ref.shape[3], own_ref.shape[4]
     shard_rows = batch_rows // places
     hidden_width = hidden_ref.shape[2]
@@ -44,11 +47,16 @@
     rows = jnp.concatenate(
         [own_ref[...].reshape(count, depth), peer_ref[...].reshape(count, depth)], axis=0
     )
-    product = jnp.dot(rows, w_ref[0, 0], preferred_element_type=F32)
+    weights = w_ref[0, 0]
+    product = jnp.dot(rows, weights, preferred_element_type=F32)
+    w_copy[...] = weights
+    down_copy[...] = down_ref[0, 0]
 
     @pl.when(step == 0)
     def _():
         total[...] = product
+        send_ref[...] = fresh_ref[at[0]].astype(BF16)
+        keep_ref[...] = fresh_ref[1 - at[0]].astype(BF16)
 
     @pl.when(step > 0)
     def _():
@@ -171,8 +179,8 @@
     blocks = [payload] + [rotate(payload, s) for s in range(1, tensor_count)]
     saved = [saved_inputs] + [to_core(saved_inputs, offset) for offset in range(1, replicas)]
     which = jnp.stack([core, replica]).astype(jnp.int32)
-    depth = lane_block(width, 512)
-    gate_factor, activated, hidden = pl.pallas_call(
+    depth = lane_block(width, 1792)
+    gate_factor, activated, hidden, fresh_send, fresh_keep, w_in_dir, w_down_dir = pl.pallas_call(
         functools.partial(factors_kernel, tensor_count),
         grid_spec=pltpu.PrefetchScalarGridSpec(
             num_scalar_prefetch=1,
@@ -181,9 +189,16 @@
                 pl.BlockSpec((1, steps, 1, batch_rows, depth), lambda i, at: (at[0], 0, 0, 0, i)),
                 pl.BlockSpec((1, steps, 1, batch_rows, depth), lambda i, at: (at[0], 0, 0, 0, i)),
                 pl.BlockSpec((1, 1, depth, 2 * hidden_width), lambda i, at: (at[0], 0, i, 0)),
+                pl.BlockSpec((1, 1, hidden_width, depth), lambda i, at: (at[0], 0, 0, i)),
+                pl.BlockSpec(fresh_grads.shape, lambda i, at: (0, 0, 0, 0)),
                 pl.BlockSpec(memory_space=pl.ANY),
             ],
-            out_specs=[pl.BlockSpec((steps, pair_rows, hidden_width), lambda i, at: (0, 0, 0))] * 3,
+            out_specs=[pl.BlockSpec((steps, pair_rows, hidden_width), lambda i, at: (0, 0, 0))] * 3
+            + [pl.BlockSpec(fresh_grads.shape[1:], lambda i, at: (0, 0, 0))] * 2
+            + [
+                pl.BlockSpec((depth, 2 * hidden_width), lambda i, at: (i, 0)),
+                pl.BlockSpec((hidden_width, depth), lambda i, at: (0, i)),
+            ],
             scratch_shapes=[
                 pltpu.VMEM((2 * steps * batch_rows, 2 * hidden_width), F32),
                 pltpu.VMEM((steps, pair_rows, 2 * hidden_width), F32),
@@ -193,18 +208,27 @@
             jax.ShapeDtypeStruct((steps, pair_rows, hidden_width), F32),
             jax.ShapeDtypeStruct((steps, pair_rows, hidden_width), F32),
             jax.ShapeDtypeStruct((steps, pair_rows, hidden_width), BF16),
+        ]
+        + [jax.ShapeDtypeStruct(fresh_grads.shape[1:], BF16)] * 2
+        + [
+            jax.ShapeDtypeStruct((width, 2 * hidden_width), BF16),
+            jax.ShapeDtypeStruct((hidden_width, width), BF16),
         ],
         compiler_params=pltpu.CompilerParams(vmem_limit_bytes=16 << 20),
         cost_estimate=pl.CostEstimate(flops=0, bytes_accessed=0, transcendentals=0),
         name="factors",
-    )(which, saved[0], saved[1], w_in, payload)
-
-    fresh_pair = jnp.concatenate(
-        [to_core(mine(fresh_grads).astype(BF16)), theirs(fresh_grads).astype(BF16)], axis=1
-    )
+    )(
+        which,
+        pltpu.with_memory_space_constraint(saved[0], pltpu.HBM),
+        saved[1],
+        pltpu.with_memory_space_constraint(w_in, pltpu.HBM),
+        pltpu.with_memory_space_constraint(w_down, pltpu.HBM),
+        fresh_grads,
+        payload,
+    )
+
+    fresh_pair = jnp.concatenate([to_core(fresh_send), fresh_keep], axis=1)
     at_end = section == jnp.where(core == 0, 0, sections - 1)
-    w_in_dir = indexed(w_in[:, 0])
-    w_down_dir = indexed(w_down[:, 0])
 
     blocks, gate_factor, activated = lax.optimization_barrier((blocks, gate_factor, activated))
 

time: 74.8 us -> 71.4 us (0.955)
  local copies, waits for them, and re-layouts: 5.79 us -> 2.09 us
  other arithmetic: 2.81 us -> 1.72 us
  Pallas kernels: 9.04 us -> 10.1 us
  waiting for transfers between devices: 21.1 us -> 21.9 us
    unnamed x14 -> x9, local copies, waits for them, and re-layouts: 5.59 us -> 1.88 us
    ppermute x8, waiting for transfers between devices: 12.6 us -> 9.39 us  [local(): lax.ppermute(payload, AXES, ring_pairs(sections, tensor_count, replicas, s))]
    ppermute x8, starting transfers between devices: 8.04 us -> 10.5 us  [local(): lax.ppermute(payload, AXES, ring_pairs(sections, tensor_count, replicas, s))]
    ppermute x12, waiting for transfers between devices: 7.51 us -> 9.84 us  [rotate(): lax.ppermute(x, 'tensor', [(i, (i + shift) % tensor_count) for i in range...]
    ppermute x12, starting transfers between devices: 16.6 us -> 14.9 us  [rotate(): lax.ppermute(x, 'tensor', [(i, (i + shift) % tensor_count) for i in range...]
    ppermute x13, waiting for transfers between devices: 0.97 us -> 2.66 us  [to_core(): return lax.ppermute(x, 'dp', [(i, i ^ offset) for i in range(replicas)])]
    pallas_call x1, Pallas kernels: 3.08 us -> 4.17 us  [local(): pl.pallas_call(functools.partial(factors_kernel, tensor_count), grid_spec...]
    convert_element_type x1 -> x0, other arithmetic: 1.08 us -> none  [local(): theirs(fresh_grads).astype(BF16)]
  transfers between devices with their start and end apart: 33 -> 33, of which waited for: 13 -> 18; matrix products, arithmetic and copies ran while one was open for 12% -> 10% of each run, Pallas kernels for 12% -> 14%
where the time goes in v3:
time: 71.4 us; the launch traced here: 70.9 us
  starting transfers between devices  28.5 us (40%)
  waiting for transfers between devices  21.9 us (31%)
  Pallas kernels  10.1 us (14%)
  matrix products  5.68 us (8%)
  local copies, waits for them, and re-layouts  2.09 us (3%)
  other arithmetic  1.72 us (2%)
  between operations  0.94 us (1%)
    ppermute x12, starting transfers between devices, rotate(): lax.ppermute(x, 'tensor', [(i, (i + shift) % tensor_count) for i in range...  14.9 us
    ppermute x8, starting transfers between devices, local(): lax.ppermute(payload, AXES, ring_pairs(sections, tensor_count, replicas, s))  10.5 us
    ppermute x12, waiting for transfers between devices, rotate(): lax.ppermute(x, 'tensor', [(i, (i + shift) % tensor_count) for i in range...  9.84 us
    ppermute x8, waiting for transfers between devices, local(): lax.ppermute(payload, AXES, ring_pairs(sections, tensor_count, replicas, s))  9.39 us
    pallas_call x1, Pallas kernels, weight_grads(): pl.pallas_call(functools.partial(weight_grads_kernel, steps, replicas, te...  5.95 us
    pallas_call x1, Pallas kernels, local(): pl.pallas_call(functools.partial(factors_kernel, tensor_count), grid_spec...  4.17 us
    dot_general x3, matrix products, local(): jnp.einsum('rc,dc->rd', pre_grad, w_in_dir, preferred_element_type=F32)  3.66 us
    ppermute x13, starting transfers between devices, to_core(): return lax.ppermute(x, 'dp', [(i, i ^ offset) for i in range(replicas)])  3.03 us
  transfers between devices with their start and end apart: 33, of which 18 were waited for; matrix products, arithmetic and copies ran while one was open for 10% of the time, Pallas kernels for 14%

profile of v3, /device:TPU:0, one launch (start us, length us, event | category | flops | bytes accessed | tf_op | source)
XLA Modules:
  0.0 70.9 jit_solution(13609122321643673491)
XLA Ops:
  0.6 0.5 collective-permute-start
  1.2 1.0 %select_bitcast_fusion = f32[8,3584]{1,0:T(8,128)S(1)} fusion(f32[2,1,8,3584]{3,2,1,0:T(8,128)} %param.11, pred[]{:T(512)S(6)} %eq.28), kind=kLoop, calls=%fused_computation.58 | loop fusion | flops 28672 | bytes 344065 | tf_op jit(solution)/shard_map/jit(_where)/select_n | solution.py:148
  2.5 3.9 %collective-permute-start.3 = (bf16[16,3584]{1,0:T(8,128)(2,1)S(1)}, bf16[16,3584]{1,0:T(8,128)(2,1)S(1)}, u32[]{:S(2)}, u32[]{:S(2)}) collective-permute-start(bf16[16,3584]{1,0:T(8,128)(2,1)S(1)} %fusion.11._), channel_id=1, source_target_pairs={{0,6},{2,0},{4,2},{6,4},{1,7},{3,1},{5,3},{7,5},{8,14},{10,8},{12,... | collective-permute-start | bytes 344072 | tf_op jit(solution)/shard_map/ppermute | solution.py:163
  6.4 0.5 collective-permute-start.2
  6.9 0.6 collective-permute-start.1
  7.6 1.0 %copy-done.1 = f32[2,2,8,3584]{3,2,1,0:T(8,128)S(1)} copy-done((f32[2,2,8,3584]{3,2,1,0:T(8,128)S(1)}, f32[2,2,8,3584]{3,2,1,0:T(8,128)}, u32[]{:S(2)}) %copy-start.1) | copy-done | bytes 458776
  8.6 4.2 %factors.1 = (f32[3,64,256]{2,1,0:T(8,128)S(1)}, f32[3,64,256]{2,1,0:T(8,128)S(1)}, bf16[3,64,256]{2,1,0:T(8,128)(2,1)S(1)}, bf16[2,8,3584]{2,1,0:T(8,128)(2,1)S...) custom-call(s32[2]{0:T(128)S(1)} %pad_add_fusion.at._, ...), custom_call_target="tpu_custom_call" | custom-call | tf_op jit(solution)/shard_map/factors/pallas_call | solution.py:183
  12.8 1.0 %collective-permute-done.2 = bf16[16,3584]{1,0:T(8,128)(2,1)S(1)} collective-permute-done((bf16[16,3584]{1,0:T(8,128)(2,1)S(1)}, bf16[16,3584]{1,0:T(8,128)(2,1)S(1)}, u32[]{:S(2)}, u32[]{:S(2)}) %collective-permute-start.2) | collective-permute-done | bytes 114720 | tf_op jit(solution)/shard_map/ppermute | solution.py:163
  13.9 0.7 fusion.21
  15.1 1.2 %convolution_convert_fusion.2 = bf16[64,3584]{1,0:T(8,128)(2,1)S(1)} fusion(bf16[3584,512]{1,0:T(8,128)(2,1)S(1)} %get-tuple-element.68, bf16[64,256]{1,0:T(8,128)(2,1)S(1)} %get-tuple-element.117, bf16[64,256]{1,0:T(8,128)(2,1)S(1)} %get-tuple-element.116), kind=kOutput, calls=%fused_computation.2 | convolution fusion | flops 235241472 | bytes 4194304 | tf_op jit(solution)/shard_map/rc,dc->rd/dot_general | solution.py:283
  16.4 1.5 %collective-permute-start.5 = (bf16[16,3584]{1,0:T(8,128)(2,1)S(1)}, bf16[16,3584]{1,0:T(8,128)(2,1)S(1)}, u32[]{:S(2)}, u32[]{:S(2)}) collective-permute-start(bf16[16,3584]{1,0:T(8,128)(2,1)S(1)} %get-tuple-element.101), channel_id=1, source_target_pairs={{0,2},{2,4},{4,6},{6,0},{1,3},{3,5},{5,7},{7,1},{8,10},{10,12},{12... | collective-permute-start | bytes 344072 | tf_op jit(solution)/shard_map/ppermute | solution.py:163
  17.9 1.5 %collective-permute-start.7 = (bf16[16,3584]{1,0:T(8,128)(2,1)S(1)}, bf16[16,3584]{1,0:T(8,128)(2,1)S(1)}, u32[]{:S(2)}, u32[]{:S(2)}) collective-permute-start(bf16[16,3584]{1,0:T(8,128)(2,1)S(1)} %get-tuple-element.102), channel_id=1, source_target_pairs={{0,6},{2,0},{4,2},{6,4},{1,7},{3,1},{5,3},{7,5},{8,14},{10,8},{12,... | collective-permute-start | bytes 344072 | tf_op jit(solution)/shard_map/ppermute | solution.py:163
  19.9 3.4 %collective-permute-done.5 = bf16[16,3584]{1,0:T(8,128)(2,1)S(1)} collective-permute-done((bf16[16,3584]{1,0:T(8,128)(2,1)S(1)}, bf16[16,3584]{1,0:T(8,128)(2,1)S(1)}, u32[]{:S(2)}, u32[]{:S(2)}) %collective-permute-start.5) | collective-permute-done | bytes 114720 | tf_op jit(solution)/shard_map/ppermute | solution.py:163
  23.3 0.6 collective-permute-done.7
  24.0 1.0 %collective-permute-done.6 = bf16[16,3584]{1,0:T(8,128)(2,1)S(1)} collective-permute-done((bf16[16,3584]{1,0:T(8,128)(2,1)S(1)}, bf16[16,3584]{1,0:T(8,128)(2,1)S(1)}, u32[]{:S(2)}, u32[]{:S(2)}) %collective-permute-start.6) | collective-permute-done | bytes 114720 | tf_op jit(solution)/shard_map/ppermute | solution.py:163
  25.0 1.0 %collective-permute-start.13 = (bf16[16,3584]{1,0:T(8,128)(2,1)S(1)}, bf16[16,3584]{1,0:T(8,128)(2,1)S(1)}, u32[]{:S(2)}, u32[]{:S(2)}) collective-permute-start(bf16[16,3584]{1,0:T(8,128)(2,1)S(1)} %get-tuple-element.84), channel_id=1, source_target_pairs={{0,3},{1,11},{2,5},{3,13},{4,7},{5,15},{6,1},{7,9},{8,2},{9,19},{1... | collective-permute-start | bytes 344072 | tf_op jit(solution)/shard_map/ppermute | solution.py:304
  26.0 0.7 collective-permute-start.12
  26.7 2.3 %collective-permute-start.11 = (bf16[16,3584]{1,0:T(8,128)(2,1)S(1)}, bf16[16,3584]{1,0:T(8,128)(2,1)S(1)}, u32[]{:S(2)}, u32[]{:S(2)}) collective-permute-start(bf16[16,3584]{1,0:T(8,128)(2,1)S(1)} %get-tuple-element.84), channel_id=1, source_target_pairs={{0,7},{1,15},{2,1},{3,9},{4,3},{5,11},{6,5},{7,13},{8,6},{9,23},{1... | collective-permute-start | bytes 344072 | tf_op jit(solution)/shard_map/ppermute | solution.py:304
  29.0 1.1 %collective-permute-start.10 = (bf16[16,3584]{1,0:T(8,128)(2,1)S(1)}, bf16[16,3584]{1,0:T(8,128)(2,1)S(1)}, u32[]{:S(2)}, u32[]{:S(2)}) collective-permute-start(bf16[16,3584]{1,0:T(8,128)(2,1)S(1)} %get-tuple-element.84), channel_id=1, source_target_pairs={{0,1},{1,9},{2,3},{3,11},{4,5},{5,13},{6,7},{7,15},{8,0},{9,17},{1... | collective-permute-start | bytes 344072 | tf_op jit(solution)/shard_map/ppermute | solution.py:304
  30.1 2.0 %collective-permute-done.13 = bf16[16,3584]{1,0:T(8,128)(2,1)S(1)} collective-permute-done((bf16[16,3584]{1,0:T(8,128)(2,1)S(1)}, bf16[16,3584]{1,0:T(8,128)(2,1)S(1)}, u32[]{:S(2)}, u32[]{:S(2)}) %collective-permute-start.13) | collective-permute-done | bytes 114720 | tf_op jit(solution)/shard_map/ppermute | solution.py:304
  32.2 0.8 %collective-permute-done.12 = bf16[16,3584]{1,0:T(8,128)(2,1)S(1)} collective-permute-done((bf16[16,3584]{1,0:T(8,128)(2,1)S(1)}, bf16[16,3584]{1,0:T(8,128)(2,1)S(1)}, u32[]{:S(2)}, u32[]{:S(2)}) %collective-permute-start.12) | collective-permute-done | bytes 114720 | tf_op jit(solution)/shard_map/ppermute | solution.py:304
  33.0 0.5 collective-permute-done.11
  33.5 1.5 %collective-permute-done.10 = bf16[16,3584]{1,0:T(8,128)(2,1)S(1)} collective-permute-done((bf16[16,3584]{1,0:T(8,128)(2,1)S(1)}, bf16[16,3584]{1,0:T(8,128)(2,1)S(1)}, u32[]{:S(2)}, u32[]{:S(2)}) %collective-permute-start.10) | collective-permute-done | bytes 114720 | tf_op jit(solution)/shard_map/ppermute | solution.py:304
  35.1 0.7 fusion.19
  35.8 1.2 %convolution_convert_fusion.1 = bf16[64,3584]{1,0:T(8,128)(2,1)S(1)} fusion(bf16[3584,512]{1,0:T(8,128)(2,1)S(1)} %get-tuple-element.68, bf16[64,256]{1,0:T(8,128)(2,1)S(1)} %get-tuple-element.115, bf16[64,256]{1,0:T(8,128)(2,1)S(1)} %get-tuple-element.114), kind=kOutput, calls=%fused_computation.1 | convolution fusion | flops 235241472 | bytes 4194304 | tf_op jit(solution)/shard_map/rc,dc->rd/dot_general | solution.py:283
  37.0 0.7 collective-permute-start.14
  37.7 2.3 %collective-permute-start.16 = (bf16[16,3584]{1,0:T(8,128)(2,1)S(1)}, bf16[16,3584]{1,0:T(8,128)(2,1)S(1)}, u32[]{:S(2)}, u32[]{:S(2)}) collective-permute-start(bf16[16,3584]{1,0:T(8,128)(2,1)S(1)} %get-tuple-element.95), channel_id=1, source_target_pairs={{0,6},{2,0},{4,2},{6,4},{1,7},{3,1},{5,3},{7,5},{8,14},{10,8},{12,... | collective-permute-start | bytes 344072 | tf_op jit(solution)/shard_map/ppermute | solution.py:163
  40.0 0.9 %collective-permute-start.15 = (bf16[16,3584]{1,0:T(8,128)(2,1)S(1)}, bf16[16,3584]{1,0:T(8,128)(2,1)S(1)}, u32[]{:S(2)}, u32[]{:S(2)}) collective-permute-start(bf16[16,3584]{1,0:T(8,128)(2,1)S(1)} %get-tuple-element.96), channel_id=1, source_target_pairs={{0,4},{2,6},{4,0},{6,2},{1,5},{3,7},{5,1},{7,3},{8,12},{10,14},{12... | collective-permute-start | bytes 344072 | tf_op jit(solution)/shard_map/ppermute | solution.py:163
  41.0 2.5 %collective-permute-done.14 = bf16[16,3584]{1,0:T(8,128)(2,1)S(1)} collective-permute-done((bf16[16,3584]{1,0:T(8,128)(2,1)S(1)}, bf16[16,3584]{1,0:T(8,128)(2,1)S(1)}, u32[]{:S(2)}, u32[]{:S(2)}) %collective-permute-start.14) | collective-permute-done | bytes 114720 | tf_op jit(solution)/shard_map/ppermute | solution.py:163
  43.4 1.2 %collective-permute-done.16 = bf16[16,3584]{1,0:T(8,128)(2,1)S(1)} collective-permute-done((bf16[16,3584]{1,0:T(8,128)(2,1)S(1)}, bf16[16,3584]{1,0:T(8,128)(2,1)S(1)}, u32[]{:S(2)}, u32[]{:S(2)}) %collective-permute-start.16) | collective-permute-done | bytes 114720 | tf_op jit(solution)/shard_map/ppermute | solution.py:163
  45.0 0.9 %collective-permute-start.20 = (bf16[16,3584]{1,0:T(8,128)(2,1)S(1)}, bf16[16,3584]{1,0:T(8,128)(2,1)S(1)}, u32[]{:S(2)}, u32[]{:S(2)}) collective-permute-start(bf16[16,3584]{1,0:T(8,128)(2,1)S(1)} %get-tuple-element.82), channel_id=1, source_target_pairs={{0,5},{1,13},{2,7},{3,15},{4,1},{5,9},{6,3},{7,11},{8,4},{9,21},{1... | collective-permute-start | bytes 344072 | tf_op jit(solution)/shard_map/ppermute | solution.py:304
  45.9 3.6 %collective-permute-start.19 = (bf16[16,3584]{1,0:T(8,128)(2,1)S(1)}, bf16[16,3584]{1,0:T(8,128)(2,1)S(1)}, u32[]{:S(2)}, u32[]{:S(2)}) collective-permute-start(bf16[16,3584]{1,0:T(8,128)(2,1)S(1)} %get-tuple-element.82), channel_id=1, source_target_pairs={{0,7},{1,15},{2,1},{3,9},{4,3},{5,11},{6,5},{7,13},{8,6},{9,23},{1... | collective-permute-start | bytes 344072 | tf_op jit(solution)/shard_map/ppermute | solution.py:304
  49.5 0.9 %collective-permute-start.18 = (bf16[16,3584]{1,0:T(8,128)(2,1)S(1)}, bf16[16,3584]{1,0:T(8,128)(2,1)S(1)}, u32[]{:S(2)}, u32[]{:S(2)}) collective-permute-start(bf16[16,3584]{1,0:T(8,128)(2,1)S(1)} %get-tuple-element.82), channel_id=1, source_target_pairs={{0,1},{1,9},{2,3},{3,11},{4,5},{5,13},{6,7},{7,15},{8,0},{9,17},{1... | collective-permute-start | bytes 344072 | tf_op jit(solution)/shard_map/ppermute | solution.py:304
  50.4 1.3 %collective-permute-done.21 = bf16[16,3584]{1,0:T(8,128)(2,1)S(1)} collective-permute-done((bf16[16,3584]{1,0:T(8,128)(2,1)S(1)}, bf16[16,3584]{1,0:T(8,128)(2,1)S(1)}, u32[]{:S(2)}, u32[]{:S(2)}) %collective-permute-start.21) | collective-permute-done | bytes 114720 | tf_op jit(solution)/shard_map/ppermute | solution.py:304
  51.7 1.3 %collective-permute-done.20 = bf16[16,3584]{1,0:T(8,128)(2,1)S(1)} collective-permute-done((bf16[16,3584]{1,0:T(8,128)(2,1)S(1)}, bf16[16,3584]{1,0:T(8,128)(2,1)S(1)}, u32[]{:S(2)}, u32[]{:S(2)}) %collective-permute-start.20) | collective-permute-done | bytes 114720 | tf_op jit(solution)/shard_map/ppermute | solution.py:304
  53.5 0.5 collective-permute-done.19
  54.0 1.4 %collective-permute-done.18 = bf16[16,3584]{1,0:T(8,128)(2,1)S(1)} collective-permute-done((bf16[16,3584]{1,0:T(8,128)(2,1)S(1)}, bf16[16,3584]{1,0:T(8,128)(2,1)S(1)}, u32[]{:S(2)}, u32[]{:S(2)}) %collective-permute-start.18) | collective-permute-done | bytes 114720 | tf_op jit(solution)/shard_map/ppermute | solution.py:304
  55.5 0.7 fusion.17
  56.2 1.2 %convolution_convert_fusion = bf16[64,3584]{1,0:T(8,128)(2,1)S(1)} fusion(bf16[3584,512]{1,0:T(8,128)(2,1)S(1)} %get-tuple-element.68, bf16[64,256]{1,0:T(8,128)(2,1)S(1)} %get-tuple-element.113, bf16[64,256]{1,0:T(8,128)(2,1)S(1)} %get-tuple-element.112), kind=kOutput, calls=%fused_computation | convolution fusion | flops 235241472 | bytes 4194304 | tf_op jit(solution)/shard_map/rc,dc->rd/dot_general | solution.py:283
  57.6 0.5 collective-permute-start.30
  58.1 1.3 %collective-permute-start.24 = (bf16[16,3584]{1,0:T(8,128)(2,1)S(1)}, bf16[16,3584]{1,0:T(8,128)(2,1)S(1)}, u32[]{:S(2)}, u32[]{:S(2)}) collective-permute-start(bf16[16,3584]{1,0:T(8,128)(2,1)S(1)} %get-tuple-element.87), channel_id=1, source_target_pairs={{0,6},{2,0},{4,2},{6,4},{1,7},{3,1},{5,3},{7,5},{8,14},{10,8},{12,... | collective-permute-start | bytes 344072 | tf_op jit(solution)/shard_map/ppermute | solution.py:163
  59.4 0.5 collective-permute-start.23
  60.0 0.7 %collective-permute-start.22 = (bf16[16,3584]{1,0:T(8,128)(2,1)S(1)}, bf16[16,3584]{1,0:T(8,128)(2,1)S(1)}, u32[]{:S(2)}, u32[]{:S(2)}) collective-permute-start(bf16[16,3584]{1,0:T(8,128)(2,1)S(1)} %get-tuple-element.89), channel_id=1, source_target_pairs={{0,2},{2,4},{4,6},{6,0},{1,3},{3,5},{5,7},{7,1},{8,10},{10,12},{12... | collective-permute-start | bytes 344072 | tf_op jit(solution)/shard_map/ppermute | solution.py:163
  60.8 0.6 collective-permute-start.17
  61.3 1.2 %collective-permute-done.31.refs_15_ = bf16[64,3584]{1,0:T(8,128)(2,1)S(1)} collective-permute-done((bf16[64,3584]{1,0:T(8,128)(2,1)S(1)}, bf16[64,3584]{1,0:T(8,128)(2,1)S(1)}, u32[]{:S(2)}, u32[]{:S(2)}) %collective-permute-start.31) | collective-permute-done | bytes 458784 | tf_op jit(solution)/shard_map/ppermute | solution.py:160
  62.5 5.9 %weight_grads.1 = (f32[2,1,1792,512]{3,2,1,0:T(8,128)}, f32[2,1,256,1792]{3,2,1,0:T(8,128)}) custom-call(s32[2]{0:T(128)S(1)} %pad_add_fusion.at._, bf16[2,3,1,32,3584]{4,3,2,1,0:T(8,128)(2,1)S(1)} %copy-done, bf16[2,3,1,32,3584]{4,3,2,1,0:T(8,128)(2,1)S(1)} %collective-permute-done.4.peer_ref.refs_1_, bf16[64,512]{1,0:T(8,128)(2,1)S(1)} %pad_maximum_fusion.4.refs_2_, ...), custom_call_target="tpu_custom_call" | custom-call | tf_op jit(solution)/shard_map/weight_grads/pallas_call | solution.py:239
  68.9 1.2 %collective-permute-done.32 = f32[8,3584]{1,0:T(8,128)S(1)} collective-permute-done((f32[8,3584]{1,0:T(8,128)S(1)}, f32[8,3584]{1,0:T(8,128)S(1)}, u32[]{:S(2)}, u32[]{:S(2)}) %collective-permute-start.32) | collective-permute-done | bytes 114720 | tf_op jit(solution)/shard_map/ppermute | solution.py:160
  70.1 0.8 %copy-done.3 = f32[2,3,1,8,3584]{4,3,1,0,2:T(8,128)} copy-done((f32[2,3,1,8,3584]{4,3,1,0,2:T(8,128)}, f32[2,3,1,8,3584]{4,3,1,0,2:T(8,128)S(1)}, u32[]{:S(2)}) %copy-start.3) | copy-done | bytes 688152
  (64 shorter events, 3.4 us)
Async XLA Ops:
  0.6 1.8 %collective-permute-start = (f32[2,1,8,3584]{3,2,1,0:T(8,128)}, f32[2,1,8,3584]{3,2,1,0:T(8,128)S(1)}, u32[]{:S(2)}, u32[]{:S(2)}) collective-permute-start(f32[2,1,8,3584]{3,2,1,0:T(8,128)} %param.11), channel_id=1, source_target_pairs={{0,1},{1,0},{2,3},{3,2},{4,5},{5,4},{6,7},{7,6},{8,9},{9,8},{10,11... | collective-permute-start | bytes 688136 | tf_op jit(solution)/shard_map/ppermute | solution.py:160
  1.1 6.4 %collective-permute-start.4 = (bf16[2,3,1,32,3584]{4,3,2,1,0:T(8,128)(2,1)}, bf16[2,3,1,32,3584]{4,3,2,1,0:T(8,128)(2,1)S(1)}, u32[]{:S(2)}, u32[]{:S(2)}) collective-permute-start(bf16[2,3,1,32,3584]{4,3,2,1,0:T(8,128)(2,1)} %refs_0_.1), channel_id=1, source_target_pairs={{0,1},{1,0},{2,3},{3,2},{4,5},{5,4},{6,7},{7,6},{8,9},{9,8},{10,11... | collective-permute-start | bytes 4128776 | tf_op jit(solution)/shard_map/ppermute | solution.py:160
  2.5 10.2 %collective-permute-start.3 = (bf16[16,3584]{1,0:T(8,128)(2,1)S(1)}, bf16[16,3584]{1,0:T(8,128)(2,1)S(1)}, u32[]{:S(2)}, u32[]{:S(2)}) collective-permute-start(bf16[16,3584]{1,0:T(8,128)(2,1)S(1)} %fusion.11._), channel_id=1, source_target_pairs={{0,6},{2,0},{4,2},{6,4},{1,7},{3,1},{5,3},{7,5},{8,14},{10,8},{12,... | collective-permute-start | bytes 344072 | tf_op jit(solution)/shard_map/ppermute | solution.py:163
  6.4 7.4 %collective-permute-start.2 = (bf16[16,3584]{1,0:T(8,128)(2,1)S(1)}, bf16[16,3584]{1,0:T(8,128)(2,1)S(1)}, u32[]{:S(2)}, u32[]{:S(2)}) collective-permute-start(bf16[16,3584]{1,0:T(8,128)(2,1)S(1)} %fusion.11._), channel_id=1, source_target_pairs={{0,4},{2,6},{4,0},{6,2},{1,5},{3,7},{5,1},{7,3},{8,12},{10,14},{12... | collective-permute-start | bytes 344072 | tf_op jit(solution)/shard_map/ppermute | solution.py:163
  6.9 6.9 %collective-permute-start.1 = (bf16[16,3584]{1,0:T(8,128)(2,1)S(1)}, bf16[16,3584]{1,0:T(8,128)(2,1)S(1)}, u32[]{:S(2)}, u32[]{:S(2)}) collective-permute-start(bf16[16,3584]{1,0:T(8,128)(2,1)S(1)} %fusion.11._), channel_id=1, source_target_pairs={{0,2},{2,4},{4,6},{6,0},{1,3},{3,5},{5,7},{7,1},{8,10},{10,12},{12... | collective-permute-start | bytes 344072 | tf_op jit(solution)/shard_map/ppermute | solution.py:163
  7.6 1.0 %copy-start.1 = (f32[2,2,8,3584]{3,2,1,0:T(8,128)S(1)}, f32[2,2,8,3584]{3,2,1,0:T(8,128)}, u32[]{:S(2)}) copy-start(f32[2,2,8,3584]{3,2,1,0:T(8,128)} %fresh_ref.1) | copy-start | bytes 1376260
  14.5 43.0 %collective-permute-start.25 = (bf16[64,512]{1,0:T(8,128)(2,1)S(1)}, bf16[64,512]{1,0:T(8,128)(2,1)S(1)}, u32[]{:S(2)}, u32[]{:S(2)}) collective-permute-start(bf16[64,512]{1,0:T(8,128)(2,1)S(1)} %pad_maximum_fusion.4.refs_2_), channel_id=1, source_target_pairs={{0,1},{1,0},{2,3},{3,2},{4,5},{5,4},{6,7},{7,6},{8,9},{9,8},{10,11... | collective-permute-start | bytes 196616 | tf_op jit(solution)/shard_map/ppermute | solution.py:160
  14.6 5.2 %collective-permute-start.9 = (bf16[2,8,3584]{2,1,0:T(8,128)(2,1)S(1)}, bf16[2,8,3584]{2,1,0:T(8,128)(2,1)S(1)}, u32[]{:S(2)}, u32[]{:S(2)}) collective-permute-start(bf16[2,8,3584]{2,1,0:T(8,128)(2,1)S(1)} %get-tuple-element.69), channel_id=1, source_target_pairs={{0,1},{1,0},{2,3},{3,2},{4,5},{5,4},{6,7},{7,6},{8,9},{9,8},{10,11... | collective-permute-start | bytes 344072 | tf_op jit(solution)/shard_map/ppermute | solution.py:160
  16.4 7.0 %collective-permute-start.5 = (bf16[16,3584]{1,0:T(8,128)(2,1)S(1)}, bf16[16,3584]{1,0:T(8,128)(2,1)S(1)}, u32[]{:S(2)}, u32[]{:S(2)}) collective-permute-start(bf16[16,3584]{1,0:T(8,128)(2,1)S(1)} %get-tuple-element.101), channel_id=1, source_target_pairs={{0,2},{2,4},{4,6},{6,0},{1,3},{3,5},{5,7},{7,1},{8,10},{10,12},{12... | collective-permute-start | bytes 344072 | tf_op jit(solution)/shard_map/ppermute | solution.py:163
  17.9 6.1 %collective-permute-start.7 = (bf16[16,3584]{1,0:T(8,128)(2,1)S(1)}, bf16[16,3584]{1,0:T(8,128)(2,1)S(1)}, u32[]{:S(2)}, u32[]{:S(2)}) collective-permute-start(bf16[16,3584]{1,0:T(8,128)(2,1)S(1)} %get-tuple-element.102), channel_id=1, source_target_pairs={{0,6},{2,0},{4,2},{6,4},{1,7},{3,1},{5,3},{7,5},{8,14},{10,8},{12,... | collective-permute-start | bytes 344072 | tf_op jit(solution)/shard_map/ppermute | solution.py:163
  19.4 5.6 %collective-permute-start.6 = (bf16[16,3584]{1,0:T(8,128)(2,1)S(1)}, bf16[16,3584]{1,0:T(8,128)(2,1)S(1)}, u32[]{:S(2)}, u32[]{:S(2)}) collective-permute-start(bf16[16,3584]{1,0:T(8,128)(2,1)S(1)} %get-tuple-element.103), channel_id=1, source_target_pairs={{0,4},{2,6},{4,0},{6,2},{1,5},{3,7},{5,1},{7,3},{8,12},{10,14},{12... | collective-permute-start | bytes 344072 | tf_op jit(solution)/shard_map/ppermute | solution.py:163
  25.0 7.2 %collective-permute-start.13 = (bf16[16,3584]{1,0:T(8,128)(2,1)S(1)}, bf16[16,3584]{1,0:T(8,128)(2,1)S(1)}, u32[]{:S(2)}, u32[]{:S(2)}) collective-permute-start(bf16[16,3584]{1,0:T(8,128)(2,1)S(1)} %get-tuple-element.84), channel_id=1, source_target_pairs={{0,3},{1,11},{2,5},{3,13},{4,7},{5,15},{6,1},{7,9},{8,2},{9,19},{1... | collective-permute-start | bytes 344072 | tf_op jit(solution)/shard_map/ppermute | solution.py:304
  26.0 7.0 %collective-permute-start.12 = (bf16[16,3584]{1,0:T(8,128)(2,1)S(1)}, bf16[16,3584]{1,0:T(8,128)(2,1)S(1)}, u32[]{:S(2)}, u32[]{:S(2)}) collective-permute-start(bf16[16,3584]{1,0:T(8,128)(2,1)S(1)} %get-tuple-element.84), channel_id=1, source_target_pairs={{0,5},{1,13},{2,7},{3,15},{4,1},{5,9},{6,3},{7,11},{8,4},{9,21},{1... | collective-permute-start | bytes 344072 | tf_op jit(solution)/shard_map/ppermute | solution.py:304
  26.7 6.9 %collective-permute-start.11 = (bf16[16,3584]{1,0:T(8,128)(2,1)S(1)}, bf16[16,3584]{1,0:T(8,128)(2,1)S(1)}, u32[]{:S(2)}, u32[]{:S(2)}) collective-permute-start(bf16[16,3584]{1,0:T(8,128)(2,1)S(1)} %get-tuple-element.84), channel_id=1, source_target_pairs={{0,7},{1,15},{2,1},{3,9},{4,3},{5,11},{6,5},{7,13},{8,6},{9,23},{1... | collective-permute-start | bytes 344072 | tf_op jit(solution)/shard_map/ppermute | solution.py:304
  29.0 6.0 %collective-permute-start.10 = (bf16[16,3584]{1,0:T(8,128)(2,1)S(1)}, bf16[16,3584]{1,0:T(8,128)(2,1)S(1)}, u32[]{:S(2)}, u32[]{:S(2)}) collective-permute-start(bf16[16,3584]{1,0:T(8,128)(2,1)S(1)} %get-tuple-element.84), channel_id=1, source_target_pairs={{0,1},{1,9},{2,3},{3,11},{4,5},{5,13},{6,7},{7,15},{8,0},{9,17},{1... | collective-permute-start | bytes 344072 | tf_op jit(solution)/shard_map/ppermute | solution.py:304
  32.2 8.7 %collective-permute-start.8 = (f32[8,3584]{1,0:T(8,128)S(1)}, f32[8,3584]{1,0:T(8,128)S(1)}, u32[]{:S(2)}, u32[]{:S(2)}) collective-permute-start(f32[8,3584]{1,0:T(8,128)S(1)} %slice.155), channel_id=1, source_target_pairs={{0,1},{1,0},{2,3},{3,2},{4,5},{5,4},{6,7},{7,6},{8,9},{9,8},{10,11... | collective-permute-start | bytes 344072 | tf_op jit(solution)/shard_map/ppermute | solution.py:160
  35.1 5.8 %copy-start.2 = (f32[2,1,8,3584]{3,2,1,0:T(8,128)S(1)}, f32[2,1,8,3584]{3,2,1,0:T(8,128)}, u32[]{:S(2)}) copy-start(f32[2,1,8,3584]{3,2,1,0:T(8,128)} %param.11) | copy-start | bytes 688132
  37.0 6.4 %collective-permute-start.14 = (bf16[16,3584]{1,0:T(8,128)(2,1)S(1)}, bf16[16,3584]{1,0:T(8,128)(2,1)S(1)}, u32[]{:S(2)}, u32[]{:S(2)}) collective-permute-start(bf16[16,3584]{1,0:T(8,128)(2,1)S(1)} %get-tuple-element.94), channel_id=1, source_target_pairs={{0,2},{2,4},{4,6},{6,0},{1,3},{3,5},{5,7},{7,1},{8,10},{10,12},{12... | collective-permute-start | bytes 344072 | tf_op jit(solution)/shard_map/ppermute | solution.py:163
  37.7 7.0 %collective-permute-start.16 = (bf16[16,3584]{1,0:T(8,128)(2,1)S(1)}, bf16[16,3584]{1,0:T(8,128)(2,1)S(1)}, u32[]{:S(2)}, u32[]{:S(2)}) collective-permute-start(bf16[16,3584]{1,0:T(8,128)(2,1)S(1)} %get-tuple-element.95), channel_id=1, source_target_pairs={{0,6},{2,0},{4,2},{6,4},{1,7},{3,1},{5,3},{7,5},{8,14},{10,8},{12,... | collective-permute-start | bytes 344072 | tf_op jit(solution)/shard_map/ppermute | solution.py:163
  40.0 4.8 %collective-permute-start.15 = (bf16[16,3584]{1,0:T(8,128)(2,1)S(1)}, bf16[16,3584]{1,0:T(8,128)(2,1)S(1)}, u32[]{:S(2)}, u32[]{:S(2)}) collective-permute-start(bf16[16,3584]{1,0:T(8,128)(2,1)S(1)} %get-tuple-element.96), channel_id=1, source_target_pairs={{0,4},{2,6},{4,0},{6,2},{1,5},{3,7},{5,1},{7,3},{8,12},{10,14},{12... | collective-permute-start | bytes 344072 | tf_op jit(solution)/shard_map/ppermute | solution.py:163
  44.9 6.8 %collective-permute-start.21 = (bf16[16,3584]{1,0:T(8,128)(2,1)S(1)}, bf16[16,3584]{1,0:T(8,128)(2,1)S(1)}, u32[]{:S(2)}, u32[]{:S(2)}) collective-permute-start(bf16[16,3584]{1,0:T(8,128)(2,1)S(1)} %get-tuple-element.82), channel_id=1, source_target_pairs={{0,3},{1,11},{2,5},{3,13},{4,7},{5,15},{6,1},{7,9},{8,2},{9,19},{1... | collective-permute-start | bytes 344072 | tf_op jit(solution)/shard_map/ppermute | solution.py:304
  45.0 8.0 %collective-permute-start.20 = (bf16[16,3584]{1,0:T(8,128)(2,1)S(1)}, bf16[16,3584]{1,0:T(8,128)(2,1)S(1)}, u32[]{:S(2)}, u32[]{:S(2)}) collective-permute-start(bf16[16,3584]{1,0:T(8,128)(2,1)S(1)} %get-tuple-element.82), channel_id=1, source_target_pairs={{0,5},{1,13},{2,7},{3,15},{4,1},{5,9},{6,3},{7,11},{8,4},{9,21},{1... | collective-permute-start | bytes 344072 | tf_op jit(solution)/shard_map/ppermute | solution.py:304
  45.9 8.1 %collective-permute-start.19 = (bf16[16,3584]{1,0:T(8,128)(2,1)S(1)}, bf16[16,3584]{1,0:T(8,128)(2,1)S(1)}, u32[]{:S(2)}, u32[]{:S(2)}) collective-permute-start(bf16[16,3584]{1,0:T(8,128)(2,1)S(1)} %get-tuple-element.82), channel_id=1, source_target_pairs={{0,7},{1,15},{2,1},{3,9},{4,3},{5,11},{6,5},{7,13},{8,6},{9,23},{1... | collective-permute-start | bytes 344072 | tf_op jit(solution)/shard_map/ppermute | solution.py:304
  49.5 5.9 %collective-permute-start.18 = (bf16[16,3584]{1,0:T(8,128)(2,1)S(1)}, bf16[16,3584]{1,0:T(8,128)(2,1)S(1)}, u32[]{:S(2)}, u32[]{:S(2)}) collective-permute-start(bf16[16,3584]{1,0:T(8,128)(2,1)S(1)} %get-tuple-element.82), channel_id=1, source_target_pairs={{0,1},{1,9},{2,3},{3,11},{4,5},{5,13},{6,7},{7,15},{8,0},{9,17},{1... | collective-permute-start | bytes 344072 | tf_op jit(solution)/shard_map/ppermute | solution.py:304
  51.7 6.5 %collective-permute-start.28 = (bf16[3,64,256]{2,1,0:T(8,128)(2,1)S(1)}, bf16[3,64,256]{2,1,0:T(8,128)(2,1)S(1)}, u32[]{:S(2)}, u32[]{:S(2)}) collective-permute-start(bf16[3,64,256]{2,1,0:T(8,128)(2,1)S(1)} %get-tuple-element.71.refs_8_), channel_id=1, source_target_pairs={{0,1},{1,0},{2,3},{3,2},{4,5},{5,4},{6,7},{7,6},{8,9},{9,8},{10,11... | collective-permute-start | bytes 294920 | tf_op jit(solution)/shard_map/ppermute | solution.py:160
  53.0 7.0 %collective-permute-start.29 = (bf16[64,3584]{1,0:T(8,128)(2,1)S(1)}, bf16[64,3584]{1,0:T(8,128)(2,1)S(1)}, u32[]{:S(2)}, u32[]{:S(2)}) collective-permute-start(bf16[64,3584]{1,0:T(8,128)(2,1)S(1)} %pad_maximum_fusion.refs_10_), channel_id=1, source_target_pairs={{0,1},{1,0},{2,3},{3,2},{4,5},{5,4},{6,7},{7,6},{8,9},{9,8},{10,11... | collective-permute-start | bytes 1376264 | tf_op jit(solution)/shard_map/ppermute | solution.py:160
  54.0 5.4 %collective-permute-start.26 = (bf16[64,512]{1,0:T(8,128)(2,1)S(1)}, bf16[64,512]{1,0:T(8,128)(2,1)S(1)}, u32[]{:S(2)}, u32[]{:S(2)}) collective-permute-start(bf16[64,512]{1,0:T(8,128)(2,1)S(1)} %pad_maximum_fusion.5.refs_3_), channel_id=1, source_target_pairs={{0,1},{1,0},{2,3},{3,2},{4,5},{5,4},{6,7},{7,6},{8,9},{9,8},{10,11... | collective-permute-start | bytes 196616 | tf_op jit(solution)/shard_map/ppermute | solution.py:160
  56.2 6.4 %copy-start = (bf16[2,3,1,32,3584]{4,3,2,1,0:T(8,128)(2,1)S(1)}, bf16[2,3,1,32,3584]{4,3,2,1,0:T(8,128)(2,1)}, u32[]{:S(2)}) copy-start(bf16[2,3,1,32,3584]{4,3,2,1,0:T(8,128)(2,1)} %refs_0_.1) | copy-start | bytes 4128772
  57.4 3.3 %collective-permute-start.27 = (bf16[64,512]{1,0:T(8,128)(2,1)S(1)}, bf16[64,512]{1,0:T(8,128)(2,1)S(1)}, u32[]{:S(2)}, u32[]{:S(2)}) collective-permute-start(bf16[64,512]{1,0:T(8,128)(2,1)S(1)} %pad_maximum_fusion.6.refs_4_), channel_id=1, source_target_pairs={{0,1},{1,0},{2,3},{3,2},{4,5},{5,4},{6,7},{7,6},{8,9},{9,8},{10,11... | collective-permute-start | bytes 196616 | tf_op jit(solution)/shard_map/ppermute | solution.py:160
  57.6 3.2 %collective-permute-start.30 = (bf16[64,3584]{1,0:T(8,128)(2,1)S(1)}, bf16[64,3584]{1,0:T(8,128)(2,1)S(1)}, u32[]{:S(2)}, u32[]{:S(2)}) collective-permute-start(bf16[64,3584]{1,0:T(8,128)(2,1)S(1)} %pad_maximum_fusion.1.refs_11_), channel_id=1, source_target_pairs={{0,1},{1,0},{2,3},{3,2},{4,5},{5,4},{6,7},{7,6},{8,9},{9,8},{10,11... | collective-permute-start | bytes 1376264 | tf_op jit(solution)/shard_map/ppermute | solution.py:160
  58.1 10.4 %collective-permute-start.24 = (bf16[16,3584]{1,0:T(8,128)(2,1)S(1)}, bf16[16,3584]{1,0:T(8,128)(2,1)S(1)}, u32[]{:S(2)}, u32[]{:S(2)}) collective-permute-start(bf16[16,3584]{1,0:T(8,128)(2,1)S(1)} %get-tuple-element.87), channel_id=1, source_target_pairs={{0,6},{2,0},{4,2},{6,4},{1,7},{3,1},{5,3},{7,5},{8,14},{10,8},{12,... | collective-permute-start | bytes 344072 | tf_op jit(solution)/shard_map/ppermute | solution.py:163
  59.4 9.1 %collective-permute-start.23 = (bf16[16,3584]{1,0:T(8,128)(2,1)S(1)}, bf16[16,3584]{1,0:T(8,128)(2,1)S(1)}, u32[]{:S(2)}, u32[]{:S(2)}) collective-permute-start(bf16[16,3584]{1,0:T(8,128)(2,1)S(1)} %get-tuple-element.88), channel_id=1, source_target_pairs={{0,4},{2,6},{4,0},{6,2},{1,5},{3,7},{5,1},{7,3},{8,12},{10,14},{12... | collective-permute-start | bytes 344072 | tf_op jit(solution)/shard_map/ppermute | solution.py:163
  60.0 8.5 %collective-permute-start.22 = (bf16[16,3584]{1,0:T(8,128)(2,1)S(1)}, bf16[16,3584]{1,0:T(8,128)(2,1)S(1)}, u32[]{:S(2)}, u32[]{:S(2)}) collective-permute-start(bf16[16,3584]{1,0:T(8,128)(2,1)S(1)} %get-tuple-element.89), channel_id=1, source_target_pairs={{0,2},{2,4},{4,6},{6,0},{1,3},{3,5},{5,7},{7,1},{8,10},{10,12},{12... | collective-permute-start | bytes 344072 | tf_op jit(solution)/shard_map/ppermute | solution.py:163
  60.7 1.8 %collective-permute-start.31 = (bf16[64,3584]{1,0:T(8,128)(2,1)S(1)}, bf16[64,3584]{1,0:T(8,128)(2,1)S(1)}, u32[]{:S(2)}, u32[]{:S(2)}) collective-permute-start(bf16[64,3584]{1,0:T(8,128)(2,1)S(1)} %pad_maximum_fusion.2.refs_12_), channel_id=1, source_target_pairs={{0,1},{1,0},{2,3},{3,2},{4,5},{5,4},{6,7},{7,6},{8,9},{9,8},{10,11... | collective-permute-start | bytes 1376264 | tf_op jit(solution)/shard_map/ppermute | solution.py:160
  60.8 8.1 %collective-permute-start.17 = (f32[8,3584]{1,0:T(8,128)S(1)}, f32[8,3584]{1,0:T(8,128)S(1)}, u32[]{:S(2)}, u32[]{:S(2)}) collective-permute-start(f32[8,3584]{1,0:T(8,128)S(1)} %get-tuple-element.111), channel_id=1, source_target_pairs={{0,1},{1,0},{2,3},{3,2},{4,5},{5,4},{6,7},{7,6},{8,9},{9,8},{10,11... | collective-permute-start | bytes 344072 | tf_op jit(solution)/shard_map/ppermute | solution.py:160
  68.6 1.4 %collective-permute-start.32 = (f32[8,3584]{1,0:T(8,128)S(1)}, f32[8,3584]{1,0:T(8,128)S(1)}, u32[]{:S(2)}, u32[]{:S(2)}) collective-permute-start(f32[8,3584]{1,0:T(8,128)S(1)} %get-tuple-element.109), channel_id=1, source_target_pairs={{0,1},{1,0},{2,3},{3,2},{4,5},{5,4},{6,7},{7,6},{8,9},{9,8},{10,11... | collective-permute-start | bytes 344072 | tf_op jit(solution)/shard_map/ppermute | solution.py:160
  70.0 0.8 %copy-start.3 = (f32[2,3,1,8,3584]{4,3,1,0,2:T(8,128)}, f32[2,3,1,8,3584]{4,3,1,0,2:T(8,128)S(1)}, u32[]{:S(2)}) copy-start(f32[2,3,1,8,3584]{4,3,1,0,2:T(8,128)S(1)} %fusion.1) | copy-start | bytes 2064388

commit v4 on v3

--- a/solution.py
+++ b/solution.py
@@ -49,8 +49,8 @@
     )
     weights = w_ref[0, 0]
     product = jnp.dot(rows, weights, preferred_element_type=F32)
-    w_copy[...] = weights
-    down_copy[...] = down_ref[0, 0]
+    w_copy[...] = weights.T
+    down_copy[...] = down_ref[0, 0].T
 
     @pl.when(step == 0)
     def _():
@@ -196,8 +196,8 @@
             out_specs=[pl.BlockSpec((steps, pair_rows, hidden_width), lambda i, at: (0, 0, 0))] * 3
             + [pl.BlockSpec(fresh_grads.shape[1:], lambda i, at: (0, 0, 0))] * 2
             + [
-                pl.BlockSpec((depth, 2 * hidden_width), lambda i, at: (i, 0)),
-                pl.BlockSpec((hidden_width, depth), lambda i, at: (0, i)),
+                pl.BlockSpec((2 * hidden_width, depth), lambda i, at: (0, i)),
+                pl.BlockSpec((depth, hidden_width), lambda i, at: (i, 0)),
             ],
             scratch_shapes=[
                 pltpu.VMEM((2 * steps * batch_rows, 2 * hidden_width), F32),
@@ -211,8 +211,8 @@
         ]
         + [jax.ShapeDtypeStruct(fresh_grads.shape[1:], BF16)] * 2
         + [
-            jax.ShapeDtypeStruct((width, 2 * hidden_width), BF16),
-            jax.ShapeDtypeStruct((hidden_width, width), BF16),
+            jax.ShapeDtypeStruct((2 * hidden_width, width), BF16),
+            jax.ShapeDtypeStruct((width, hidden_width), BF16),
         ],
         compiler_params=pltpu.CompilerParams(vmem_limit_bytes=16 << 20),
         cost_estimate=pl.CostEstimate(flops=0, bytes_accessed=0, transcendentals=0),
@@ -223,7 +223,7 @@
         saved[1],
         pltpu.with_memory_space_constraint(w_in, pltpu.HBM),
         pltpu.with_memory_space_constraint(w_down, pltpu.HBM),
-        fresh_grads,
+        pltpu.with_memory_space_constraint(fresh_grads, pltpu.HBM),
         payload,
     )
 
@@ -278,9 +278,12 @@
     dy_all, pre_all = [], []
     for k in range(steps):
         dy = placed(blocks)
-        dh = jnp.einsum("rd,hd->rh", dy, w_down_dir, preferred_element_type=F32)
+        dh = jnp.einsum("rd,dh->rh", dy, w_down_dir, preferred_element_type=F32)
         pre_grad = jnp.concatenate([dh * gate_factor[k], dh * activated[k]], axis=1).astype(BF16)
-        part = jnp.einsum("rc,dc->rd", pre_grad, w_in_dir, preferred_element_type=F32).astype(BF16)
+        part = jnp.einsum("rc,cd->rd", pre_grad, w_in_dir, preferred_element_type=F32).astype(BF16)
+        dy_all.append([to_core(dy, o) if o else dy for o in range(replicas)])
+        if k + 1 == steps:
+            part, dy_all[k] = lax.optimization_barrier((part, dy_all[k]))
         part = part.reshape(tensor_count, block_rows, width)
 
         def part_for(target):
@@ -290,7 +293,6 @@
         parts = []
         for s in range(1, tensor_count):
             parts.append(rotate(part_for(lax.rem(place + s, tensor_count)), s))
-        dy_all.append([to_core(dy, o) if o else dy for o in range(replicas)])
         pre_all.append([to_core(pre_grad, o) if o else pre_grad for o in range(replicas)])
         if k + 1 == steps:
             parts, grads = lax.optimization_barrier((parts, weight_grads()))
@@ -308,6 +310,8 @@
             other = theirs(entry) + to_core(summed[shard_rows:])
         else:
             other = to_core(handed[shard_rows:])
+        if 0 < k < steps - 1:
+            blocks, other = lax.optimization_barrier((blocks, other))
         hand_offs = hand_offs.at[:, k].set(by_direction(handed[:shard_rows], other))
         incoming = blocks[0].astype(F32)
     return (hand_offs[:, :, None], *grads)

time: 71.4 us -> 69 us (0.966)
  starting transfers between devices: 28.5 us -> 30.6 us
  matrix products: 5.68 us -> 3.58 us
  waiting for transfers between devices: 21.9 us -> 20.3 us
  local copies, waits for them, and re-layouts: 2.09 us -> 1.06 us
    ppermute x12, starting transfers between devices: 14.9 us -> 17.7 us  [rotate(): lax.ppermute(x, 'tensor', [(i, (i + shift) % tensor_count) for i in range...]
    dot_general x6, matrix products: 5.68 us -> 3.58 us  [the longest x3 2.25 us: local(): jnp.einsum('rc,cd->rd', pre_grad, w_in_dir, preferred_element_type=F32)]
    ppermute x8, starting transfers between devices: 10.5 us -> 8.46 us  [local(): lax.ppermute(payload, AXES, ring_pairs(sections, tensor_count, replicas, s))]
    ppermute x8, waiting for transfers between devices: 9.39 us -> 7.35 us  [local(): lax.ppermute(payload, AXES, ring_pairs(sections, tensor_count, replicas, s))]
    ppermute x13, starting transfers between devices: 3.03 us -> 4.48 us  [to_core(): return lax.ppermute(x, 'dp', [(i, i ^ offset) for i in range(replicas)])]
    unnamed x9 -> x7, local copies, waits for them, and re-layouts: 1.88 us -> 0.86 us
  transfers between devices with their start and end apart: 33 -> 33, of which waited for: 18 -> 14; matrix products, arithmetic and copies ran while one was open for 10% -> 8% of each run, Pallas kernels for 14% -> 15%
where the time goes in v4:
time: 69 us; the launch traced here: 68.8 us
  starting transfers between devices  30.6 us (44%)
  waiting for transfers between devices  20.3 us (29%)
  Pallas kernels  10.6 us (15%)
  matrix products  3.58 us (5%)
  other arithmetic  1.71 us (2%)
  local copies, waits for them, and re-layouts  1.06 us (2%)
  between operations  1 us (1%)
    ppermute x12, starting transfers between devices, rotate(): lax.ppermute(x, 'tensor', [(i, (i + shift) % tensor_count) for i in range...  17.7 us
    ppermute x12, waiting for transfers between devices, rotate(): lax.ppermute(x, 'tensor', [(i, (i + shift) % tensor_count) for i in range...  9.83 us
    ppermute x8, starting transfers between devices, local(): lax.ppermute(payload, AXES, ring_pairs(sections, tensor_count, replicas, s))  8.46 us
    ppermute x8, waiting for transfers between devices, local(): lax.ppermute(payload, AXES, ring_pairs(sections, tensor_count, replicas, s))  7.35 us
    pallas_call x1, Pallas kernels, weight_grads(): pl.pallas_call(functools.partial(weight_grads_kernel, steps, replicas, te...  5.97 us
    pallas_call x1, Pallas kernels, local(): pl.pallas_call(functools.partial(factors_kernel, tensor_count), grid_spec...  4.63 us
    ppermute x13, starting transfers between devices, to_core(): return lax.ppermute(x, 'dp', [(i, i ^ offset) for i in range(replicas)])  4.48 us
    ppermute x13, waiting for transfers between devices, to_core(): return lax.ppermute(x, 'dp', [(i, i ^ offset) for i in range(replicas)])  3.08 us
  transfers between devices with their start and end apart: 33, of which 14 were waited for; matrix products, arithmetic and copies ran while one was open for 8% of the time, Pallas kernels for 15%

profile of v4, /device:TPU:0, one launch (start us, length us, event | category | flops | bytes accessed | tf_op | source)
XLA Modules:
  0.0 68.8 jit_solution(4128096982700622133)
XLA Ops:
  0.6 0.5 collective-permute-start
  1.2 1.0 %select_bitcast_fusion = f32[8,3584]{1,0:T(8,128)S(1)} fusion(f32[2,1,8,3584]{3,2,1,0:T(8,128)} %param.11, pred[]{:T(512)S(6)} %eq.28), kind=kLoop, calls=%fused_computation.58 | loop fusion | flops 28672 | bytes 344065 | tf_op jit(solution)/shard_map/jit(_where)/select_n | solution.py:148
  2.2 0.3 collective-permute-done
  2.5 2.9 %collective-permute-start.1 = (bf16[16,3584]{1,0:T(8,128)(2,1)S(1)}, bf16[16,3584]{1,0:T(8,128)(2,1)S(1)}, u32[]{:S(2)}, u32[]{:S(2)}) collective-permute-start(bf16[16,3584]{1,0:T(8,128)(2,1)S(1)} %fusion.11._), channel_id=1, source_target_pairs={{0,2},{2,4},{4,6},{6,0},{1,3},{3,5},{5,7},{7,1},{8,10},{10,12},{12... | collective-permute-start | bytes 344072 | tf_op jit(solution)/shard_map/ppermute | solution.py:163
  5.4 1.5 %collective-permute-start.2 = (bf16[16,3584]{1,0:T(8,128)(2,1)S(1)}, bf16[16,3584]{1,0:T(8,128)(2,1)S(1)}, u32[]{:S(2)}, u32[]{:S(2)}) collective-permute-start(bf16[16,3584]{1,0:T(8,128)(2,1)S(1)} %fusion.11._), channel_id=1, source_target_pairs={{0,4},{2,6},{4,0},{6,2},{1,5},{3,7},{5,1},{7,3},{8,12},{10,14},{12... | collective-permute-start | bytes 344072 | tf_op jit(solution)/shard_map/ppermute | solution.py:163
  6.9 1.4 %collective-permute-start.3 = (bf16[16,3584]{1,0:T(8,128)(2,1)S(1)}, bf16[16,3584]{1,0:T(8,128)(2,1)S(1)}, u32[]{:S(2)}, u32[]{:S(2)}) collective-permute-start(bf16[16,3584]{1,0:T(8,128)(2,1)S(1)} %fusion.11._), channel_id=1, source_target_pairs={{0,6},{2,0},{4,2},{6,4},{1,7},{3,1},{5,3},{7,5},{8,14},{10,8},{12,... | collective-permute-start | bytes 344072 | tf_op jit(solution)/shard_map/ppermute | solution.py:163
  8.5 4.6 %factors.1 = (f32[3,64,256]{2,1,0:T(8,128)S(1)}, f32[3,64,256]{2,1,0:T(8,128)S(1)}, bf16[3,64,256]{2,1,0:T(8,128)(2,1)S(1)}, bf16[2,8,3584]{2,1,0:T(8,128)(2,1)S...) custom-call(s32[2]{0:T(128)S(1)} %pad_add_fusion.at._, ...), custom_call_target="tpu_custom_call" | custom-call | tf_op jit(solution)/shard_map/factors/pallas_call | solution.py:183
  13.3 0.4 fusion.21
  13.8 0.8 %convolution_convert_fusion.2 = bf16[64,3584]{1,0:T(8,128)(2,1)S(1)} fusion(bf16[512,3584]{1,0:T(8,128)(2,1)S(1)} %get-tuple-element.76, bf16[64,256]{1,0:T(8,128)(2,1)S(1)} %get-tuple-element.133, bf16[64,256]{1,0:T(8,128)(2,1)S(1)} %get-tuple-element.132), kind=kOutput, calls=%fused_computation.2 | convolution fusion | flops 235241472 | bytes 4194304 | tf_op jit(solution)/shard_map/rc,cd->rd/dot_general | solution.py:283
  14.6 1.1 %collective-permute-start.5 = (bf16[16,3584]{1,0:T(8,128)(2,1)S(1)}, bf16[16,3584]{1,0:T(8,128)(2,1)S(1)}, u32[]{:S(2)}, u32[]{:S(2)}) collective-permute-start(bf16[16,3584]{1,0:T(8,128)(2,1)S(1)} %get-tuple-element.117), channel_id=1, source_target_pairs={{0,2},{2,4},{4,6},{6,0},{1,3},{3,5},{5,7},{7,1},{8,10},{10,12},{12... | collective-permute-start | bytes 344072 | tf_op jit(solution)/shard_map/ppermute | solution.py:163
  15.7 0.4 collective-permute-start.6
  16.1 2.3 %collective-permute-start.7 = (bf16[16,3584]{1,0:T(8,128)(2,1)S(1)}, bf16[16,3584]{1,0:T(8,128)(2,1)S(1)}, u32[]{:S(2)}, u32[]{:S(2)}) collective-permute-start(bf16[16,3584]{1,0:T(8,128)(2,1)S(1)} %get-tuple-element.118), channel_id=1, source_target_pairs={{0,6},{2,0},{4,2},{6,4},{1,7},{3,1},{5,3},{7,5},{8,14},{10,8},{12,... | collective-permute-start | bytes 344072 | tf_op jit(solution)/shard_map/ppermute | solution.py:163
  18.4 3.1 %collective-permute-done.5 = bf16[16,3584]{1,0:T(8,128)(2,1)S(1)} collective-permute-done((bf16[16,3584]{1,0:T(8,128)(2,1)S(1)}, bf16[16,3584]{1,0:T(8,128)(2,1)S(1)}, u32[]{:S(2)}, u32[]{:S(2)}) %collective-permute-start.5) | collective-permute-done | bytes 114720 | tf_op jit(solution)/shard_map/ppermute | solution.py:163
  21.5 1.9 %collective-permute-done.6 = bf16[16,3584]{1,0:T(8,128)(2,1)S(1)} collective-permute-done((bf16[16,3584]{1,0:T(8,128)(2,1)S(1)}, bf16[16,3584]{1,0:T(8,128)(2,1)S(1)}, u32[]{:S(2)}, u32[]{:S(2)}) %collective-permute-start.6) | collective-permute-done | bytes 114720 | tf_op jit(solution)/shard_map/ppermute | solution.py:163
  23.6 1.6 %collective-permute-start.11 = (bf16[16,3584]{1,0:T(8,128)(2,1)S(1)}, bf16[16,3584]{1,0:T(8,128)(2,1)S(1)}, u32[]{:S(2)}, u32[]{:S(2)}) collective-permute-start(bf16[16,3584]{1,0:T(8,128)(2,1)S(1)} %get-tuple-element.100), channel_id=1, source_target_pairs={{0,7},{1,15},{2,1},{3,9},{4,3},{5,11},{6,5},{7,13},{8,6},{9,23},{1... | collective-permute-start | bytes 344072 | tf_op jit(solution)/shard_map/ppermute | solution.py:306
  25.1 1.2 %collective-permute-start.12 = (bf16[16,3584]{1,0:T(8,128)(2,1)S(1)}, bf16[16,3584]{1,0:T(8,128)(2,1)S(1)}, u32[]{:S(2)}, u32[]{:S(2)}) collective-permute-start(bf16[16,3584]{1,0:T(8,128)(2,1)S(1)} %get-tuple-element.100), channel_id=1, source_target_pairs={{0,5},{1,13},{2,7},{3,15},{4,1},{5,9},{6,3},{7,11},{8,4},{9,21},{1... | collective-permute-start | bytes 344072 | tf_op jit(solution)/shard_map/ppermute | solution.py:306
  26.3 2.0 %collective-permute-start.13 = (bf16[16,3584]{1,0:T(8,128)(2,1)S(1)}, bf16[16,3584]{1,0:T(8,128)(2,1)S(1)}, u32[]{:S(2)}, u32[]{:S(2)}) collective-permute-start(bf16[16,3584]{1,0:T(8,128)(2,1)S(1)} %get-tuple-element.100), channel_id=1, source_target_pairs={{0,3},{1,11},{2,5},{3,13},{4,7},{5,15},{6,1},{7,9},{8,2},{9,19},{1... | collective-permute-start | bytes 344072 | tf_op jit(solution)/shard_map/ppermute | solution.py:306
  28.3 0.7 %collective-permute-start.8 = (f32[8,3584]{1,0:T(8,128)S(1)}, f32[8,3584]{1,0:T(8,128)S(1)}, u32[]{:S(2)}, u32[]{:S(2)}) collective-permute-start(f32[8,3584]{1,0:T(8,128)S(1)} %slice.155), channel_id=1, source_target_pairs={{0,1},{1,0},{2,3},{3,2},{4,5},{5,4},{6,7},{7,6},{8,9},{9,8},{10,11... | collective-permute-start | bytes 344072 | tf_op jit(solution)/shard_map/ppermute | solution.py:160
  29.1 1.2 %collective-permute-done.11 = bf16[16,3584]{1,0:T(8,128)(2,1)S(1)} collective-permute-done((bf16[16,3584]{1,0:T(8,128)(2,1)S(1)}, bf16[16,3584]{1,0:T(8,128)(2,1)S(1)}, u32[]{:S(2)}, u32[]{:S(2)}) %collective-permute-start.11) | collective-permute-done | bytes 114720 | tf_op jit(solution)/shard_map/ppermute | solution.py:306
  30.3 1.0 %collective-permute-done.12 = bf16[16,3584]{1,0:T(8,128)(2,1)S(1)} collective-permute-done((bf16[16,3584]{1,0:T(8,128)(2,1)S(1)}, bf16[16,3584]{1,0:T(8,128)(2,1)S(1)}, u32[]{:S(2)}, u32[]{:S(2)}) %collective-permute-start.12) | collective-permute-done | bytes 114720 | tf_op jit(solution)/shard_map/ppermute | solution.py:306
  31.3 2.2 %collective-permute-done.13 = bf16[16,3584]{1,0:T(8,128)(2,1)S(1)} collective-permute-done((bf16[16,3584]{1,0:T(8,128)(2,1)S(1)}, bf16[16,3584]{1,0:T(8,128)(2,1)S(1)}, u32[]{:S(2)}, u32[]{:S(2)}) %collective-permute-start.13) | collective-permute-done | bytes 114720 | tf_op jit(solution)/shard_map/ppermute | solution.py:306
  33.5 0.4 fusion.19
  34.0 0.7 %convolution_convert_fusion.1 = bf16[64,3584]{1,0:T(8,128)(2,1)S(1)} fusion(bf16[512,3584]{1,0:T(8,128)(2,1)S(1)} %get-tuple-element.76, bf16[64,256]{1,0:T(8,128)(2,1)S(1)} %get-tuple-element.131, bf16[64,256]{1,0:T(8,128)(2,1)S(1)} %get-tuple-element.130), kind=kOutput, calls=%fused_computation.1 | convolution fusion | flops 235241472 | bytes 4194304 | tf_op jit(solution)/shard_map/rc,cd->rd/dot_general | solution.py:283
  34.8 0.3 collective-permute-start.14
  35.1 1.3 %collective-permute-start.15 = (bf16[16,3584]{1,0:T(8,128)(2,1)S(1)}, bf16[16,3584]{1,0:T(8,128)(2,1)S(1)}, u32[]{:S(2)}, u32[]{:S(2)}) collective-permute-start(bf16[16,3584]{1,0:T(8,128)(2,1)S(1)} %get-tuple-element.112), channel_id=1, source_target_pairs={{0,4},{2,6},{4,0},{6,2},{1,5},{3,7},{5,1},{7,3},{8,12},{10,14},{12... | collective-permute-start | bytes 344072 | tf_op jit(solution)/shard_map/ppermute | solution.py:163
  36.3 2.5 %collective-permute-start.16 = (bf16[16,3584]{1,0:T(8,128)(2,1)S(1)}, bf16[16,3584]{1,0:T(8,128)(2,1)S(1)}, u32[]{:S(2)}, u32[]{:S(2)}) collective-permute-start(bf16[16,3584]{1,0:T(8,128)(2,1)S(1)} %get-tuple-element.111), channel_id=1, source_target_pairs={{0,6},{2,0},{4,2},{6,4},{1,7},{3,1},{5,3},{7,5},{8,14},{10,8},{12,... | collective-permute-start | bytes 344072 | tf_op jit(solution)/shard_map/ppermute | solution.py:163
  38.9 2.9 %collective-permute-done.14 = bf16[16,3584]{1,0:T(8,128)(2,1)S(1)} collective-permute-done((bf16[16,3584]{1,0:T(8,128)(2,1)S(1)}, bf16[16,3584]{1,0:T(8,128)(2,1)S(1)}, u32[]{:S(2)}, u32[]{:S(2)}) %collective-permute-start.14) | collective-permute-done | bytes 114720 | tf_op jit(solution)/shard_map/ppermute | solution.py:163
  41.8 1.3 %collective-permute-done.15 = bf16[16,3584]{1,0:T(8,128)(2,1)S(1)} collective-permute-done((bf16[16,3584]{1,0:T(8,128)(2,1)S(1)}, bf16[16,3584]{1,0:T(8,128)(2,1)S(1)}, u32[]{:S(2)}, u32[]{:S(2)}) %collective-permute-start.15) | collective-permute-done | bytes 114720 | tf_op jit(solution)/shard_map/ppermute | solution.py:163
  43.1 0.6 collective-permute-done.16
  43.8 1.1 %collective-permute-start.18 = (bf16[16,3584]{1,0:T(8,128)(2,1)S(1)}, bf16[16,3584]{1,0:T(8,128)(2,1)S(1)}, u32[]{:S(2)}, u32[]{:S(2)}) collective-permute-start(bf16[16,3584]{1,0:T(8,128)(2,1)S(1)} %get-tuple-element.98), channel_id=1, source_target_pairs={{0,3},{1,11},{2,5},{3,13},{4,7},{5,15},{6,1},{7,9},{8,2},{9,19},{1... | collective-permute-start | bytes 344072 | tf_op jit(solution)/shard_map/ppermute | solution.py:306
  44.9 0.6 collective-permute-start.19
  45.5 2.0 %collective-permute-start.20 = (bf16[16,3584]{1,0:T(8,128)(2,1)S(1)}, bf16[16,3584]{1,0:T(8,128)(2,1)S(1)}, u32[]{:S(2)}, u32[]{:S(2)}) collective-permute-start(bf16[16,3584]{1,0:T(8,128)(2,1)S(1)} %get-tuple-element.98), channel_id=1, source_target_pairs={{0,7},{1,15},{2,1},{3,9},{4,3},{5,11},{6,5},{7,13},{8,6},{9,23},{1... | collective-permute-start | bytes 344072 | tf_op jit(solution)/shard_map/ppermute | solution.py:306
  47.5 1.4 %collective-permute-start.21 = (f32[8,3584]{1,0:T(8,128)S(1)}, f32[8,3584]{1,0:T(8,128)S(1)}, u32[]{:S(2)}, u32[]{:S(2)}) collective-permute-start(f32[8,3584]{1,0:T(8,128)S(1)} %get-tuple-element.127), channel_id=1, source_target_pairs={{0,1},{1,0},{2,3},{3,2},{4,5},{5,4},{6,7},{7,6},{8,9},{9,8},{10,11... | collective-permute-start | bytes 344072 | tf_op jit(solution)/shard_map/ppermute | solution.py:160
  48.9 0.9 %collective-permute-done.21 = f32[8,3584]{1,0:T(8,128)S(1)} collective-permute-done((f32[8,3584]{1,0:T(8,128)S(1)}, f32[8,3584]{1,0:T(8,128)S(1)}, u32[]{:S(2)}, u32[]{:S(2)}) %collective-permute-start.21) | collective-permute-done | bytes 114720 | tf_op jit(solution)/shard_map/ppermute | solution.py:160
  49.8 0.4 collective-permute-start.30
  50.4 2.3 %collective-permute-done.18 = bf16[16,3584]{1,0:T(8,128)(2,1)S(1)} collective-permute-done((bf16[16,3584]{1,0:T(8,128)(2,1)S(1)}, bf16[16,3584]{1,0:T(8,128)(2,1)S(1)}, u32[]{:S(2)}, u32[]{:S(2)}) %collective-permute-start.18) | collective-permute-done | bytes 114720 | tf_op jit(solution)/shard_map/ppermute | solution.py:306
  52.7 0.5 collective-permute-start.31
  53.2 0.6 collective-permute-done.20
  54.0 0.4 fusion.17
  54.5 0.7 %convolution_convert_fusion = bf16[64,3584]{1,0:T(8,128)(2,1)S(1)} fusion(bf16[512,3584]{1,0:T(8,128)(2,1)S(1)} %get-tuple-element.76, bf16[64,256]{1,0:T(8,128)(2,1)S(1)} %get-tuple-element.129, bf16[64,256]{1,0:T(8,128)(2,1)S(1)} %get-tuple-element.128), kind=kOutput, calls=%fused_computation | convolution fusion | flops 235241472 | bytes 4194304 | tf_op jit(solution)/shard_map/rc,cd->rd/dot_general | solution.py:283
  55.2 0.6 collective-permute-done.22.refs_15_
  56.0 0.4 collective-permute-start.28
  56.4 1.5 %collective-permute-start.23 = (bf16[16,3584]{1,0:T(8,128)(2,1)S(1)}, bf16[16,3584]{1,0:T(8,128)(2,1)S(1)}, u32[]{:S(2)}, u32[]{:S(2)}) collective-permute-start(bf16[16,3584]{1,0:T(8,128)(2,1)S(1)} %get-tuple-element.105), channel_id=1, source_target_pairs={{0,2},{2,4},{4,6},{6,0},{1,3},{3,5},{5,7},{7,1},{8,10},{10,12},{12... | collective-permute-start | bytes 344072 | tf_op jit(solution)/shard_map/ppermute | solution.py:163
  57.9 1.2 %collective-permute-start.24 = (bf16[16,3584]{1,0:T(8,128)(2,1)S(1)}, bf16[16,3584]{1,0:T(8,128)(2,1)S(1)}, u32[]{:S(2)}, u32[]{:S(2)}) collective-permute-start(bf16[16,3584]{1,0:T(8,128)(2,1)S(1)} %get-tuple-element.104), channel_id=1, source_target_pairs={{0,4},{2,6},{4,0},{6,2},{1,5},{3,7},{5,1},{7,3},{8,12},{10,14},{12... | collective-permute-start | bytes 344072 | tf_op jit(solution)/shard_map/ppermute | solution.py:163
  59.1 1.3 %collective-permute-start.25 = (bf16[16,3584]{1,0:T(8,128)(2,1)S(1)}, bf16[16,3584]{1,0:T(8,128)(2,1)S(1)}, u32[]{:S(2)}, u32[]{:S(2)}) collective-permute-start(bf16[16,3584]{1,0:T(8,128)(2,1)S(1)} %get-tuple-element.103), channel_id=1, source_target_pairs={{0,6},{2,0},{4,2},{6,4},{1,7},{3,1},{5,3},{7,5},{8,14},{10,8},{12,... | collective-permute-start | bytes 344072 | tf_op jit(solution)/shard_map/ppermute | solution.py:163
  60.4 6.0 %weight_grads.1 = (f32[2,1,1792,512]{3,2,1,0:T(8,128)}, f32[2,1,256,1792]{3,2,1,0:T(8,128)}) custom-call(s32[2]{0:T(128)S(1)} %pad_add_fusion.at._, bf16[2,3,1,32,3584]{4,3,2,1,0:T(8,128)(2,1)S(1)} %copy-done, bf16[2,3,1,32,3584]{4,3,2,1,0:T(8,128)(2,1)S(1)} %collective-permute-done.4.peer_ref.refs_1_, bf16[64,512]{1,0:T(8,128)(2,1)S(1)} %pad_maximum_fusion.4.refs_2_, ...), custom_call_target="tpu_custom_call" | custom-call | tf_op jit(solution)/shard_map/weight_grads/pallas_call | solution.py:239
  66.6 1.3 %collective-permute-done.32 = f32[8,3584]{1,0:T(8,128)S(1)} collective-permute-done((f32[8,3584]{1,0:T(8,128)S(1)}, f32[8,3584]{1,0:T(8,128)S(1)}, u32[]{:S(2)}, u32[]{:S(2)}) %collective-permute-start.32) | collective-permute-done | bytes 114720 | tf_op jit(solution)/shard_map/ppermute | solution.py:160
  68.0 0.8 %copy-done.2 = f32[2,3,1,8,3584]{4,3,1,0,2:T(8,128)} copy-done((f32[2,3,1,8,3584]{4,3,1,0,2:T(8,128)}, f32[2,3,1,8,3584]{4,3,1,0,2:T(8,128)S(1)}, u32[]{:S(2)}) %copy-start.2) | copy-done | bytes 688152
  (62 shorter events, 1.6 us)
Async XLA Ops:
  0.6 1.8 %collective-permute-start = (f32[2,1,8,3584]{3,2,1,0:T(8,128)}, f32[2,1,8,3584]{3,2,1,0:T(8,128)S(1)}, u32[]{:S(2)}, u32[]{:S(2)}) collective-permute-start(f32[2,1,8,3584]{3,2,1,0:T(8,128)} %param.11), channel_id=1, source_target_pairs={{0,1},{1,0},{2,3},{3,2},{4,5},{5,4},{6,7},{7,6},{8,9},{9,8},{10,11... | collective-permute-start | bytes 688136 | tf_op jit(solution)/shard_map/ppermute | solution.py:160
  1.1 7.3 %collective-permute-start.4 = (bf16[2,3,1,32,3584]{4,3,2,1,0:T(8,128)(2,1)}, bf16[2,3,1,32,3584]{4,3,2,1,0:T(8,128)(2,1)S(1)}, u32[]{:S(2)}, u32[]{:S(2)}) collective-permute-start(bf16[2,3,1,32,3584]{4,3,2,1,0:T(8,128)(2,1)} %refs_0_.1), channel_id=1, source_target_pairs={{0,1},{1,0},{2,3},{3,2},{4,5},{5,4},{6,7},{7,6},{8,9},{9,8},{10,11... | collective-permute-start | bytes 4128776 | tf_op jit(solution)/shard_map/ppermute | solution.py:160
  2.5 10.6 %collective-permute-start.1 = (bf16[16,3584]{1,0:T(8,128)(2,1)S(1)}, bf16[16,3584]{1,0:T(8,128)(2,1)S(1)}, u32[]{:S(2)}, u32[]{:S(2)}) collective-permute-start(bf16[16,3584]{1,0:T(8,128)(2,1)S(1)} %fusion.11._), channel_id=1, source_target_pairs={{0,2},{2,4},{4,6},{6,0},{1,3},{3,5},{5,7},{7,1},{8,10},{10,12},{12... | collective-permute-start | bytes 344072 | tf_op jit(solution)/shard_map/ppermute | solution.py:163
  5.4 7.7 %collective-permute-start.2 = (bf16[16,3584]{1,0:T(8,128)(2,1)S(1)}, bf16[16,3584]{1,0:T(8,128)(2,1)S(1)}, u32[]{:S(2)}, u32[]{:S(2)}) collective-permute-start(bf16[16,3584]{1,0:T(8,128)(2,1)S(1)} %fusion.11._), channel_id=1, source_target_pairs={{0,4},{2,6},{4,0},{6,2},{1,5},{3,7},{5,1},{7,3},{8,12},{10,14},{12... | collective-permute-start | bytes 344072 | tf_op jit(solution)/shard_map/ppermute | solution.py:163
  6.9 6.2 %collective-permute-start.3 = (bf16[16,3584]{1,0:T(8,128)(2,1)S(1)}, bf16[16,3584]{1,0:T(8,128)(2,1)S(1)}, u32[]{:S(2)}, u32[]{:S(2)}) collective-permute-start(bf16[16,3584]{1,0:T(8,128)(2,1)S(1)} %fusion.11._), channel_id=1, source_target_pairs={{0,6},{2,0},{4,2},{6,4},{1,7},{3,1},{5,3},{7,5},{8,14},{10,8},{12,... | collective-permute-start | bytes 344072 | tf_op jit(solution)/shard_map/ppermute | solution.py:163
  13.1 5.2 %collective-permute-start.9 = (bf16[2,8,3584]{2,1,0:T(8,128)(2,1)S(1)}, bf16[2,8,3584]{2,1,0:T(8,128)(2,1)S(1)}, u32[]{:S(2)}, u32[]{:S(2)}) collective-permute-start(bf16[2,8,3584]{2,1,0:T(8,128)(2,1)S(1)} %get-tuple-element.77), channel_id=1, source_target_pairs={{0,1},{1,0},{2,3},{3,2},{4,5},{5,4},{6,7},{7,6},{8,9},{9,8},{10,11... | collective-permute-start | bytes 344072 | tf_op jit(solution)/shard_map/ppermute | solution.py:160
  14.6 6.9 %collective-permute-start.5 = (bf16[16,3584]{1,0:T(8,128)(2,1)S(1)}, bf16[16,3584]{1,0:T(8,128)(2,1)S(1)}, u32[]{:S(2)}, u32[]{:S(2)}) collective-permute-start(bf16[16,3584]{1,0:T(8,128)(2,1)S(1)} %get-tuple-element.117), channel_id=1, source_target_pairs={{0,2},{2,4},{4,6},{6,0},{1,3},{3,5},{5,7},{7,1},{8,10},{10,12},{12... | collective-permute-start | bytes 344072 | tf_op jit(solution)/shard_map/ppermute | solution.py:163
  15.7 7.7 %collective-permute-start.6 = (bf16[16,3584]{1,0:T(8,128)(2,1)S(1)}, bf16[16,3584]{1,0:T(8,128)(2,1)S(1)}, u32[]{:S(2)}, u32[]{:S(2)}) collective-permute-start(bf16[16,3584]{1,0:T(8,128)(2,1)S(1)} %get-tuple-element.119), channel_id=1, source_target_pairs={{0,4},{2,6},{4,0},{6,2},{1,5},{3,7},{5,1},{7,3},{8,12},{10,14},{12... | collective-permute-start | bytes 344072 | tf_op jit(solution)/shard_map/ppermute | solution.py:163
  16.1 7.4 %collective-permute-start.7 = (bf16[16,3584]{1,0:T(8,128)(2,1)S(1)}, bf16[16,3584]{1,0:T(8,128)(2,1)S(1)}, u32[]{:S(2)}, u32[]{:S(2)}) collective-permute-start(bf16[16,3584]{1,0:T(8,128)(2,1)S(1)} %get-tuple-element.118), channel_id=1, source_target_pairs={{0,6},{2,0},{4,2},{6,4},{1,7},{3,1},{5,3},{7,5},{8,14},{10,8},{12,... | collective-permute-start | bytes 344072 | tf_op jit(solution)/shard_map/ppermute | solution.py:163
  23.5 5.5 %collective-permute-start.10 = (bf16[16,3584]{1,0:T(8,128)(2,1)S(1)}, bf16[16,3584]{1,0:T(8,128)(2,1)S(1)}, u32[]{:S(2)}, u32[]{:S(2)}) collective-permute-start(bf16[16,3584]{1,0:T(8,128)(2,1)S(1)} %get-tuple-element.100), channel_id=1, source_target_pairs={{0,1},{1,9},{2,3},{3,11},{4,5},{5,13},{6,7},{7,15},{8,0},{9,17},{1... | collective-permute-start | bytes 344072 | tf_op jit(solution)/shard_map/ppermute | solution.py:306
  23.6 6.7 %collective-permute-start.11 = (bf16[16,3584]{1,0:T(8,128)(2,1)S(1)}, bf16[16,3584]{1,0:T(8,128)(2,1)S(1)}, u32[]{:S(2)}, u32[]{:S(2)}) collective-permute-start(bf16[16,3584]{1,0:T(8,128)(2,1)S(1)} %get-tuple-element.100), channel_id=1, source_target_pairs={{0,7},{1,15},{2,1},{3,9},{4,3},{5,11},{6,5},{7,13},{8,6},{9,23},{1... | collective-permute-start | bytes 344072 | tf_op jit(solution)/shard_map/ppermute | solution.py:306
  25.1 6.1 %collective-permute-start.12 = (bf16[16,3584]{1,0:T(8,128)(2,1)S(1)}, bf16[16,3584]{1,0:T(8,128)(2,1)S(1)}, u32[]{:S(2)}, u32[]{:S(2)}) collective-permute-start(bf16[16,3584]{1,0:T(8,128)(2,1)S(1)} %get-tuple-element.100), channel_id=1, source_target_pairs={{0,5},{1,13},{2,7},{3,15},{4,1},{5,9},{6,3},{7,11},{8,4},{9,21},{1... | collective-permute-start | bytes 344072 | tf_op jit(solution)/shard_map/ppermute | solution.py:306
  26.3 7.1 %collective-permute-start.13 = (bf16[16,3584]{1,0:T(8,128)(2,1)S(1)}, bf16[16,3584]{1,0:T(8,128)(2,1)S(1)}, u32[]{:S(2)}, u32[]{:S(2)}) collective-permute-start(bf16[16,3584]{1,0:T(8,128)(2,1)S(1)} %get-tuple-element.100), channel_id=1, source_target_pairs={{0,3},{1,11},{2,5},{3,13},{4,7},{5,15},{6,1},{7,9},{8,2},{9,19},{1... | collective-permute-start | bytes 344072 | tf_op jit(solution)/shard_map/ppermute | solution.py:306
  28.3 10.5 %collective-permute-start.8 = (f32[8,3584]{1,0:T(8,128)S(1)}, f32[8,3584]{1,0:T(8,128)S(1)}, u32[]{:S(2)}, u32[]{:S(2)}) collective-permute-start(f32[8,3584]{1,0:T(8,128)S(1)} %slice.155), channel_id=1, source_target_pairs={{0,1},{1,0},{2,3},{3,2},{4,5},{5,4},{6,7},{7,6},{8,9},{9,8},{10,11... | collective-permute-start | bytes 344072 | tf_op jit(solution)/shard_map/ppermute | solution.py:160
  33.5 5.3 %copy-start.1 = (f32[2,1,8,3584]{3,2,1,0:T(8,128)S(1)}, f32[2,1,8,3584]{3,2,1,0:T(8,128)}, u32[]{:S(2)}) copy-start(f32[2,1,8,3584]{3,2,1,0:T(8,128)} %param.11) | copy-start | bytes 688132
  34.8 7.0 %collective-permute-start.14 = (bf16[16,3584]{1,0:T(8,128)(2,1)S(1)}, bf16[16,3584]{1,0:T(8,128)(2,1)S(1)}, u32[]{:S(2)}, u32[]{:S(2)}) collective-permute-start(bf16[16,3584]{1,0:T(8,128)(2,1)S(1)} %get-tuple-element.110), channel_id=1, source_target_pairs={{0,2},{2,4},{4,6},{6,0},{1,3},{3,5},{5,7},{7,1},{8,10},{10,12},{12... | collective-permute-start | bytes 344072 | tf_op jit(solution)/shard_map/ppermute | solution.py:163
  35.1 8.0 %collective-permute-start.15 = (bf16[16,3584]{1,0:T(8,128)(2,1)S(1)}, bf16[16,3584]{1,0:T(8,128)(2,1)S(1)}, u32[]{:S(2)}, u32[]{:S(2)}) collective-permute-start(bf16[16,3584]{1,0:T(8,128)(2,1)S(1)} %get-tuple-element.112), channel_id=1, source_target_pairs={{0,4},{2,6},{4,0},{6,2},{1,5},{3,7},{5,1},{7,3},{8,12},{10,14},{12... | collective-permute-start | bytes 344072 | tf_op jit(solution)/shard_map/ppermute | solution.py:163
  36.3 7.4 %collective-permute-start.16 = (bf16[16,3584]{1,0:T(8,128)(2,1)S(1)}, bf16[16,3584]{1,0:T(8,128)(2,1)S(1)}, u32[]{:S(2)}, u32[]{:S(2)}) collective-permute-start(bf16[16,3584]{1,0:T(8,128)(2,1)S(1)} %get-tuple-element.111), channel_id=1, source_target_pairs={{0,6},{2,0},{4,2},{6,4},{1,7},{3,1},{5,3},{7,5},{8,14},{10,8},{12,... | collective-permute-start | bytes 344072 | tf_op jit(solution)/shard_map/ppermute | solution.py:163
  43.8 6.4 %collective-permute-start.17 = (bf16[16,3584]{1,0:T(8,128)(2,1)S(1)}, bf16[16,3584]{1,0:T(8,128)(2,1)S(1)}, u32[]{:S(2)}, u32[]{:S(2)}) collective-permute-start(bf16[16,3584]{1,0:T(8,128)(2,1)S(1)} %get-tuple-element.98), channel_id=1, source_target_pairs={{0,1},{1,9},{2,3},{3,11},{4,5},{5,13},{6,7},{7,15},{8,0},{9,17},{1... | collective-permute-start | bytes 344072 | tf_op jit(solution)/shard_map/ppermute | solution.py:306
  43.8 8.9 %collective-permute-start.18 = (bf16[16,3584]{1,0:T(8,128)(2,1)S(1)}, bf16[16,3584]{1,0:T(8,128)(2,1)S(1)}, u32[]{:S(2)}, u32[]{:S(2)}) collective-permute-start(bf16[16,3584]{1,0:T(8,128)(2,1)S(1)} %get-tuple-element.98), channel_id=1, source_target_pairs={{0,3},{1,11},{2,5},{3,13},{4,7},{5,15},{6,1},{7,9},{8,2},{9,19},{1... | collective-permute-start | bytes 344072 | tf_op jit(solution)/shard_map/ppermute | solution.py:306
  44.9 7.8 %collective-permute-start.19 = (bf16[16,3584]{1,0:T(8,128)(2,1)S(1)}, bf16[16,3584]{1,0:T(8,128)(2,1)S(1)}, u32[]{:S(2)}, u32[]{:S(2)}) collective-permute-start(bf16[16,3584]{1,0:T(8,128)(2,1)S(1)} %get-tuple-element.98), channel_id=1, source_target_pairs={{0,5},{1,13},{2,7},{3,15},{4,1},{5,9},{6,3},{7,11},{8,4},{9,21},{1... | collective-permute-start | bytes 344072 | tf_op jit(solution)/shard_map/ppermute | solution.py:306
  45.5 8.3 %collective-permute-start.20 = (bf16[16,3584]{1,0:T(8,128)(2,1)S(1)}, bf16[16,3584]{1,0:T(8,128)(2,1)S(1)}, u32[]{:S(2)}, u32[]{:S(2)}) collective-permute-start(bf16[16,3584]{1,0:T(8,128)(2,1)S(1)} %get-tuple-element.98), channel_id=1, source_target_pairs={{0,7},{1,15},{2,1},{3,9},{4,3},{5,11},{6,5},{7,13},{8,6},{9,23},{1... | collective-permute-start | bytes 344072 | tf_op jit(solution)/shard_map/ppermute | solution.py:306
  47.5 2.3 %collective-permute-start.21 = (f32[8,3584]{1,0:T(8,128)S(1)}, f32[8,3584]{1,0:T(8,128)S(1)}, u32[]{:S(2)}, u32[]{:S(2)}) collective-permute-start(f32[8,3584]{1,0:T(8,128)S(1)} %get-tuple-element.127), channel_id=1, source_target_pairs={{0,1},{1,0},{2,3},{3,2},{4,5},{5,4},{6,7},{7,6},{8,9},{9,8},{10,11... | collective-permute-start | bytes 344072 | tf_op jit(solution)/shard_map/ppermute | solution.py:160
  49.8 9.2 %collective-permute-start.30 = (bf16[64,3584]{1,0:T(8,128)(2,1)S(1)}, bf16[64,3584]{1,0:T(8,128)(2,1)S(1)}, u32[]{:S(2)}, u32[]{:S(2)}) collective-permute-start(bf16[64,3584]{1,0:T(8,128)(2,1)S(1)} %pad_maximum_fusion.refs_10_), channel_id=1, source_target_pairs={{0,1},{1,0},{2,3},{3,2},{4,5},{5,4},{6,7},{7,6},{8,9},{9,8},{10,11... | collective-permute-start | bytes 1376264 | tf_op jit(solution)/shard_map/ppermute | solution.py:160
  50.2 5.8 %collective-permute-start.26 = (bf16[64,512]{1,0:T(8,128)(2,1)S(1)}, bf16[64,512]{1,0:T(8,128)(2,1)S(1)}, u32[]{:S(2)}, u32[]{:S(2)}) collective-permute-start(bf16[64,512]{1,0:T(8,128)(2,1)S(1)} %pad_maximum_fusion.4.refs_2_), channel_id=1, source_target_pairs={{0,1},{1,0},{2,3},{3,2},{4,5},{5,4},{6,7},{7,6},{8,9},{9,8},{10,11... | collective-permute-start | bytes 196616 | tf_op jit(solution)/shard_map/ppermute | solution.py:160
  52.7 3.7 %collective-permute-start.29 = (bf16[3,64,256]{2,1,0:T(8,128)(2,1)S(1)}, bf16[3,64,256]{2,1,0:T(8,128)(2,1)S(1)}, u32[]{:S(2)}, u32[]{:S(2)}) collective-permute-start(bf16[3,64,256]{2,1,0:T(8,128)(2,1)S(1)} %get-tuple-element.85.refs_8_), channel_id=1, source_target_pairs={{0,1},{1,0},{2,3},{3,2},{4,5},{5,4},{6,7},{7,6},{8,9},{9,8},{10,11... | collective-permute-start | bytes 294920 | tf_op jit(solution)/shard_map/ppermute | solution.py:160
  52.7 7.7 %collective-permute-start.31 = (bf16[64,3584]{1,0:T(8,128)(2,1)S(1)}, bf16[64,3584]{1,0:T(8,128)(2,1)S(1)}, u32[]{:S(2)}, u32[]{:S(2)}) collective-permute-start(bf16[64,3584]{1,0:T(8,128)(2,1)S(1)} %pad_maximum_fusion.1.refs_11_), channel_id=1, source_target_pairs={{0,1},{1,0},{2,3},{3,2},{4,5},{5,4},{6,7},{7,6},{8,9},{9,8},{10,11... | collective-permute-start | bytes 1376264 | tf_op jit(solution)/shard_map/ppermute | solution.py:160
  53.9 1.9 %collective-permute-start.22 = (bf16[64,3584]{1,0:T(8,128)(2,1)S(1)}, bf16[64,3584]{1,0:T(8,128)(2,1)S(1)}, u32[]{:S(2)}, u32[]{:S(2)}) collective-permute-start(bf16[64,3584]{1,0:T(8,128)(2,1)S(1)} %pad_maximum_fusion.2.refs_12_), channel_id=1, source_target_pairs={{0,1},{1,0},{2,3},{3,2},{4,5},{5,4},{6,7},{7,6},{8,9},{9,8},{10,11... | collective-permute-start | bytes 1376264 | tf_op jit(solution)/shard_map/ppermute | solution.py:160
  54.4 6.0 %copy-start = (bf16[2,3,1,32,3584]{4,3,2,1,0:T(8,128)(2,1)S(1)}, bf16[2,3,1,32,3584]{4,3,2,1,0:T(8,128)(2,1)}, u32[]{:S(2)}) copy-start(bf16[2,3,1,32,3584]{4,3,2,1,0:T(8,128)(2,1)} %refs_0_.1) | copy-start | bytes 4128772
  55.8 2.1 %collective-permute-start.27 = (bf16[64,512]{1,0:T(8,128)(2,1)S(1)}, bf16[64,512]{1,0:T(8,128)(2,1)S(1)}, u32[]{:S(2)}, u32[]{:S(2)}) collective-permute-start(bf16[64,512]{1,0:T(8,128)(2,1)S(1)} %pad_maximum_fusion.5.refs_3_), channel_id=1, source_target_pairs={{0,1},{1,0},{2,3},{3,2},{4,5},{5,4},{6,7},{7,6},{8,9},{9,8},{10,11... | collective-permute-start | bytes 196616 | tf_op jit(solution)/shard_map/ppermute | solution.py:160
  56.0 4.5 %collective-permute-start.28 = (bf16[64,512]{1,0:T(8,128)(2,1)S(1)}, bf16[64,512]{1,0:T(8,128)(2,1)S(1)}, u32[]{:S(2)}, u32[]{:S(2)}) collective-permute-start(bf16[64,512]{1,0:T(8,128)(2,1)S(1)} %pad_maximum_fusion.6.refs_4_), channel_id=1, source_target_pairs={{0,1},{1,0},{2,3},{3,2},{4,5},{5,4},{6,7},{7,6},{8,9},{9,8},{10,11... | collective-permute-start | bytes 196616 | tf_op jit(solution)/shard_map/ppermute | solution.py:160
  56.4 10.0 %collective-permute-start.23 = (bf16[16,3584]{1,0:T(8,128)(2,1)S(1)}, bf16[16,3584]{1,0:T(8,128)(2,1)S(1)}, u32[]{:S(2)}, u32[]{:S(2)}) collective-permute-start(bf16[16,3584]{1,0:T(8,128)(2,1)S(1)} %get-tuple-element.105), channel_id=1, source_target_pairs={{0,2},{2,4},{4,6},{6,0},{1,3},{3,5},{5,7},{7,1},{8,10},{10,12},{12... | collective-permute-start | bytes 344072 | tf_op jit(solution)/shard_map/ppermute | solution.py:163
  57.9 8.5 %collective-permute-start.24 = (bf16[16,3584]{1,0:T(8,128)(2,1)S(1)}, bf16[16,3584]{1,0:T(8,128)(2,1)S(1)}, u32[]{:S(2)}, u32[]{:S(2)}) collective-permute-start(bf16[16,3584]{1,0:T(8,128)(2,1)S(1)} %get-tuple-element.104), channel_id=1, source_target_pairs={{0,4},{2,6},{4,0},{6,2},{1,5},{3,7},{5,1},{7,3},{8,12},{10,14},{12... | collective-permute-start | bytes 344072 | tf_op jit(solution)/shard_map/ppermute | solution.py:163
  59.1 7.4 %collective-permute-start.25 = (bf16[16,3584]{1,0:T(8,128)(2,1)S(1)}, bf16[16,3584]{1,0:T(8,128)(2,1)S(1)}, u32[]{:S(2)}, u32[]{:S(2)}) collective-permute-start(bf16[16,3584]{1,0:T(8,128)(2,1)S(1)} %get-tuple-element.103), channel_id=1, source_target_pairs={{0,6},{2,0},{4,2},{6,4},{1,7},{3,1},{5,3},{7,5},{8,14},{10,8},{12,... | collective-permute-start | bytes 344072 | tf_op jit(solution)/shard_map/ppermute | solution.py:163
  66.5 1.4 %collective-permute-start.32 = (f32[8,3584]{1,0:T(8,128)S(1)}, f32[8,3584]{1,0:T(8,128)S(1)}, u32[]{:S(2)}, u32[]{:S(2)}) collective-permute-start(f32[8,3584]{1,0:T(8,128)S(1)} %get-tuple-element.125), channel_id=1, source_target_pairs={{0,1},{1,0},{2,3},{3,2},{4,5},{5,4},{6,7},{7,6},{8,9},{9,8},{10,11... | collective-permute-start | bytes 344072 | tf_op jit(solution)/shard_map/ppermute | solution.py:160
  68.0 0.9 %copy-start.2 = (f32[2,3,1,8,3584]{4,3,1,0,2:T(8,128)}, f32[2,3,1,8,3584]{4,3,1,0,2:T(8,128)S(1)}, u32[]{:S(2)}) copy-start(f32[2,3,1,8,3584]{4,3,1,0,2:T(8,128)S(1)} %fusion.1) | copy-start | bytes 2064388

commit v5 on v4

--- a/solution.py
+++ b/solution.py
@@ -36,8 +36,8 @@
 
 
 def factors_kernel(
-    places, at, own_ref, peer_ref, w_ref, down_ref, fresh_ref, _,
-    gate_ref, up_ref, hidden_ref, send_ref, keep_ref, w_copy, down_copy, total, mixed
+    places, at, own_ref, peer_ref, w_ref, down_ref, fresh_ref, fresh_peer_ref, _,
+    gate_ref, up_ref, hidden_ref, fresh_out, w_copy, down_copy, total, mixed
 ):
     steps, batch_rows, depth = own_ref.shape[1], own_ref.shape[3], own_ref.shape[4]
     shard_rows = batch_rows // places
@@ -55,8 +55,10 @@
     @pl.when(step == 0)
     def _():
         total[...] = product
-        send_ref[...] = fresh_ref[at[0]].astype(BF16)
-        keep_ref[...] = fresh_ref[1 - at[0]].astype(BF16)
+        for k in range(fresh_out.shape[0]):
+            fresh_out[k] = jnp.concatenate(
+                [fresh_peer_ref[1 - at[0], k], fresh_ref[1 - at[0], k]], axis=0
+            ).astype(BF16)
 
     @pl.when(step > 0)
     def _():
@@ -80,20 +82,12 @@
 
 
 def weight_grads_kernel(steps, replicas, places, _, *refs):
-    saved = refs[:replicas]
-    pre = refs[replicas:replicas + replicas * steps]
-    hidden = refs[replicas + replicas * steps:2 * replicas + replicas * steps]
-    dy = refs[2 * replicas + replicas * steps:2 * replicas + 2 * replicas * steps]
+    saved, pre, dy = refs[:replicas], refs[replicas:2 * replicas], refs[2 * replicas:3 * replicas]
     in_ref, down_ref, pre_rows, hidden_rows = refs[-4:]
     batch_rows, block = saved[0].shape[3], saved[0].shape[4]
-    pair_rows = 2 * batch_rows
     shard_rows = batch_rows // places
+    hidden_width = hidden_rows.shape[1]
     count = steps * batch_rows
-
-    def columns_of(parity):
-        return jnp.concatenate(
-            [dy[offset * steps + k][...] for offset in range(parity, replicas, 2) for k in range(steps)], axis=0
-        )
 
     for parity in range(2):
 
@@ -102,12 +96,12 @@
             @pl.when(pl.program_id(1) == 0)
             def _():
                 for pair in range(replicas // 2):
-                    offset = 2 * pair + parity
-                    hidden_rows[pair * 2 * count:(pair + 1) * 2 * count] = hidden[offset][...].reshape(
-                        2 * count, hidden[offset].shape[2]
+                    held = pre[2 * pair + parity]
+                    hidden_rows[pair * 2 * count:(pair + 1) * 2 * count] = held[:, :, 2 * hidden_width:].reshape(
+                        2 * count, hidden_width
                     )
                     for k in range(steps):
-                        values = pre[offset * steps + k][...].astype(F32)
+                        values = held[k, :, :2 * hidden_width].astype(F32)
                         for r in range(2):
                             half = jnp.concatenate(
                                 [
@@ -120,7 +114,10 @@
                             pre_rows[start:start + batch_rows] = half.astype(BF16)
 
             down_ref[0, 0] = lax.dot_general(
-                hidden_rows[...], columns_of(parity), (((0,), (0,)), ((), ())), preferred_element_type=F32
+                hidden_rows[...],
+                jnp.concatenate([dy[offset][...] for offset in range(parity, replicas, 2)], axis=0),
+                (((0,), (0,)), ((), ())),
+                preferred_element_type=F32,
             )
 
     inputs = jnp.concatenate([x[...].reshape(count, block) for x in saved], axis=0)
@@ -174,13 +171,14 @@
 
     entry = entry_grads[:, 0]
     entry_peer = to_core(entry_grads)[:, 0]
+    fresh_peer = to_core(fresh_grads)
     incoming = jnp.concatenate([mine(entry), mine(entry_peer)])
     payload = incoming.astype(BF16)
     blocks = [payload] + [rotate(payload, s) for s in range(1, tensor_count)]
     saved = [saved_inputs] + [to_core(saved_inputs, offset) for offset in range(1, replicas)]
     which = jnp.stack([core, replica]).astype(jnp.int32)
     depth = lane_block(width, 1792)
-    gate_factor, activated, hidden, fresh_send, fresh_keep, w_in_dir, w_down_dir = pl.pallas_call(
+    gate_factor, activated, hidden, fresh_pair, w_in_dir, w_down_dir = pl.pallas_call(
         functools.partial(factors_kernel, tensor_count),
         grid_spec=pltpu.PrefetchScalarGridSpec(
             num_scalar_prefetch=1,
@@ -191,10 +189,11 @@
                 pl.BlockSpec((1, 1, depth, 2 * hidden_width), lambda i, at: (at[0], 0, i, 0)),
                 pl.BlockSpec((1, 1, hidden_width, depth), lambda i, at: (at[0], 0, 0, i)),
                 pl.BlockSpec(fresh_grads.shape, lambda i, at: (0, 0, 0, 0)),
+                pl.BlockSpec(fresh_grads.shape, lambda i, at: (0, 0, 0, 0)),
                 pl.BlockSpec(memory_space=pl.ANY),
             ],
             out_specs=[pl.BlockSpec((steps, pair_rows, hidden_width), lambda i, at: (0, 0, 0))] * 3
-            + [pl.BlockSpec(fresh_grads.shape[1:], lambda i, at: (0, 0, 0))] * 2
+            + [pl.BlockSpec((steps - 1, block_rows, width), lambda i, at: (0, 0, 0))]
             + [
                 pl.BlockSpec((2 * hidden_width, depth), lambda i, at: (0, i)),
                 pl.BlockSpec((depth, hidden_width), lambda i, at: (i, 0)),
@@ -209,7 +208,7 @@
             jax.ShapeDtypeStruct((steps, pair_rows, hidden_width), F32),
             jax.ShapeDtypeStruct((steps, pair_rows, hidden_width), BF16),
         ]
-        + [jax.ShapeDtypeStruct(fresh_grads.shape[1:], BF16)] * 2
+        + [jax.ShapeDtypeStruct((steps - 1, block_rows, width), BF16)]
         + [
             jax.ShapeDtypeStruct((2 * hidden_width, width), BF16),
             jax.ShapeDtypeStruct((width, hidden_width), BF16),
@@ -224,16 +223,15 @@
         pltpu.with_memory_space_constraint(w_in, pltpu.HBM),
         pltpu.with_memory_space_constraint(w_down, pltpu.HBM),
         pltpu.with_memory_space_constraint(fresh_grads, pltpu.HBM),
+        fresh_peer,
         payload,
     )
 
-    fresh_pair = jnp.concatenate([to_core(fresh_send), fresh_keep], axis=1)
     at_end = section == jnp.where(core == 0, 0, sections - 1)
 
     blocks, gate_factor, activated = lax.optimization_barrier((blocks, gate_factor, activated))
 
-    def weight_grads():
-        hidden_all = [to_core(hidden, o) if o else hidden for o in range(replicas)]
+    def weight_grads(pre_held, dy_all):
         block = lane_block(part_width, 1024)
         blocks_each = part_width // block
         return pl.pallas_call(
@@ -247,9 +245,8 @@
                         lambda i, j, at: (at[0] ^ i, 0, 0, 0, at[1] * blocks_each + j),
                     )
                 ] * replicas
-                + [pl.BlockSpec((pair_rows, 2 * hidden_width), lambda i, j, at: (0, 0))] * (replicas * steps)
-                + [pl.BlockSpec((steps, pair_rows, hidden_width), lambda i, j, at: (0, 0, 0))] * replicas
-                + [pl.BlockSpec((pair_rows, block), lambda i, j, at: (0, at[1] * blocks_each + j))] * (replicas * steps),
+                + [pl.BlockSpec((steps, pair_rows, 3 * hidden_width), lambda i, j, at: (0, 0, 0))] * replicas
+                + [pl.BlockSpec((steps * pair_rows, block), lambda i, j, at: (0, at[1] * blocks_each + j))] * replicas,
                 out_specs=[
                     pl.BlockSpec((1, 1, block, 2 * hidden_width), lambda i, j, at: (at[0] ^ i, 0, j, 0)),
                     pl.BlockSpec((1, 1, hidden_width, block), lambda i, j, at: (at[0] ^ i, 0, 0, j)),
@@ -269,21 +266,23 @@
         )(
             which,
             *saved,
-            *[pre_all[k][o] for o in range(replicas) for k in range(steps)],
-            *hidden_all,
-            *[dy_all[k][o] for o in range(replicas) for k in range(steps)],
+            *[to_core(pre_held, o) if o else pre_held for o in range(replicas)],
+            *dy_all,
         )
 
     hand_offs = jnp.zeros((2, steps, shard_rows, width), F32)
-    dy_all, pre_all = [], []
+    hand_rows = steps * pair_rows
+    dy_held = jnp.zeros((hand_rows + (steps - 1) * shard_rows, width), BF16)
+    pre_held = jnp.zeros((steps, pair_rows, 3 * hidden_width), BF16).at[:, :, 2 * hidden_width:].set(hidden)
     for k in range(steps):
         dy = placed(blocks)
+        dy_held = dy_held.at[k * pair_rows:(k + 1) * pair_rows].set(dy)
+        if k + 1 == steps:
+            dy_all = [to_core(dy_held, o) if o else dy_held for o in range(replicas)]
         dh = jnp.einsum("rd,dh->rh", dy, w_down_dir, preferred_element_type=F32)
         pre_grad = jnp.concatenate([dh * gate_factor[k], dh * activated[k]], axis=1).astype(BF16)
+        pre_held = pre_held.at[k, :, :2 * hidden_width].set(pre_grad)
         part = jnp.einsum("rc,cd->rd", pre_grad, w_in_dir, preferred_element_type=F32).astype(BF16)
-        dy_all.append([to_core(dy, o) if o else dy for o in range(replicas)])
-        if k + 1 == steps:
-            part, dy_all[k] = lax.optimization_barrier((part, dy_all[k]))
         part = part.reshape(tensor_count, block_rows, width)
 
         def part_for(target):
@@ -293,27 +292,34 @@
         parts = []
         for s in range(1, tensor_count):
             parts.append(rotate(part_for(lax.rem(place + s, tensor_count)), s))
-        pre_all.append([to_core(pre_grad, o) if o else pre_grad for o in range(replicas)])
         if k + 1 == steps:
-            parts, grads = lax.optimization_barrier((parts, weight_grads()))
+            parts, grads = lax.optimization_barrier((parts, weight_grads(pre_held, dy_all)))
         summed = own_part.astype(F32)
         for x in parts:
             summed = summed + x.astype(F32)
         handed = incoming + summed
+        hand_offs = lax.dynamic_update_slice(hand_offs, handed[None, None, :shard_rows], (core, k, 0, 0))
         if k + 1 < steps:
             payload = jnp.where(at_end, fresh_pair[k], handed.astype(BF16))
             blocks = [
                 lax.ppermute(payload, AXES, ring_pairs(sections, tensor_count, replicas, s))
                 for s in range(tensor_count)
             ]
-        if k == 0:
-            other = theirs(entry) + to_core(summed[shard_rows:])
+            leaving = summed if k == 0 else handed
+            dy_held = dy_held.at[hand_rows + k * shard_rows:hand_rows + (k + 1) * shard_rows].set(
+                leaving[shard_rows:].astype(BF16)
+            )
+            incoming = blocks[0].astype(F32)
         else:
-            other = to_core(handed[shard_rows:])
-        if 0 < k < steps - 1:
-            blocks, other = lax.optimization_barrier((blocks, other))
-        hand_offs = hand_offs.at[:, k].set(by_direction(handed[:shard_rows], other))
-        incoming = blocks[0].astype(F32)
+            last = to_core(handed[shard_rows:])
+    for k in range(steps):
+        if k + 1 < steps:
+            start = hand_rows + k * shard_rows
+            arrived = dy_all[1][start:start + shard_rows].astype(F32)
+            arrived = arrived + theirs(entry) if k == 0 else arrived
+        else:
+            arrived = last
+        hand_offs = lax.dynamic_update_slice(hand_offs, arrived[None, None], (1 - core, k, 0, 0))
     return (hand_offs[:, :, None], *grads)
 
 

time: 69 us -> 65.6 us (0.951)
  starting transfers between devices: 30.6 us -> 26.7 us
    ppermute x8, waiting for transfers between devices: 7.35 us -> 10.4 us  [local(): lax.ppermute(payload, AXES, ring_pairs(sections, tensor_count, replicas, s))]
    ppermute x13 -> x6, starting transfers between devices: 4.48 us -> 1.72 us  [to_core(): return lax.ppermute(x, 'dp', [(i, i ^ offset) for i in range(replicas)])]
    ppermute x12, starting transfers between devices: 17.7 us -> 15.5 us  [rotate(): lax.ppermute(x, 'tensor', [(i, (i + shift) % tensor_count) for i in range...]
    ppermute x13 -> x6, waiting for transfers between devices: 3.08 us -> 1.26 us  [to_core(): return lax.ppermute(x, 'dp', [(i, i ^ offset) for i in range(replicas)])]
    ppermute x8, starting transfers between devices: 8.46 us -> 9.42 us  [local(): lax.ppermute(payload, AXES, ring_pairs(sections, tensor_count, replicas, s))]
  transfers between devices with their start and end apart: 33 -> 26, of which waited for: 14 -> 14; matrix products, arithmetic and copies ran while one was open for 8% -> 3% of each run, Pallas kernels for 15% -> 16%
where the time goes in v5:
time: 65.6 us; the launch traced here: 65.4 us
  starting transfers between devices  26.7 us (41%)
  waiting for transfers between devices  20.9 us (32%)
  Pallas kernels  10.4 us (16%)
  matrix products  3.58 us (5%)
  other arithmetic  1.67 us (3%)
  local copies, waits for them, and re-layouts  1.19 us (2%)
  between operations  0.98 us (1%)
    ppermute x12, starting transfers between devices, rotate(): lax.ppermute(x, 'tensor', [(i, (i + shift) % tensor_count) for i in range...  15.5 us
    ppermute x8, waiting for transfers between devices, local(): lax.ppermute(payload, AXES, ring_pairs(sections, tensor_count, replicas, s))  10.4 us
    ppermute x8, starting transfers between devices, local(): lax.ppermute(payload, AXES, ring_pairs(sections, tensor_count, replicas, s))  9.42 us
    ppermute x12, waiting for transfers between devices, rotate(): lax.ppermute(x, 'tensor', [(i, (i + shift) % tensor_count) for i in range...  9.21 us
    pallas_call x1, Pallas kernels, weight_grads(): pl.pallas_call(functools.partial(weight_grads_kernel, steps, replicas, te...  5.81 us
    pallas_call x1, Pallas kernels, local(): pl.pallas_call(functools.partial(factors_kernel, tensor_count), grid_spec...  4.63 us
    dot_general x3, matrix products, local(): jnp.einsum('rc,cd->rd', pre_grad, w_in_dir, preferred_element_type=F32)  2.25 us
    ppermute x6, starting transfers between devices, to_core(): return lax.ppermute(x, 'dp', [(i, i ^ offset) for i in range(replicas)])  1.72 us
  transfers between devices with their start and end apart: 26, of which 14 were waited for; matrix products, arithmetic and copies ran while one was open for 3% of the time, Pallas kernels for 16%

profile of v5, /device:TPU:0, one launch (start us, length us, event | category | flops | bytes accessed | tf_op | source)
XLA Modules:
  0.0 65.4 jit_solution(3482045422119809132)
XLA Ops:
  0.6 0.5 collective-permute-start
  1.2 0.4 collective-permute-start.4
  1.7 1.0 %select_bitcast_fusion = f32[8,3584]{1,0:T(8,128)S(1)} fusion(f32[2,1,8,3584]{3,2,1,0:T(8,128)} %param.23, pred[]{:T(512)S(6)} %eq.28), kind=kLoop, calls=%fused_computation.56 | loop fusion | flops 28672 | bytes 344065 | tf_op jit(solution)/shard_map/jit(_where)/select_n | solution.py:145
  2.7 3.7 %collective-permute-start.3 = (bf16[16,3584]{1,0:T(8,128)(2,1)S(1)}, bf16[16,3584]{1,0:T(8,128)(2,1)S(1)}, u32[]{:S(2)}, u32[]{:S(2)}) collective-permute-start(bf16[16,3584]{1,0:T(8,128)(2,1)S(1)} %fusion.9._), channel_id=1, source_target_pairs={{0,6},{2,0},{4,2},{6,4},{1,7},{3,1},{5,3},{7,5},{8,14},{10,8},{12,... | collective-permute-start | bytes 344072 | tf_op jit(solution)/shard_map/ppermute | solution.py:160
  6.4 0.5 collective-permute-start.2
  6.9 0.6 collective-permute-start.1
  7.6 4.6 %factors.1 = (f32[3,64,256]{2,1,0:T(8,128)S(1)}, f32[3,64,256]{2,1,0:T(8,128)S(1)}, bf16[3,64,256]{2,1,0:T(8,128)(2,1)S(1)}, bf16[2,16,3584]{2,1,0:T(8,128)(2,1)...) custom-call(s32[2]{0:T(128)S(1)} %pad_add_fusion.at._, bf16[2,3,1,32,3584]{4,3,2,1,0:T(8,128)(2,1)} %refs_0_.1, ...), custom_call_target="tpu_custom_call" | custom-call | tf_op jit(solution)/shard_map/factors/pallas_call | solution.py:181
  12.2 1.7 %collective-permute-done.2 = bf16[16,3584]{1,0:T(8,128)(2,1)S(1)} collective-permute-done((bf16[16,3584]{1,0:T(8,128)(2,1)S(1)}, bf16[16,3584]{1,0:T(8,128)(2,1)S(1)}, u32[]{:S(2)}, u32[]{:S(2)}) %collective-permute-start.2) | collective-permute-done | bytes 114720 | tf_op jit(solution)/shard_map/ppermute | solution.py:160
  14.0 0.4 fusion.32
  14.4 0.8 %convolution_convert_fusion.2 = bf16[64,3584]{1,0:T(8,128)(2,1)S(1)} fusion(bf16[512,3584]{1,0:T(8,128)(2,1)S(1)} %get-tuple-element.139, bf16[64,256]{1,0:T(8,128)(2,1)S(1)} %get-tuple-element.181, bf16[64,256]{1,0:T(8,128)(2,1)S(1)} %get-tuple-element.180), kind=kOutput, calls=%fused_computation.2 | convolution fusion | flops 235241472 | bytes 4194304 | tf_op jit(solution)/shard_map/rc,cd->rd/dot_general | solution.py:285
  15.2 0.7 %collective-permute-start.6 = (bf16[16,3584]{1,0:T(8,128)(2,1)S(1)}, bf16[16,3584]{1,0:T(8,128)(2,1)S(1)}, u32[]{:S(2)}, u32[]{:S(2)}) collective-permute-start(bf16[16,3584]{1,0:T(8,128)(2,1)S(1)} %get-tuple-element.169), channel_id=1, source_target_pairs={{0,2},{2,4},{4,6},{6,0},{1,3},{3,5},{5,7},{7,1},{8,10},{10,12},{12... | collective-permute-start | bytes 344072 | tf_op jit(solution)/shard_map/ppermute | solution.py:160
  16.0 2.2 %collective-permute-start.8 = (bf16[16,3584]{1,0:T(8,128)(2,1)S(1)}, bf16[16,3584]{1,0:T(8,128)(2,1)S(1)}, u32[]{:S(2)}, u32[]{:S(2)}) collective-permute-start(bf16[16,3584]{1,0:T(8,128)(2,1)S(1)} %get-tuple-element.170), channel_id=1, source_target_pairs={{0,6},{2,0},{4,2},{6,4},{1,7},{3,1},{5,3},{7,5},{8,14},{10,8},{12,... | collective-permute-start | bytes 344072 | tf_op jit(solution)/shard_map/ppermute | solution.py:160
  18.2 0.5 collective-permute-start.7
  18.8 0.1 scatter.36
  18.9 2.9 %collective-permute-done.6 = bf16[16,3584]{1,0:T(8,128)(2,1)S(1)} collective-permute-done((bf16[16,3584]{1,0:T(8,128)(2,1)S(1)}, bf16[16,3584]{1,0:T(8,128)(2,1)S(1)}, u32[]{:S(2)}, u32[]{:S(2)}) %collective-permute-start.6) | collective-permute-done | bytes 114720 | tf_op jit(solution)/shard_map/ppermute | solution.py:160
  21.8 1.4 %collective-permute-done.7 = bf16[16,3584]{1,0:T(8,128)(2,1)S(1)} collective-permute-done((bf16[16,3584]{1,0:T(8,128)(2,1)S(1)}, bf16[16,3584]{1,0:T(8,128)(2,1)S(1)}, u32[]{:S(2)}, u32[]{:S(2)}) %collective-permute-start.7) | collective-permute-done | bytes 114720 | tf_op jit(solution)/shard_map/ppermute | solution.py:160
  23.1 0.1 bitcast_select_fusion.1
  23.3 1.0 %collective-permute-start.11 = (bf16[16,3584]{1,0:T(8,128)(2,1)S(1)}, bf16[16,3584]{1,0:T(8,128)(2,1)S(1)}, u32[]{:S(2)}, u32[]{:S(2)}) collective-permute-start(bf16[16,3584]{1,0:T(8,128)(2,1)S(1)} %get-tuple-element.152), channel_id=1, source_target_pairs={{0,5},{1,13},{2,7},{3,15},{4,1},{5,9},{6,3},{7,11},{8,4},{9,21},{1... | collective-permute-start | bytes 344072 | tf_op jit(solution)/shard_map/ppermute | solution.py:305
  24.3 1.9 %collective-permute-start.10 = (bf16[16,3584]{1,0:T(8,128)(2,1)S(1)}, bf16[16,3584]{1,0:T(8,128)(2,1)S(1)}, u32[]{:S(2)}, u32[]{:S(2)}) collective-permute-start(bf16[16,3584]{1,0:T(8,128)(2,1)S(1)} %get-tuple-element.152), channel_id=1, source_target_pairs={{0,7},{1,15},{2,1},{3,9},{4,3},{5,11},{6,5},{7,13},{8,6},{9,23},{1... | collective-permute-start | bytes 344072 | tf_op jit(solution)/shard_map/ppermute | solution.py:305
  26.2 1.1 %collective-permute-start.9 = (bf16[16,3584]{1,0:T(8,128)(2,1)S(1)}, bf16[16,3584]{1,0:T(8,128)(2,1)S(1)}, u32[]{:S(2)}, u32[]{:S(2)}) collective-permute-start(bf16[16,3584]{1,0:T(8,128)(2,1)S(1)} %get-tuple-element.152), channel_id=1, source_target_pairs={{0,1},{1,9},{2,3},{3,11},{4,5},{5,13},{6,7},{7,15},{8,0},{9,17},{1... | collective-permute-start | bytes 344072 | tf_op jit(solution)/shard_map/ppermute | solution.py:305
  27.4 3.3 %collective-permute-done.12 = bf16[16,3584]{1,0:T(8,128)(2,1)S(1)} collective-permute-done((bf16[16,3584]{1,0:T(8,128)(2,1)S(1)}, bf16[16,3584]{1,0:T(8,128)(2,1)S(1)}, u32[]{:S(2)}, u32[]{:S(2)}) %collective-permute-start.12) | collective-permute-done | bytes 114720 | tf_op jit(solution)/shard_map/ppermute | solution.py:305
  30.7 0.5 collective-permute-done.11
  31.3 1.4 %collective-permute-done.9 = bf16[16,3584]{1,0:T(8,128)(2,1)S(1)} collective-permute-done((bf16[16,3584]{1,0:T(8,128)(2,1)S(1)}, bf16[16,3584]{1,0:T(8,128)(2,1)S(1)}, u32[]{:S(2)}, u32[]{:S(2)}) %collective-permute-start.9) | collective-permute-done | bytes 114720 | tf_op jit(solution)/shard_map/ppermute | solution.py:305
  32.8 0.4 fusion.30
  33.2 0.8 %convolution_convert_fusion.1 = bf16[64,3584]{1,0:T(8,128)(2,1)S(1)} fusion(bf16[512,3584]{1,0:T(8,128)(2,1)S(1)} %get-tuple-element.139, bf16[64,256]{1,0:T(8,128)(2,1)S(1)} %get-tuple-element.179, bf16[64,256]{1,0:T(8,128)(2,1)S(1)} %get-tuple-element.178), kind=kOutput, calls=%fused_computation.1 | convolution fusion | flops 235241472 | bytes 4194304 | tf_op jit(solution)/shard_map/rc,cd->rd/dot_general | solution.py:285
  34.0 1.4 %collective-permute-start.13 = (bf16[16,3584]{1,0:T(8,128)(2,1)S(1)}, bf16[16,3584]{1,0:T(8,128)(2,1)S(1)}, u32[]{:S(2)}, u32[]{:S(2)}) collective-permute-start(bf16[16,3584]{1,0:T(8,128)(2,1)S(1)} %get-tuple-element.162), channel_id=1, source_target_pairs={{0,2},{2,4},{4,6},{6,0},{1,3},{3,5},{5,7},{7,1},{8,10},{10,12},{12... | collective-permute-start | bytes 344072 | tf_op jit(solution)/shard_map/ppermute | solution.py:160
  35.4 1.6 %collective-permute-start.15 = (bf16[16,3584]{1,0:T(8,128)(2,1)S(1)}, bf16[16,3584]{1,0:T(8,128)(2,1)S(1)}, u32[]{:S(2)}, u32[]{:S(2)}) collective-permute-start(bf16[16,3584]{1,0:T(8,128)(2,1)S(1)} %get-tuple-element.163), channel_id=1, source_target_pairs={{0,6},{2,0},{4,2},{6,4},{1,7},{3,1},{5,3},{7,5},{8,14},{10,8},{12,... | collective-permute-start | bytes 344072 | tf_op jit(solution)/shard_map/ppermute | solution.py:160
  37.0 1.5 %collective-permute-start.14 = (bf16[16,3584]{1,0:T(8,128)(2,1)S(1)}, bf16[16,3584]{1,0:T(8,128)(2,1)S(1)}, u32[]{:S(2)}, u32[]{:S(2)}) collective-permute-start(bf16[16,3584]{1,0:T(8,128)(2,1)S(1)} %get-tuple-element.164), channel_id=1, source_target_pairs={{0,4},{2,6},{4,0},{6,2},{1,5},{3,7},{5,1},{7,3},{8,12},{10,14},{12... | collective-permute-start | bytes 344072 | tf_op jit(solution)/shard_map/ppermute | solution.py:160
  38.5 1.4 %collective-permute-done.13 = bf16[16,3584]{1,0:T(8,128)(2,1)S(1)} collective-permute-done((bf16[16,3584]{1,0:T(8,128)(2,1)S(1)}, bf16[16,3584]{1,0:T(8,128)(2,1)S(1)}, u32[]{:S(2)}, u32[]{:S(2)}) %collective-permute-start.13) | collective-permute-done | bytes 114720 | tf_op jit(solution)/shard_map/ppermute | solution.py:160
  39.9 1.4 %collective-permute-done.15 = bf16[16,3584]{1,0:T(8,128)(2,1)S(1)} collective-permute-done((bf16[16,3584]{1,0:T(8,128)(2,1)S(1)}, bf16[16,3584]{1,0:T(8,128)(2,1)S(1)}, u32[]{:S(2)}, u32[]{:S(2)}) %collective-permute-start.15) | collective-permute-done | bytes 114720 | tf_op jit(solution)/shard_map/ppermute | solution.py:160
  41.4 0.4 collective-permute-done.14
  41.8 0.1 bitcast_select_fusion
  41.9 1.2 %collective-permute-start.19 = (bf16[16,3584]{1,0:T(8,128)(2,1)S(1)}, bf16[16,3584]{1,0:T(8,128)(2,1)S(1)}, u32[]{:S(2)}, u32[]{:S(2)}) collective-permute-start(bf16[16,3584]{1,0:T(8,128)(2,1)S(1)} %get-tuple-element.149), channel_id=1, source_target_pairs={{0,3},{1,11},{2,5},{3,13},{4,7},{5,15},{6,1},{7,9},{8,2},{9,19},{1... | collective-permute-start | bytes 344072 | tf_op jit(solution)/shard_map/ppermute | solution.py:305
  43.1 3.8 %collective-permute-start.17 = (bf16[16,3584]{1,0:T(8,128)(2,1)S(1)}, bf16[16,3584]{1,0:T(8,128)(2,1)S(1)}, u32[]{:S(2)}, u32[]{:S(2)}) collective-permute-start(bf16[16,3584]{1,0:T(8,128)(2,1)S(1)} %get-tuple-element.149), channel_id=1, source_target_pairs={{0,7},{1,15},{2,1},{3,9},{4,3},{5,11},{6,5},{7,13},{8,6},{9,23},{1... | collective-permute-start | bytes 344072 | tf_op jit(solution)/shard_map/ppermute | solution.py:305
  46.8 0.4 collective-permute-start.16
  47.3 1.4 %collective-permute-done.19 = bf16[16,3584]{1,0:T(8,128)(2,1)S(1)} collective-permute-done((bf16[16,3584]{1,0:T(8,128)(2,1)S(1)}, bf16[16,3584]{1,0:T(8,128)(2,1)S(1)}, u32[]{:S(2)}, u32[]{:S(2)}) %collective-permute-start.19) | collective-permute-done | bytes 114720 | tf_op jit(solution)/shard_map/ppermute | solution.py:305
  48.7 1.4 %collective-permute-done.18 = bf16[16,3584]{1,0:T(8,128)(2,1)S(1)} collective-permute-done((bf16[16,3584]{1,0:T(8,128)(2,1)S(1)}, bf16[16,3584]{1,0:T(8,128)(2,1)S(1)}, u32[]{:S(2)}, u32[]{:S(2)}) %collective-permute-start.18) | collective-permute-done | bytes 114720 | tf_op jit(solution)/shard_map/ppermute | solution.py:305
  50.1 1.0 %collective-permute-done.17 = bf16[16,3584]{1,0:T(8,128)(2,1)S(1)} collective-permute-done((bf16[16,3584]{1,0:T(8,128)(2,1)S(1)}, bf16[16,3584]{1,0:T(8,128)(2,1)S(1)}, u32[]{:S(2)}, u32[]{:S(2)}) %collective-permute-start.17) | collective-permute-done | bytes 114720 | tf_op jit(solution)/shard_map/ppermute | solution.py:305
  51.1 1.3 %collective-permute-done.16 = bf16[16,3584]{1,0:T(8,128)(2,1)S(1)} collective-permute-done((bf16[16,3584]{1,0:T(8,128)(2,1)S(1)}, bf16[16,3584]{1,0:T(8,128)(2,1)S(1)}, u32[]{:S(2)}, u32[]{:S(2)}) %collective-permute-start.16) | collective-permute-done | bytes 114720 | tf_op jit(solution)/shard_map/ppermute | solution.py:305
  52.4 0.4 fusion.28
  53.0 0.7 %convolution_convert_fusion = bf16[64,3584]{1,0:T(8,128)(2,1)S(1)} fusion(bf16[512,3584]{1,0:T(8,128)(2,1)S(1)} %get-tuple-element.139, bf16[64,256]{1,0:T(8,128)(2,1)S(1)} %get-tuple-element.177, bf16[64,256]{1,0:T(8,128)(2,1)S(1)} %get-tuple-element.176), kind=kOutput, calls=%fused_computation | convolution fusion | flops 235241472 | bytes 4194304 | tf_op jit(solution)/shard_map/rc,cd->rd/dot_general | solution.py:285
  53.8 0.6 collective-permute-start.23
  54.4 1.3 %collective-permute-start.22 = (bf16[16,3584]{1,0:T(8,128)(2,1)S(1)}, bf16[16,3584]{1,0:T(8,128)(2,1)S(1)}, u32[]{:S(2)}, u32[]{:S(2)}) collective-permute-start(bf16[16,3584]{1,0:T(8,128)(2,1)S(1)} %get-tuple-element.155), channel_id=1, source_target_pairs={{0,6},{2,0},{4,2},{6,4},{1,7},{3,1},{5,3},{7,5},{8,14},{10,8},{12,... | collective-permute-start | bytes 344072 | tf_op jit(solution)/shard_map/ppermute | solution.py:160
  55.6 0.8 %collective-permute-start.21 = (bf16[16,3584]{1,0:T(8,128)(2,1)S(1)}, bf16[16,3584]{1,0:T(8,128)(2,1)S(1)}, u32[]{:S(2)}, u32[]{:S(2)}) collective-permute-start(bf16[16,3584]{1,0:T(8,128)(2,1)S(1)} %get-tuple-element.156), channel_id=1, source_target_pairs={{0,4},{2,6},{4,0},{6,2},{1,5},{3,7},{5,1},{7,3},{8,12},{10,14},{12... | collective-permute-start | bytes 344072 | tf_op jit(solution)/shard_map/ppermute | solution.py:160
  56.4 0.8 %collective-permute-start.20 = (bf16[16,3584]{1,0:T(8,128)(2,1)S(1)}, bf16[16,3584]{1,0:T(8,128)(2,1)S(1)}, u32[]{:S(2)}, u32[]{:S(2)}) collective-permute-start(bf16[16,3584]{1,0:T(8,128)(2,1)S(1)} %get-tuple-element.157), channel_id=1, source_target_pairs={{0,2},{2,4},{4,6},{6,0},{1,3},{3,5},{5,7},{7,1},{8,10},{10,12},{12... | collective-permute-start | bytes 344072 | tf_op jit(solution)/shard_map/ppermute | solution.py:160
  57.2 5.8 %weight_grads.1 = (f32[2,1,1792,512]{3,2,1,0:T(8,128)}, f32[2,1,256,1792]{3,2,1,0:T(8,128)}) custom-call(s32[2]{0:T(128)S(1)} %pad_add_fusion.at._, bf16[2,3,1,32,3584]{4,3,2,1,0:T(8,128)(2,1)S(1)} %copy-done, bf16[2,3,1,32,3584]{4,3,2,1,0:T(8,128)(2,1)S(1)} %collective-permute-done.4.peer_ref.refs_1_, ...), custom_call_target="tpu_custom_call" | custom-call | tf_op jit(solution)/shard_map/weight_grads/pallas_call | solution.py:237
  63.3 1.2 %collective-permute-done.25 = f32[8,3584]{1,0:T(8,128)S(1)} collective-permute-done((f32[8,3584]{1,0:T(8,128)S(1)}, f32[8,3584]{1,0:T(8,128)S(1)}, u32[]{:S(2)}, u32[]{:S(2)}) %collective-permute-start.25) | collective-permute-done | bytes 114720 | tf_op jit(solution)/shard_map/ppermute | solution.py:157
  64.6 0.8 %copy-done.2 = f32[2,3,1,8,3584]{4,3,2,1,0:T(8,128)} copy-done((f32[2,3,1,8,3584]{4,3,2,1,0:T(8,128)}, f32[2,3,1,8,3584]{4,3,2,1,0:T(8,128)S(1)}, u32[]{:S(2)}) %copy-start.2) | copy-done | bytes 688152
  (49 shorter events, 1.1 us)
Async XLA Ops:
  0.6 2.0 %collective-permute-start = (f32[2,1,8,3584]{3,2,1,0:T(8,128)}, f32[2,1,8,3584]{3,2,1,0:T(8,128)S(1)}, u32[]{:S(2)}, u32[]{:S(2)}) collective-permute-start(f32[2,1,8,3584]{3,2,1,0:T(8,128)} %param.23), channel_id=1, source_target_pairs={{0,1},{1,0},{2,3},{3,2},{4,5},{5,4},{6,7},{7,6},{8,9},{9,8},{10,11... | collective-permute-start | bytes 688136 | tf_op jit(solution)/shard_map/ppermute | solution.py:157
  1.1 6.4 %collective-permute-start.5 = (f32[2,2,8,3584]{3,2,1,0:T(8,128)}, f32[2,2,8,3584]{3,2,1,0:T(8,128)S(1)}, u32[]{:S(2)}, u32[]{:S(2)}) collective-permute-start(f32[2,2,8,3584]{3,2,1,0:T(8,128)} %fresh_ref.1), channel_id=1, source_target_pairs={{0,1},{1,0},{2,3},{3,2},{4,5},{5,4},{6,7},{7,6},{8,9},{9,8},{10,11... | collective-permute-start | bytes 1376264 | tf_op jit(solution)/shard_map/ppermute | solution.py:157
  1.2 6.3 %collective-permute-start.4 = (bf16[2,3,1,32,3584]{4,3,2,1,0:T(8,128)(2,1)}, bf16[2,3,1,32,3584]{4,3,2,1,0:T(8,128)(2,1)S(1)}, u32[]{:S(2)}, u32[]{:S(2)}) collective-permute-start(bf16[2,3,1,32,3584]{4,3,2,1,0:T(8,128)(2,1)} %refs_0_.1), channel_id=1, source_target_pairs={{0,1},{1,0},{2,3},{3,2},{4,5},{5,4},{6,7},{7,6},{8,9},{9,8},{10,11... | collective-permute-start | bytes 4128776 | tf_op jit(solution)/shard_map/ppermute | solution.py:157
  2.7 9.5 %collective-permute-start.3 = (bf16[16,3584]{1,0:T(8,128)(2,1)S(1)}, bf16[16,3584]{1,0:T(8,128)(2,1)S(1)}, u32[]{:S(2)}, u32[]{:S(2)}) collective-permute-start(bf16[16,3584]{1,0:T(8,128)(2,1)S(1)} %fusion.9._), channel_id=1, source_target_pairs={{0,6},{2,0},{4,2},{6,4},{1,7},{3,1},{5,3},{7,5},{8,14},{10,8},{12,... | collective-permute-start | bytes 344072 | tf_op jit(solution)/shard_map/ppermute | solution.py:160
  6.4 7.6 %collective-permute-start.2 = (bf16[16,3584]{1,0:T(8,128)(2,1)S(1)}, bf16[16,3584]{1,0:T(8,128)(2,1)S(1)}, u32[]{:S(2)}, u32[]{:S(2)}) collective-permute-start(bf16[16,3584]{1,0:T(8,128)(2,1)S(1)} %fusion.9._), channel_id=1, source_target_pairs={{0,4},{2,6},{4,0},{6,2},{1,5},{3,7},{5,1},{7,3},{8,12},{10,14},{12... | collective-permute-start | bytes 344072 | tf_op jit(solution)/shard_map/ppermute | solution.py:160
  6.9 7.0 %collective-permute-start.1 = (bf16[16,3584]{1,0:T(8,128)(2,1)S(1)}, bf16[16,3584]{1,0:T(8,128)(2,1)S(1)}, u32[]{:S(2)}, u32[]{:S(2)}) collective-permute-start(bf16[16,3584]{1,0:T(8,128)(2,1)S(1)} %fusion.9._), channel_id=1, source_target_pairs={{0,2},{2,4},{4,6},{6,0},{1,3},{3,5},{5,7},{7,1},{8,10},{10,12},{12... | collective-permute-start | bytes 344072 | tf_op jit(solution)/shard_map/ppermute | solution.py:160
  15.2 6.5 %collective-permute-start.6 = (bf16[16,3584]{1,0:T(8,128)(2,1)S(1)}, bf16[16,3584]{1,0:T(8,128)(2,1)S(1)}, u32[]{:S(2)}, u32[]{:S(2)}) collective-permute-start(bf16[16,3584]{1,0:T(8,128)(2,1)S(1)} %get-tuple-element.169), channel_id=1, source_target_pairs={{0,2},{2,4},{4,6},{6,0},{1,3},{3,5},{5,7},{7,1},{8,10},{10,12},{12... | collective-permute-start | bytes 344072 | tf_op jit(solution)/shard_map/ppermute | solution.py:160
  16.0 5.8 %collective-permute-start.8 = (bf16[16,3584]{1,0:T(8,128)(2,1)S(1)}, bf16[16,3584]{1,0:T(8,128)(2,1)S(1)}, u32[]{:S(2)}, u32[]{:S(2)}) collective-permute-start(bf16[16,3584]{1,0:T(8,128)(2,1)S(1)} %get-tuple-element.170), channel_id=1, source_target_pairs={{0,6},{2,0},{4,2},{6,4},{1,7},{3,1},{5,3},{7,5},{8,14},{10,8},{12,... | collective-permute-start | bytes 344072 | tf_op jit(solution)/shard_map/ppermute | solution.py:160
  18.2 4.9 %collective-permute-start.7 = (bf16[16,3584]{1,0:T(8,128)(2,1)S(1)}, bf16[16,3584]{1,0:T(8,128)(2,1)S(1)}, u32[]{:S(2)}, u32[]{:S(2)}) collective-permute-start(bf16[16,3584]{1,0:T(8,128)(2,1)S(1)} %get-tuple-element.171), channel_id=1, source_target_pairs={{0,4},{2,6},{4,0},{6,2},{1,5},{3,7},{5,1},{7,3},{8,12},{10,14},{12... | collective-permute-start | bytes 344072 | tf_op jit(solution)/shard_map/ppermute | solution.py:160
  23.2 7.4 %collective-permute-start.12 = (bf16[16,3584]{1,0:T(8,128)(2,1)S(1)}, bf16[16,3584]{1,0:T(8,128)(2,1)S(1)}, u32[]{:S(2)}, u32[]{:S(2)}) collective-permute-start(bf16[16,3584]{1,0:T(8,128)(2,1)S(1)} %get-tuple-element.152), channel_id=1, source_target_pairs={{0,3},{1,11},{2,5},{3,13},{4,7},{5,15},{6,1},{7,9},{8,2},{9,19},{1... | collective-permute-start | bytes 344072 | tf_op jit(solution)/shard_map/ppermute | solution.py:305
  23.3 7.9 %collective-permute-start.11 = (bf16[16,3584]{1,0:T(8,128)(2,1)S(1)}, bf16[16,3584]{1,0:T(8,128)(2,1)S(1)}, u32[]{:S(2)}, u32[]{:S(2)}) collective-permute-start(bf16[16,3584]{1,0:T(8,128)(2,1)S(1)} %get-tuple-element.152), channel_id=1, source_target_pairs={{0,5},{1,13},{2,7},{3,15},{4,1},{5,9},{6,3},{7,11},{8,4},{9,21},{1... | collective-permute-start | bytes 344072 | tf_op jit(solution)/shard_map/ppermute | solution.py:305
  24.3 7.0 %collective-permute-start.10 = (bf16[16,3584]{1,0:T(8,128)(2,1)S(1)}, bf16[16,3584]{1,0:T(8,128)(2,1)S(1)}, u32[]{:S(2)}, u32[]{:S(2)}) collective-permute-start(bf16[16,3584]{1,0:T(8,128)(2,1)S(1)} %get-tuple-element.152), channel_id=1, source_target_pairs={{0,7},{1,15},{2,1},{3,9},{4,3},{5,11},{6,5},{7,13},{8,6},{9,23},{1... | collective-permute-start | bytes 344072 | tf_op jit(solution)/shard_map/ppermute | solution.py:305
  26.2 6.5 %collective-permute-start.9 = (bf16[16,3584]{1,0:T(8,128)(2,1)S(1)}, bf16[16,3584]{1,0:T(8,128)(2,1)S(1)}, u32[]{:S(2)}, u32[]{:S(2)}) collective-permute-start(bf16[16,3584]{1,0:T(8,128)(2,1)S(1)} %get-tuple-element.152), channel_id=1, source_target_pairs={{0,1},{1,9},{2,3},{3,11},{4,5},{5,13},{6,7},{7,15},{8,0},{9,17},{1... | collective-permute-start | bytes 344072 | tf_op jit(solution)/shard_map/ppermute | solution.py:305
  34.0 5.9 %collective-permute-start.13 = (bf16[16,3584]{1,0:T(8,128)(2,1)S(1)}, bf16[16,3584]{1,0:T(8,128)(2,1)S(1)}, u32[]{:S(2)}, u32[]{:S(2)}) collective-permute-start(bf16[16,3584]{1,0:T(8,128)(2,1)S(1)} %get-tuple-element.162), channel_id=1, source_target_pairs={{0,2},{2,4},{4,6},{6,0},{1,3},{3,5},{5,7},{7,1},{8,10},{10,12},{12... | collective-permute-start | bytes 344072 | tf_op jit(solution)/shard_map/ppermute | solution.py:160
  35.4 6.0 %collective-permute-start.15 = (bf16[16,3584]{1,0:T(8,128)(2,1)S(1)}, bf16[16,3584]{1,0:T(8,128)(2,1)S(1)}, u32[]{:S(2)}, u32[]{:S(2)}) collective-permute-start(bf16[16,3584]{1,0:T(8,128)(2,1)S(1)} %get-tuple-element.163), channel_id=1, source_target_pairs={{0,6},{2,0},{4,2},{6,4},{1,7},{3,1},{5,3},{7,5},{8,14},{10,8},{12,... | collective-permute-start | bytes 344072 | tf_op jit(solution)/shard_map/ppermute | solution.py:160
  37.0 4.8 %collective-permute-start.14 = (bf16[16,3584]{1,0:T(8,128)(2,1)S(1)}, bf16[16,3584]{1,0:T(8,128)(2,1)S(1)}, u32[]{:S(2)}, u32[]{:S(2)}) collective-permute-start(bf16[16,3584]{1,0:T(8,128)(2,1)S(1)} %get-tuple-element.164), channel_id=1, source_target_pairs={{0,4},{2,6},{4,0},{6,2},{1,5},{3,7},{5,1},{7,3},{8,12},{10,14},{12... | collective-permute-start | bytes 344072 | tf_op jit(solution)/shard_map/ppermute | solution.py:160
  41.9 6.8 %collective-permute-start.19 = (bf16[16,3584]{1,0:T(8,128)(2,1)S(1)}, bf16[16,3584]{1,0:T(8,128)(2,1)S(1)}, u32[]{:S(2)}, u32[]{:S(2)}) collective-permute-start(bf16[16,3584]{1,0:T(8,128)(2,1)S(1)} %get-tuple-element.149), channel_id=1, source_target_pairs={{0,3},{1,11},{2,5},{3,13},{4,7},{5,15},{6,1},{7,9},{8,2},{9,19},{1... | collective-permute-start | bytes 344072 | tf_op jit(solution)/shard_map/ppermute | solution.py:305
  43.1 7.0 %collective-permute-start.18 = (bf16[16,3584]{1,0:T(8,128)(2,1)S(1)}, bf16[16,3584]{1,0:T(8,128)(2,1)S(1)}, u32[]{:S(2)}, u32[]{:S(2)}) collective-permute-start(bf16[16,3584]{1,0:T(8,128)(2,1)S(1)} %get-tuple-element.149), channel_id=1, source_target_pairs={{0,5},{1,13},{2,7},{3,15},{4,1},{5,9},{6,3},{7,11},{8,4},{9,21},{1... | collective-permute-start | bytes 344072 | tf_op jit(solution)/shard_map/ppermute | solution.py:305
  43.1 8.0 %collective-permute-start.17 = (bf16[16,3584]{1,0:T(8,128)(2,1)S(1)}, bf16[16,3584]{1,0:T(8,128)(2,1)S(1)}, u32[]{:S(2)}, u32[]{:S(2)}) collective-permute-start(bf16[16,3584]{1,0:T(8,128)(2,1)S(1)} %get-tuple-element.149), channel_id=1, source_target_pairs={{0,7},{1,15},{2,1},{3,9},{4,3},{5,11},{6,5},{7,13},{8,6},{9,23},{1... | collective-permute-start | bytes 344072 | tf_op jit(solution)/shard_map/ppermute | solution.py:305
  46.8 5.6 %collective-permute-start.16 = (bf16[16,3584]{1,0:T(8,128)(2,1)S(1)}, bf16[16,3584]{1,0:T(8,128)(2,1)S(1)}, u32[]{:S(2)}, u32[]{:S(2)}) collective-permute-start(bf16[16,3584]{1,0:T(8,128)(2,1)S(1)} %get-tuple-element.149), channel_id=1, source_target_pairs={{0,1},{1,9},{2,3},{3,11},{4,5},{5,13},{6,7},{7,15},{8,0},{9,17},{1... | collective-permute-start | bytes 344072 | tf_op jit(solution)/shard_map/ppermute | solution.py:305
  52.9 4.3 %collective-permute-start.24 = (bf16[208,3584]{1,0:T(8,128)(2,1)S(1)}, bf16[208,3584]{1,0:T(8,128)(2,1)S(1)}, u32[]{:S(2)}, u32[]{:S(2)}) collective-permute-start(bf16[208,3584]{1,0:T(8,128)(2,1)S(1)} %fusion.14.refs_4_), channel_id=1, source_target_pairs={{0,1},{1,0},{2,3},{3,2},{4,5},{5,4},{6,7},{7,6},{8,9},{9,8},{10,11... | collective-permute-start | bytes 4472840 | tf_op jit(solution)/shard_map/ppermute | solution.py:157
  53.0 4.2 %copy-start = (bf16[2,3,1,32,3584]{4,3,2,1,0:T(8,128)(2,1)S(1)}, bf16[2,3,1,32,3584]{4,3,2,1,0:T(8,128)(2,1)}, u32[]{:S(2)}) copy-start(bf16[2,3,1,32,3584]{4,3,2,1,0:T(8,128)(2,1)} %refs_0_.1) | copy-start | bytes 4128772
  53.8 3.4 %collective-permute-start.23 = (bf16[3,64,768]{2,1,0:T(8,128)(2,1)S(1)}, bf16[3,64,768]{2,1,0:T(8,128)(2,1)S(1)}, u32[]{:S(2)}, u32[]{:S(2)}) collective-permute-start(bf16[3,64,768]{2,1,0:T(8,128)(2,1)S(1)} %maximum_dynamic-update-slice_fusion.2.refs_2_), channel_id=1, source_target_pairs={{0,1},{1,0},{2,3},{3,2},{4,5},{5,4},{6,7},{7,6},{8,9},{9,8},{10,11... | collective-permute-start | bytes 884744 | tf_op jit(solution)/shard_map/ppermute | solution.py:157
  54.4 8.7 %collective-permute-start.22 = (bf16[16,3584]{1,0:T(8,128)(2,1)S(1)}, bf16[16,3584]{1,0:T(8,128)(2,1)S(1)}, u32[]{:S(2)}, u32[]{:S(2)}) collective-permute-start(bf16[16,3584]{1,0:T(8,128)(2,1)S(1)} %get-tuple-element.155), channel_id=1, source_target_pairs={{0,6},{2,0},{4,2},{6,4},{1,7},{3,1},{5,3},{7,5},{8,14},{10,8},{12,... | collective-permute-start | bytes 344072 | tf_op jit(solution)/shard_map/ppermute | solution.py:160
  55.6 7.4 %collective-permute-start.21 = (bf16[16,3584]{1,0:T(8,128)(2,1)S(1)}, bf16[16,3584]{1,0:T(8,128)(2,1)S(1)}, u32[]{:S(2)}, u32[]{:S(2)}) collective-permute-start(bf16[16,3584]{1,0:T(8,128)(2,1)S(1)} %get-tuple-element.156), channel_id=1, source_target_pairs={{0,4},{2,6},{4,0},{6,2},{1,5},{3,7},{5,1},{7,3},{8,12},{10,14},{12... | collective-permute-start | bytes 344072 | tf_op jit(solution)/shard_map/ppermute | solution.py:160
  56.4 6.7 %collective-permute-start.20 = (bf16[16,3584]{1,0:T(8,128)(2,1)S(1)}, bf16[16,3584]{1,0:T(8,128)(2,1)S(1)}, u32[]{:S(2)}, u32[]{:S(2)}) collective-permute-start(bf16[16,3584]{1,0:T(8,128)(2,1)S(1)} %get-tuple-element.157), channel_id=1, source_target_pairs={{0,2},{2,4},{4,6},{6,0},{1,3},{3,5},{5,7},{7,1},{8,10},{10,12},{12... | collective-permute-start | bytes 344072 | tf_op jit(solution)/shard_map/ppermute | solution.py:160
  57.2 6.1 %copy-start.1 = (f32[2,1,8,3584]{3,2,1,0:T(8,128)S(1)}, f32[2,1,8,3584]{3,2,1,0:T(8,128)}, u32[]{:S(2)}) copy-start(f32[2,1,8,3584]{3,2,1,0:T(8,128)} %param.23) | copy-start | bytes 688132
  63.2 1.4 %collective-permute-start.25 = (f32[8,3584]{1,0:T(8,128)S(1)}, f32[8,3584]{1,0:T(8,128)S(1)}, u32[]{:S(2)}, u32[]{:S(2)}) collective-permute-start(f32[8,3584]{1,0:T(8,128)S(1)} %slice.276), channel_id=1, source_target_pairs={{0,1},{1,0},{2,3},{3,2},{4,5},{5,4},{6,7},{7,6},{8,9},{9,8},{10,11... | collective-permute-start | bytes 344072 | tf_op jit(solution)/shard_map/ppermute | solution.py:157
  64.6 0.9 %copy-start.2 = (f32[2,3,1,8,3584]{4,3,2,1,0:T(8,128)}, f32[2,3,1,8,3584]{4,3,2,1,0:T(8,128)S(1)}, u32[]{:S(2)}) copy-start(f32[2,3,1,8,3584]{4,3,2,1,0:T(8,128)S(1)} %bitcast_dynamic-update-slice_fusion) | copy-start | bytes 2064388

commit v6 on v5

--- a/solution.py
+++ b/solution.py
@@ -83,6 +83,7 @@
 
 def weight_grads_kernel(steps, replicas, places, _, *refs):
     saved, pre, dy = refs[:replicas], refs[replicas:2 * replicas], refs[2 * replicas:3 * replicas]
+    pair_rows = 2 * saved[0].shape[3]
     in_ref, down_ref, pre_rows, hidden_rows = refs[-4:]
     batch_rows, block = saved[0].shape[3], saved[0].shape[4]
     shard_rows = batch_rows // places
@@ -97,11 +98,9 @@
             def _():
                 for pair in range(replicas // 2):
                     held = pre[2 * pair + parity]
-                    hidden_rows[pair * 2 * count:(pair + 1) * 2 * count] = held[:, :, 2 * hidden_width:].reshape(
-                        2 * count, hidden_width
-                    )
+                    hidden_rows[pair * 2 * count:(pair + 1) * 2 * count] = held[:, 2 * hidden_width:3 * hidden_width]
                     for k in range(steps):
-                        values = held[k, :, :2 * hidden_width].astype(F32)
+                        values = held[k * pair_rows:(k + 1) * pair_rows, :2 * hidden_width].astype(F32)
                         for r in range(2):
                             half = jnp.concatenate(
                                 [
@@ -231,9 +230,11 @@
 
     blocks, gate_factor, activated = lax.optimization_barrier((blocks, gate_factor, activated))
 
-    def weight_grads(pre_held, dy_all):
-        block = lane_block(part_width, 1024)
-        blocks_each = part_width // block
+    block = lane_block(part_width, 1024)
+    blocks_each = part_width // block
+    dy_start = -(-3 * hidden_width // block) * block
+
+    def weight_grads(held_all):
         return pl.pallas_call(
             functools.partial(weight_grads_kernel, steps, replicas, tensor_count),
             grid_spec=pltpu.PrefetchScalarGridSpec(
@@ -245,8 +246,14 @@
                         lambda i, j, at: (at[0] ^ i, 0, 0, 0, at[1] * blocks_each + j),
                     )
                 ] * replicas
-                + [pl.BlockSpec((steps, pair_rows, 3 * hidden_width), lambda i, j, at: (0, 0, 0))] * replicas
-                + [pl.BlockSpec((steps * pair_rows, block), lambda i, j, at: (0, at[1] * blocks_each + j))] * replicas,
+                + [pl.BlockSpec((steps * pair_rows, dy_start), lambda i, j, at: (0, 0))] * replicas
+                + [
+                    pl.BlockSpec(
+                        (steps * pair_rows, block),
+                        lambda i, j, at: (0, dy_start // block + at[1] * blocks_each + j),
+                    )
+                ]
+                * replicas,
                 out_specs=[
                     pl.BlockSpec((1, 1, block, 2 * hidden_width), lambda i, j, at: (at[0] ^ i, 0, j, 0)),
                     pl.BlockSpec((1, 1, hidden_width, block), lambda i, j, at: (at[0] ^ i, 0, 0, j)),
@@ -266,22 +273,22 @@
         )(
             which,
             *saved,
-            *[to_core(pre_held, o) if o else pre_held for o in range(replicas)],
-            *dy_all,
+            *held_all,
+            *held_all,
         )
 
     hand_offs = jnp.zeros((2, steps, shard_rows, width), F32)
     hand_rows = steps * pair_rows
-    dy_held = jnp.zeros((hand_rows + (steps - 1) * shard_rows, width), BF16)
-    pre_held = jnp.zeros((steps, pair_rows, 3 * hidden_width), BF16).at[:, :, 2 * hidden_width:].set(hidden)
+    held = jnp.zeros((hand_rows + (steps - 1) * shard_rows, dy_start + width), BF16)
+    held = lax.dynamic_update_slice(held, hidden.reshape(hand_rows, hidden_width), (0, 2 * hidden_width))
     for k in range(steps):
         dy = placed(blocks)
-        dy_held = dy_held.at[k * pair_rows:(k + 1) * pair_rows].set(dy)
-        if k + 1 == steps:
-            dy_all = [to_core(dy_held, o) if o else dy_held for o in range(replicas)]
+        held = lax.dynamic_update_slice(held, dy, (k * pair_rows, dy_start))
         dh = jnp.einsum("rd,dh->rh", dy, w_down_dir, preferred_element_type=F32)
         pre_grad = jnp.concatenate([dh * gate_factor[k], dh * activated[k]], axis=1).astype(BF16)
-        pre_held = pre_held.at[k, :, :2 * hidden_width].set(pre_grad)
+        held = lax.dynamic_update_slice(held, pre_grad, (k * pair_rows, 0))
+        if k + 1 == steps:
+            held_all = [to_core(held, o) if o else held for o in range(replicas)]
         part = jnp.einsum("rc,cd->rd", pre_grad, w_in_dir, preferred_element_type=F32).astype(BF16)
         part = part.reshape(tensor_count, block_rows, width)
 
@@ -290,10 +297,10 @@
 
         own_part = part_for(place)
         parts = []
-        for s in range(1, tensor_count):
+        for s in [*range(1, tensor_count, 2), *range(2, tensor_count, 2)]:
             parts.append(rotate(part_for(lax.rem(place + s, tensor_count)), s))
         if k + 1 == steps:
-            parts, grads = lax.optimization_barrier((parts, weight_grads(pre_held, dy_all)))
+            parts, grads = lax.optimization_barrier((parts, weight_grads(held_all)))
         summed = own_part.astype(F32)
         for x in parts:
             summed = summed + x.astype(F32)
@@ -306,8 +313,8 @@
                 for s in range(tensor_count)
             ]
             leaving = summed if k == 0 else handed
-            dy_held = dy_held.at[hand_rows + k * shard_rows:hand_rows + (k + 1) * shard_rows].set(
-                leaving[shard_rows:].astype(BF16)
+            held = lax.dynamic_update_slice(
+                held, leaving[shard_rows:].astype(BF16), (hand_rows + k * shard_rows, dy_start)
             )
             incoming = blocks[0].astype(F32)
         else:
@@ -315,7 +322,7 @@
     for k in range(steps):
         if k + 1 < steps:
             start = hand_rows + k * shard_rows
-            arrived = dy_all[1][start:start + shard_rows].astype(F32)
+            arrived = held_all[1][start:start + shard_rows, dy_start:].astype(F32)
             arrived = arrived + theirs(entry) if k == 0 else arrived
         else:
             arrived = last

time: 65.6 us -> 65.3 us (level)
  starting transfers between devices: 26.7 us -> 25.8 us
    ppermute x6 -> x5, starting transfers between devices: 1.72 us -> 1.17 us  [to_core(): return lax.ppermute(x, 'dp', [(i, i ^ offset) for i in range(replicas)])]
  transfers between devices with their start and end apart: 26 -> 25, of which waited for: 14 -> 16; matrix products, arithmetic and copies ran while one was open for 3% -> 3% of each run, Pallas kernels for 16% -> 16%
where the time goes in v6:
time: 65.3 us; the launch traced here: 65.1 us
  starting transfers between devices  25.8 us (40%)
  waiting for transfers between devices  21.4 us (33%)
  Pallas kernels  10.5 us (16%)
  matrix products  3.58 us (5%)
  other arithmetic  1.68 us (3%)
  local copies, waits for them, and re-layouts  1.2 us (2%)
  between operations  0.96 us (1%)
    ppermute x12, starting transfers between devices, rotate(): lax.ppermute(x, 'tensor', [(i, (i + shift) % tensor_count) for i in range...  15.2 us
    ppermute x8, waiting for transfers between devices, local(): lax.ppermute(payload, AXES, ring_pairs(sections, tensor_count, replicas, s))  10.7 us
    ppermute x12, waiting for transfers between devices, rotate(): lax.ppermute(x, 'tensor', [(i, (i + shift) % tensor_count) for i in range...  9.43 us
    ppermute x8, starting transfers between devices, local(): lax.ppermute(payload, AXES, ring_pairs(sections, tensor_count, replicas, s))  9.41 us
    pallas_call x1, Pallas kernels, weight_grads(): pl.pallas_call(functools.partial(weight_grads_kernel, steps, replicas, te...  5.86 us
    pallas_call x1, Pallas kernels, local(): pl.pallas_call(functools.partial(factors_kernel, tensor_count), grid_spec...  4.63 us
    dot_general x3, matrix products, local(): jnp.einsum('rc,cd->rd', pre_grad, w_in_dir, preferred_element_type=F32)  2.25 us
    dot_general x3, matrix products, local(): dh = jnp.einsum('rd,dh->rh', dy, w_down_dir, preferred_element_type=F32)  1.33 us
  transfers between devices with their start and end apart: 25, of which 16 were waited for; matrix products, arithmetic and copies ran while one was open for 3% of the time, Pallas kernels for 16%

profile of v6, /device:TPU:0, one launch (start us, length us, event | category | flops | bytes accessed | tf_op | source)
XLA Modules:
  0.0 65.1 jit_solution(9168960241717641493)
XLA Ops:
  0.6 0.5 collective-permute-start
  1.2 0.4 collective-permute-start.4
  1.7 1.0 %select_bitcast_fusion = f32[8,3584]{1,0:T(8,128)S(1)} fusion(f32[2,1,8,3584]{3,2,1,0:T(8,128)} %param.5, pred[]{:T(512)S(6)} %eq.28), kind=kLoop, calls=%fused_computation.56 | loop fusion | flops 28672 | bytes 344065 | tf_op jit(solution)/shard_map/jit(_where)/select_n | solution.py:144
  2.7 3.7 %collective-permute-start.3 = (bf16[16,3584]{1,0:T(8,128)(2,1)S(1)}, bf16[16,3584]{1,0:T(8,128)(2,1)S(1)}, u32[]{:S(2)}, u32[]{:S(2)}) collective-permute-start(bf16[16,3584]{1,0:T(8,128)(2,1)S(1)} %fusion.9._), channel_id=1, source_target_pairs={{0,6},{2,0},{4,2},{6,4},{1,7},{3,1},{5,3},{7,5},{8,14},{10,8},{12,... | collective-permute-start | bytes 344072 | tf_op jit(solution)/shard_map/ppermute | solution.py:159
  6.4 0.5 collective-permute-start.2
  6.9 0.6 collective-permute-start.1
  7.6 4.6 %factors.1 = (f32[3,64,256]{2,1,0:T(8,128)S(1)}, f32[3,64,256]{2,1,0:T(8,128)S(1)}, bf16[3,64,256]{2,1,0:T(8,128)(2,1)S(1)}, bf16[2,16,3584]{2,1,0:T(8,128)(2,1)...) custom-call(s32[2]{0:T(128)S(1)} %pad_add_fusion.at._, bf16[2,3,1,32,3584]{4,3,2,1,0:T(8,128)(2,1)} %refs_0_.1, ...), custom_call_target="tpu_custom_call" | custom-call | tf_op jit(solution)/shard_map/factors/pallas_call | solution.py:180
  12.2 1.7 %collective-permute-done.2 = bf16[16,3584]{1,0:T(8,128)(2,1)S(1)} collective-permute-done((bf16[16,3584]{1,0:T(8,128)(2,1)S(1)}, bf16[16,3584]{1,0:T(8,128)(2,1)S(1)}, u32[]{:S(2)}, u32[]{:S(2)}) %collective-permute-start.2) | collective-permute-done | bytes 114720 | tf_op jit(solution)/shard_map/ppermute | solution.py:159
  14.0 0.4 fusion.25
  14.4 0.8 %convolution_convert_fusion.2 = bf16[64,3584]{1,0:T(8,128)(2,1)S(1)} fusion(bf16[512,3584]{1,0:T(8,128)(2,1)S(1)} %get-tuple-element.31, bf16[64,256]{1,0:T(8,128)(2,1)S(1)} %get-tuple-element.73, bf16[64,256]{1,0:T(8,128)(2,1)S(1)} %get-tuple-element.72), kind=kOutput, calls=%fused_computation.2 | convolution fusion | flops 235241472 | bytes 4194304 | tf_op jit(solution)/shard_map/rc,cd->rd/dot_general | solution.py:292
  15.2 0.7 %collective-permute-start.6 = (bf16[16,3584]{1,0:T(8,128)(2,1)S(1)}, bf16[16,3584]{1,0:T(8,128)(2,1)S(1)}, u32[]{:S(2)}, u32[]{:S(2)}) collective-permute-start(bf16[16,3584]{1,0:T(8,128)(2,1)S(1)} %get-tuple-element.61), channel_id=1, source_target_pairs={{0,2},{2,4},{4,6},{6,0},{1,3},{3,5},{5,7},{7,1},{8,10},{10,12},{12... | collective-permute-start | bytes 344072 | tf_op jit(solution)/shard_map/ppermute | solution.py:159
  16.0 0.5 collective-permute-start.8
  16.5 2.2 %collective-permute-start.7 = (bf16[16,3584]{1,0:T(8,128)(2,1)S(1)}, bf16[16,3584]{1,0:T(8,128)(2,1)S(1)}, u32[]{:S(2)}, u32[]{:S(2)}) collective-permute-start(bf16[16,3584]{1,0:T(8,128)(2,1)S(1)} %get-tuple-element.63), channel_id=1, source_target_pairs={{0,6},{2,0},{4,2},{6,4},{1,7},{3,1},{5,3},{7,5},{8,14},{10,8},{12,... | collective-permute-start | bytes 344072 | tf_op jit(solution)/shard_map/ppermute | solution.py:159
  18.7 0.1 dynamic_update_slice.53
  18.9 2.9 %collective-permute-done.6 = bf16[16,3584]{1,0:T(8,128)(2,1)S(1)} collective-permute-done((bf16[16,3584]{1,0:T(8,128)(2,1)S(1)}, bf16[16,3584]{1,0:T(8,128)(2,1)S(1)}, u32[]{:S(2)}, u32[]{:S(2)}) %collective-permute-start.6) | collective-permute-done | bytes 114720 | tf_op jit(solution)/shard_map/ppermute | solution.py:159
  21.8 0.9 %collective-permute-done.8 = bf16[16,3584]{1,0:T(8,128)(2,1)S(1)} collective-permute-done((bf16[16,3584]{1,0:T(8,128)(2,1)S(1)}, bf16[16,3584]{1,0:T(8,128)(2,1)S(1)}, u32[]{:S(2)}, u32[]{:S(2)}) %collective-permute-start.8) | collective-permute-done | bytes 114720 | tf_op jit(solution)/shard_map/ppermute | solution.py:159
  22.7 0.1 bitcast_select_fusion.1
  22.9 1.0 %collective-permute-start.11 = (bf16[16,3584]{1,0:T(8,128)(2,1)S(1)}, bf16[16,3584]{1,0:T(8,128)(2,1)S(1)}, u32[]{:S(2)}, u32[]{:S(2)}) collective-permute-start(bf16[16,3584]{1,0:T(8,128)(2,1)S(1)} %get-tuple-element.44), channel_id=1, source_target_pairs={{0,5},{1,13},{2,7},{3,15},{4,1},{5,9},{6,3},{7,11},{8,4},{9,21},{1... | collective-permute-start | bytes 344072 | tf_op jit(solution)/shard_map/ppermute | solution.py:312
  23.9 2.1 %collective-permute-start.10 = (bf16[16,3584]{1,0:T(8,128)(2,1)S(1)}, bf16[16,3584]{1,0:T(8,128)(2,1)S(1)}, u32[]{:S(2)}, u32[]{:S(2)}) collective-permute-start(bf16[16,3584]{1,0:T(8,128)(2,1)S(1)} %get-tuple-element.44), channel_id=1, source_target_pairs={{0,7},{1,15},{2,1},{3,9},{4,3},{5,11},{6,5},{7,13},{8,6},{9,23},{1... | collective-permute-start | bytes 344072 | tf_op jit(solution)/shard_map/ppermute | solution.py:312
  26.0 1.1 %collective-permute-start.9 = (bf16[16,3584]{1,0:T(8,128)(2,1)S(1)}, bf16[16,3584]{1,0:T(8,128)(2,1)S(1)}, u32[]{:S(2)}, u32[]{:S(2)}) collective-permute-start(bf16[16,3584]{1,0:T(8,128)(2,1)S(1)} %get-tuple-element.44), channel_id=1, source_target_pairs={{0,1},{1,9},{2,3},{3,11},{4,5},{5,13},{6,7},{7,15},{8,0},{9,17},{1... | collective-permute-start | bytes 344072 | tf_op jit(solution)/shard_map/ppermute | solution.py:312
  27.1 2.7 %collective-permute-done.12 = bf16[16,3584]{1,0:T(8,128)(2,1)S(1)} collective-permute-done((bf16[16,3584]{1,0:T(8,128)(2,1)S(1)}, bf16[16,3584]{1,0:T(8,128)(2,1)S(1)}, u32[]{:S(2)}, u32[]{:S(2)}) %collective-permute-start.12) | collective-permute-done | bytes 114720 | tf_op jit(solution)/shard_map/ppermute | solution.py:312
  29.8 1.0 %collective-permute-done.11 = bf16[16,3584]{1,0:T(8,128)(2,1)S(1)} collective-permute-done((bf16[16,3584]{1,0:T(8,128)(2,1)S(1)}, bf16[16,3584]{1,0:T(8,128)(2,1)S(1)}, u32[]{:S(2)}, u32[]{:S(2)}) %collective-permute-start.11) | collective-permute-done | bytes 114720 | tf_op jit(solution)/shard_map/ppermute | solution.py:312
  30.8 0.5 collective-permute-done.10
  31.3 1.5 %collective-permute-done.9 = bf16[16,3584]{1,0:T(8,128)(2,1)S(1)} collective-permute-done((bf16[16,3584]{1,0:T(8,128)(2,1)S(1)}, bf16[16,3584]{1,0:T(8,128)(2,1)S(1)}, u32[]{:S(2)}, u32[]{:S(2)}) %collective-permute-start.9) | collective-permute-done | bytes 114720 | tf_op jit(solution)/shard_map/ppermute | solution.py:312
  32.8 0.4 fusion.23
  33.3 0.7 %convolution_convert_fusion.1 = bf16[64,3584]{1,0:T(8,128)(2,1)S(1)} fusion(bf16[512,3584]{1,0:T(8,128)(2,1)S(1)} %get-tuple-element.31, bf16[64,256]{1,0:T(8,128)(2,1)S(1)} %get-tuple-element.71, bf16[64,256]{1,0:T(8,128)(2,1)S(1)} %get-tuple-element.70), kind=kOutput, calls=%fused_computation.1 | convolution fusion | flops 235241472 | bytes 4194304 | tf_op jit(solution)/shard_map/rc,cd->rd/dot_general | solution.py:292
  34.1 0.8 %collective-permute-start.13 = (bf16[16,3584]{1,0:T(8,128)(2,1)S(1)}, bf16[16,3584]{1,0:T(8,128)(2,1)S(1)}, u32[]{:S(2)}, u32[]{:S(2)}) collective-permute-start(bf16[16,3584]{1,0:T(8,128)(2,1)S(1)} %get-tuple-element.54), channel_id=1, source_target_pairs={{0,2},{2,4},{4,6},{6,0},{1,3},{3,5},{5,7},{7,1},{8,10},{10,12},{12... | collective-permute-start | bytes 344072 | tf_op jit(solution)/shard_map/ppermute | solution.py:159
  34.9 1.0 %collective-permute-start.15 = (bf16[16,3584]{1,0:T(8,128)(2,1)S(1)}, bf16[16,3584]{1,0:T(8,128)(2,1)S(1)}, u32[]{:S(2)}, u32[]{:S(2)}) collective-permute-start(bf16[16,3584]{1,0:T(8,128)(2,1)S(1)} %get-tuple-element.55), channel_id=1, source_target_pairs={{0,4},{2,6},{4,0},{6,2},{1,5},{3,7},{5,1},{7,3},{8,12},{10,14},{12... | collective-permute-start | bytes 344072 | tf_op jit(solution)/shard_map/ppermute | solution.py:159
  35.9 2.2 %collective-permute-start.14 = (bf16[16,3584]{1,0:T(8,128)(2,1)S(1)}, bf16[16,3584]{1,0:T(8,128)(2,1)S(1)}, u32[]{:S(2)}, u32[]{:S(2)}) collective-permute-start(bf16[16,3584]{1,0:T(8,128)(2,1)S(1)} %get-tuple-element.56), channel_id=1, source_target_pairs={{0,6},{2,0},{4,2},{6,4},{1,7},{3,1},{5,3},{7,5},{8,14},{10,8},{12,... | collective-permute-start | bytes 344072 | tf_op jit(solution)/shard_map/ppermute | solution.py:159
  38.1 2.9 %collective-permute-done.13 = bf16[16,3584]{1,0:T(8,128)(2,1)S(1)} collective-permute-done((bf16[16,3584]{1,0:T(8,128)(2,1)S(1)}, bf16[16,3584]{1,0:T(8,128)(2,1)S(1)}, u32[]{:S(2)}, u32[]{:S(2)}) %collective-permute-start.13) | collective-permute-done | bytes 114720 | tf_op jit(solution)/shard_map/ppermute | solution.py:159
  41.2 0.5 collective-permute-done.14
  41.7 0.1 bitcast_select_fusion
  41.8 1.6 %collective-permute-start.18 = (bf16[16,3584]{1,0:T(8,128)(2,1)S(1)}, bf16[16,3584]{1,0:T(8,128)(2,1)S(1)}, u32[]{:S(2)}, u32[]{:S(2)}) collective-permute-start(bf16[16,3584]{1,0:T(8,128)(2,1)S(1)} %get-tuple-element.41), channel_id=1, source_target_pairs={{0,5},{1,13},{2,7},{3,15},{4,1},{5,9},{6,3},{7,11},{8,4},{9,21},{1... | collective-permute-start | bytes 344072 | tf_op jit(solution)/shard_map/ppermute | solution.py:312
  43.5 1.8 %collective-permute-start.17 = (bf16[16,3584]{1,0:T(8,128)(2,1)S(1)}, bf16[16,3584]{1,0:T(8,128)(2,1)S(1)}, u32[]{:S(2)}, u32[]{:S(2)}) collective-permute-start(bf16[16,3584]{1,0:T(8,128)(2,1)S(1)} %get-tuple-element.41), channel_id=1, source_target_pairs={{0,7},{1,15},{2,1},{3,9},{4,3},{5,11},{6,5},{7,13},{8,6},{9,23},{1... | collective-permute-start | bytes 344072 | tf_op jit(solution)/shard_map/ppermute | solution.py:312
  45.3 1.6 %collective-permute-start.16 = (bf16[16,3584]{1,0:T(8,128)(2,1)S(1)}, bf16[16,3584]{1,0:T(8,128)(2,1)S(1)}, u32[]{:S(2)}, u32[]{:S(2)}) collective-permute-start(bf16[16,3584]{1,0:T(8,128)(2,1)S(1)} %get-tuple-element.41), channel_id=1, source_target_pairs={{0,1},{1,9},{2,3},{3,11},{4,5},{5,13},{6,7},{7,15},{8,0},{9,17},{1... | collective-permute-start | bytes 344072 | tf_op jit(solution)/shard_map/ppermute | solution.py:312
  46.9 1.6 %collective-permute-done.19 = bf16[16,3584]{1,0:T(8,128)(2,1)S(1)} collective-permute-done((bf16[16,3584]{1,0:T(8,128)(2,1)S(1)}, bf16[16,3584]{1,0:T(8,128)(2,1)S(1)}, u32[]{:S(2)}, u32[]{:S(2)}) %collective-permute-start.19) | collective-permute-done | bytes 114720 | tf_op jit(solution)/shard_map/ppermute | solution.py:312
  48.5 1.2 %collective-permute-done.18 = bf16[16,3584]{1,0:T(8,128)(2,1)S(1)} collective-permute-done((bf16[16,3584]{1,0:T(8,128)(2,1)S(1)}, bf16[16,3584]{1,0:T(8,128)(2,1)S(1)}, u32[]{:S(2)}, u32[]{:S(2)}) %collective-permute-start.18) | collective-permute-done | bytes 114720 | tf_op jit(solution)/shard_map/ppermute | solution.py:312
  49.8 0.8 %collective-permute-done.17 = bf16[16,3584]{1,0:T(8,128)(2,1)S(1)} collective-permute-done((bf16[16,3584]{1,0:T(8,128)(2,1)S(1)}, bf16[16,3584]{1,0:T(8,128)(2,1)S(1)}, u32[]{:S(2)}, u32[]{:S(2)}) %collective-permute-start.17) | collective-permute-done | bytes 114720 | tf_op jit(solution)/shard_map/ppermute | solution.py:312
  50.5 1.4 %collective-permute-done.16 = bf16[16,3584]{1,0:T(8,128)(2,1)S(1)} collective-permute-done((bf16[16,3584]{1,0:T(8,128)(2,1)S(1)}, bf16[16,3584]{1,0:T(8,128)(2,1)S(1)}, u32[]{:S(2)}, u32[]{:S(2)}) %collective-permute-start.16) | collective-permute-done | bytes 114720 | tf_op jit(solution)/shard_map/ppermute | solution.py:312
  52.0 0.4 fusion.21
  52.7 0.7 %convolution_convert_fusion = bf16[64,3584]{1,0:T(8,128)(2,1)S(1)} fusion(bf16[512,3584]{1,0:T(8,128)(2,1)S(1)} %get-tuple-element.31, bf16[64,256]{1,0:T(8,128)(2,1)S(1)} %get-tuple-element.69, bf16[64,256]{1,0:T(8,128)(2,1)S(1)} %get-tuple-element.68), kind=kOutput, calls=%fused_computation | convolution fusion | flops 235241472 | bytes 4194304 | tf_op jit(solution)/shard_map/rc,cd->rd/dot_general | solution.py:292
  53.5 0.9 %collective-permute-start.22 = (bf16[16,3584]{1,0:T(8,128)(2,1)S(1)}, bf16[16,3584]{1,0:T(8,128)(2,1)S(1)}, u32[]{:S(2)}, u32[]{:S(2)}) collective-permute-start(bf16[16,3584]{1,0:T(8,128)(2,1)S(1)} %get-tuple-element.47), channel_id=1, source_target_pairs={{0,4},{2,6},{4,0},{6,2},{1,5},{3,7},{5,1},{7,3},{8,12},{10,14},{12... | collective-permute-start | bytes 344072 | tf_op jit(solution)/shard_map/ppermute | solution.py:159
  54.4 1.2 %collective-permute-start.21 = (bf16[16,3584]{1,0:T(8,128)(2,1)S(1)}, bf16[16,3584]{1,0:T(8,128)(2,1)S(1)}, u32[]{:S(2)}, u32[]{:S(2)}) collective-permute-start(bf16[16,3584]{1,0:T(8,128)(2,1)S(1)} %get-tuple-element.48), channel_id=1, source_target_pairs={{0,6},{2,0},{4,2},{6,4},{1,7},{3,1},{5,3},{7,5},{8,14},{10,8},{12,... | collective-permute-start | bytes 344072 | tf_op jit(solution)/shard_map/ppermute | solution.py:159
  55.7 0.8 %collective-permute-start.20 = (bf16[16,3584]{1,0:T(8,128)(2,1)S(1)}, bf16[16,3584]{1,0:T(8,128)(2,1)S(1)}, u32[]{:S(2)}, u32[]{:S(2)}) collective-permute-start(bf16[16,3584]{1,0:T(8,128)(2,1)S(1)} %get-tuple-element.49), channel_id=1, source_target_pairs={{0,2},{2,4},{4,6},{6,0},{1,3},{3,5},{5,7},{7,1},{8,10},{10,12},{12... | collective-permute-start | bytes 344072 | tf_op jit(solution)/shard_map/ppermute | solution.py:159
  56.5 5.9 %weight_grads.1 = (f32[2,1,1792,512]{3,2,1,0:T(8,128)}, f32[2,1,256,1792]{3,2,1,0:T(8,128)}) custom-call(s32[2]{0:T(128)S(1)} %pad_add_fusion.at._, bf16[2,3,1,32,3584]{4,3,2,1,0:T(8,128)(2,1)S(1)} %copy-done, bf16[2,3,1,32,3584]{4,3,2,1,0:T(8,128)(2,1)S(1)} %collective-permute-done.4.peer_ref.refs_1_, bf16[208,4480]{1,0:T(8,128)(2,1)S(1)} %fusion.27.refs_2_.refs_4_, ...), custom_call_target="tpu_custom_call" | custom-call | tf_op jit(solution)/shard_map/weight_grads/pallas_call | solution.py:238
  62.4 0.4 collective-permute-done.20
  63.0 1.2 %collective-permute-done.24 = f32[8,3584]{1,0:T(8,128)S(1)} collective-permute-done((f32[8,3584]{1,0:T(8,128)S(1)}, f32[8,3584]{1,0:T(8,128)S(1)}, u32[]{:S(2)}, u32[]{:S(2)}) %collective-permute-start.24) | collective-permute-done | bytes 114720 | tf_op jit(solution)/shard_map/ppermute | solution.py:156
  64.3 0.8 %copy-done.2 = f32[2,3,1,8,3584]{4,3,2,1,0:T(8,128)} copy-done((f32[2,3,1,8,3584]{4,3,2,1,0:T(8,128)}, f32[2,3,1,8,3584]{4,3,2,1,0:T(8,128)S(1)}, u32[]{:S(2)}) %copy-start.2) | copy-done | bytes 688152
  (46 shorter events, 1.2 us)
Async XLA Ops:
  0.6 2.0 %collective-permute-start = (f32[2,1,8,3584]{3,2,1,0:T(8,128)}, f32[2,1,8,3584]{3,2,1,0:T(8,128)S(1)}, u32[]{:S(2)}, u32[]{:S(2)}) collective-permute-start(f32[2,1,8,3584]{3,2,1,0:T(8,128)} %param.5), channel_id=1, source_target_pairs={{0,1},{1,0},{2,3},{3,2},{4,5},{5,4},{6,7},{7,6},{8,9},{9,8},{10,11... | collective-permute-start | bytes 688136 | tf_op jit(solution)/shard_map/ppermute | solution.py:156
  1.1 6.4 %collective-permute-start.5 = (f32[2,2,8,3584]{3,2,1,0:T(8,128)}, f32[2,2,8,3584]{3,2,1,0:T(8,128)S(1)}, u32[]{:S(2)}, u32[]{:S(2)}) collective-permute-start(f32[2,2,8,3584]{3,2,1,0:T(8,128)} %fresh_ref.1), channel_id=1, source_target_pairs={{0,1},{1,0},{2,3},{3,2},{4,5},{5,4},{6,7},{7,6},{8,9},{9,8},{10,11... | collective-permute-start | bytes 1376264 | tf_op jit(solution)/shard_map/ppermute | solution.py:156
  1.2 6.3 %collective-permute-start.4 = (bf16[2,3,1,32,3584]{4,3,2,1,0:T(8,128)(2,1)}, bf16[2,3,1,32,3584]{4,3,2,1,0:T(8,128)(2,1)S(1)}, u32[]{:S(2)}, u32[]{:S(2)}) collective-permute-start(bf16[2,3,1,32,3584]{4,3,2,1,0:T(8,128)(2,1)} %refs_0_.1), channel_id=1, source_target_pairs={{0,1},{1,0},{2,3},{3,2},{4,5},{5,4},{6,7},{7,6},{8,9},{9,8},{10,11... | collective-permute-start | bytes 4128776 | tf_op jit(solution)/shard_map/ppermute | solution.py:156
  2.7 9.5 %collective-permute-start.3 = (bf16[16,3584]{1,0:T(8,128)(2,1)S(1)}, bf16[16,3584]{1,0:T(8,128)(2,1)S(1)}, u32[]{:S(2)}, u32[]{:S(2)}) collective-permute-start(bf16[16,3584]{1,0:T(8,128)(2,1)S(1)} %fusion.9._), channel_id=1, source_target_pairs={{0,6},{2,0},{4,2},{6,4},{1,7},{3,1},{5,3},{7,5},{8,14},{10,8},{12,... | collective-permute-start | bytes 344072 | tf_op jit(solution)/shard_map/ppermute | solution.py:159
  6.4 7.6 %collective-permute-start.2 = (bf16[16,3584]{1,0:T(8,128)(2,1)S(1)}, bf16[16,3584]{1,0:T(8,128)(2,1)S(1)}, u32[]{:S(2)}, u32[]{:S(2)}) collective-permute-start(bf16[16,3584]{1,0:T(8,128)(2,1)S(1)} %fusion.9._), channel_id=1, source_target_pairs={{0,4},{2,6},{4,0},{6,2},{1,5},{3,7},{5,1},{7,3},{8,12},{10,14},{12... | collective-permute-start | bytes 344072 | tf_op jit(solution)/shard_map/ppermute | solution.py:159
  6.9 7.0 %collective-permute-start.1 = (bf16[16,3584]{1,0:T(8,128)(2,1)S(1)}, bf16[16,3584]{1,0:T(8,128)(2,1)S(1)}, u32[]{:S(2)}, u32[]{:S(2)}) collective-permute-start(bf16[16,3584]{1,0:T(8,128)(2,1)S(1)} %fusion.9._), channel_id=1, source_target_pairs={{0,2},{2,4},{4,6},{6,0},{1,3},{3,5},{5,7},{7,1},{8,10},{10,12},{12... | collective-permute-start | bytes 344072 | tf_op jit(solution)/shard_map/ppermute | solution.py:159
  15.2 6.6 %collective-permute-start.6 = (bf16[16,3584]{1,0:T(8,128)(2,1)S(1)}, bf16[16,3584]{1,0:T(8,128)(2,1)S(1)}, u32[]{:S(2)}, u32[]{:S(2)}) collective-permute-start(bf16[16,3584]{1,0:T(8,128)(2,1)S(1)} %get-tuple-element.61), channel_id=1, source_target_pairs={{0,2},{2,4},{4,6},{6,0},{1,3},{3,5},{5,7},{7,1},{8,10},{10,12},{12... | collective-permute-start | bytes 344072 | tf_op jit(solution)/shard_map/ppermute | solution.py:159
  16.0 6.7 %collective-permute-start.8 = (bf16[16,3584]{1,0:T(8,128)(2,1)S(1)}, bf16[16,3584]{1,0:T(8,128)(2,1)S(1)}, u32[]{:S(2)}, u32[]{:S(2)}) collective-permute-start(bf16[16,3584]{1,0:T(8,128)(2,1)S(1)} %get-tuple-element.62), channel_id=1, source_target_pairs={{0,4},{2,6},{4,0},{6,2},{1,5},{3,7},{5,1},{7,3},{8,12},{10,14},{12... | collective-permute-start | bytes 344072 | tf_op jit(solution)/shard_map/ppermute | solution.py:159
  16.5 6.2 %collective-permute-start.7 = (bf16[16,3584]{1,0:T(8,128)(2,1)S(1)}, bf16[16,3584]{1,0:T(8,128)(2,1)S(1)}, u32[]{:S(2)}, u32[]{:S(2)}) collective-permute-start(bf16[16,3584]{1,0:T(8,128)(2,1)S(1)} %get-tuple-element.63), channel_id=1, source_target_pairs={{0,6},{2,0},{4,2},{6,4},{1,7},{3,1},{5,3},{7,5},{8,14},{10,8},{12,... | collective-permute-start | bytes 344072 | tf_op jit(solution)/shard_map/ppermute | solution.py:159
  22.8 7.0 %collective-permute-start.12 = (bf16[16,3584]{1,0:T(8,128)(2,1)S(1)}, bf16[16,3584]{1,0:T(8,128)(2,1)S(1)}, u32[]{:S(2)}, u32[]{:S(2)}) collective-permute-start(bf16[16,3584]{1,0:T(8,128)(2,1)S(1)} %get-tuple-element.44), channel_id=1, source_target_pairs={{0,3},{1,11},{2,5},{3,13},{4,7},{5,15},{6,1},{7,9},{8,2},{9,19},{1... | collective-permute-start | bytes 344072 | tf_op jit(solution)/shard_map/ppermute | solution.py:312
  22.9 7.9 %collective-permute-start.11 = (bf16[16,3584]{1,0:T(8,128)(2,1)S(1)}, bf16[16,3584]{1,0:T(8,128)(2,1)S(1)}, u32[]{:S(2)}, u32[]{:S(2)}) collective-permute-start(bf16[16,3584]{1,0:T(8,128)(2,1)S(1)} %get-tuple-element.44), channel_id=1, source_target_pairs={{0,5},{1,13},{2,7},{3,15},{4,1},{5,9},{6,3},{7,11},{8,4},{9,21},{1... | collective-permute-start | bytes 344072 | tf_op jit(solution)/shard_map/ppermute | solution.py:312
  23.9 7.4 %collective-permute-start.10 = (bf16[16,3584]{1,0:T(8,128)(2,1)S(1)}, bf16[16,3584]{1,0:T(8,128)(2,1)S(1)}, u32[]{:S(2)}, u32[]{:S(2)}) collective-permute-start(bf16[16,3584]{1,0:T(8,128)(2,1)S(1)} %get-tuple-element.44), channel_id=1, source_target_pairs={{0,7},{1,15},{2,1},{3,9},{4,3},{5,11},{6,5},{7,13},{8,6},{9,23},{1... | collective-permute-start | bytes 344072 | tf_op jit(solution)/shard_map/ppermute | solution.py:312
  26.0 6.8 %collective-permute-start.9 = (bf16[16,3584]{1,0:T(8,128)(2,1)S(1)}, bf16[16,3584]{1,0:T(8,128)(2,1)S(1)}, u32[]{:S(2)}, u32[]{:S(2)}) collective-permute-start(bf16[16,3584]{1,0:T(8,128)(2,1)S(1)} %get-tuple-element.44), channel_id=1, source_target_pairs={{0,1},{1,9},{2,3},{3,11},{4,5},{5,13},{6,7},{7,15},{8,0},{9,17},{1... | collective-permute-start | bytes 344072 | tf_op jit(solution)/shard_map/ppermute | solution.py:312
  34.1 7.0 %collective-permute-start.13 = (bf16[16,3584]{1,0:T(8,128)(2,1)S(1)}, bf16[16,3584]{1,0:T(8,128)(2,1)S(1)}, u32[]{:S(2)}, u32[]{:S(2)}) collective-permute-start(bf16[16,3584]{1,0:T(8,128)(2,1)S(1)} %get-tuple-element.54), channel_id=1, source_target_pairs={{0,2},{2,4},{4,6},{6,0},{1,3},{3,5},{5,7},{7,1},{8,10},{10,12},{12... | collective-permute-start | bytes 344072 | tf_op jit(solution)/shard_map/ppermute | solution.py:159
  34.9 6.3 %collective-permute-start.15 = (bf16[16,3584]{1,0:T(8,128)(2,1)S(1)}, bf16[16,3584]{1,0:T(8,128)(2,1)S(1)}, u32[]{:S(2)}, u32[]{:S(2)}) collective-permute-start(bf16[16,3584]{1,0:T(8,128)(2,1)S(1)} %get-tuple-element.55), channel_id=1, source_target_pairs={{0,4},{2,6},{4,0},{6,2},{1,5},{3,7},{5,1},{7,3},{8,12},{10,14},{12... | collective-permute-start | bytes 344072 | tf_op jit(solution)/shard_map/ppermute | solution.py:159
  35.9 5.7 %collective-permute-start.14 = (bf16[16,3584]{1,0:T(8,128)(2,1)S(1)}, bf16[16,3584]{1,0:T(8,128)(2,1)S(1)}, u32[]{:S(2)}, u32[]{:S(2)}) collective-permute-start(bf16[16,3584]{1,0:T(8,128)(2,1)S(1)} %get-tuple-element.56), channel_id=1, source_target_pairs={{0,6},{2,0},{4,2},{6,4},{1,7},{3,1},{5,3},{7,5},{8,14},{10,8},{12,... | collective-permute-start | bytes 344072 | tf_op jit(solution)/shard_map/ppermute | solution.py:159
  41.8 6.7 %collective-permute-start.19 = (bf16[16,3584]{1,0:T(8,128)(2,1)S(1)}, bf16[16,3584]{1,0:T(8,128)(2,1)S(1)}, u32[]{:S(2)}, u32[]{:S(2)}) collective-permute-start(bf16[16,3584]{1,0:T(8,128)(2,1)S(1)} %get-tuple-element.41), channel_id=1, source_target_pairs={{0,3},{1,11},{2,5},{3,13},{4,7},{5,15},{6,1},{7,9},{8,2},{9,19},{1... | collective-permute-start | bytes 344072 | tf_op jit(solution)/shard_map/ppermute | solution.py:312
  41.8 7.9 %collective-permute-start.18 = (bf16[16,3584]{1,0:T(8,128)(2,1)S(1)}, bf16[16,3584]{1,0:T(8,128)(2,1)S(1)}, u32[]{:S(2)}, u32[]{:S(2)}) collective-permute-start(bf16[16,3584]{1,0:T(8,128)(2,1)S(1)} %get-tuple-element.41), channel_id=1, source_target_pairs={{0,5},{1,13},{2,7},{3,15},{4,1},{5,9},{6,3},{7,11},{8,4},{9,21},{1... | collective-permute-start | bytes 344072 | tf_op jit(solution)/shard_map/ppermute | solution.py:312
  43.5 7.1 %collective-permute-start.17 = (bf16[16,3584]{1,0:T(8,128)(2,1)S(1)}, bf16[16,3584]{1,0:T(8,128)(2,1)S(1)}, u32[]{:S(2)}, u32[]{:S(2)}) collective-permute-start(bf16[16,3584]{1,0:T(8,128)(2,1)S(1)} %get-tuple-element.41), channel_id=1, source_target_pairs={{0,7},{1,15},{2,1},{3,9},{4,3},{5,11},{6,5},{7,13},{8,6},{9,23},{1... | collective-permute-start | bytes 344072 | tf_op jit(solution)/shard_map/ppermute | solution.py:312
  45.3 6.7 %collective-permute-start.16 = (bf16[16,3584]{1,0:T(8,128)(2,1)S(1)}, bf16[16,3584]{1,0:T(8,128)(2,1)S(1)}, u32[]{:S(2)}, u32[]{:S(2)}) collective-permute-start(bf16[16,3584]{1,0:T(8,128)(2,1)S(1)} %get-tuple-element.41), channel_id=1, source_target_pairs={{0,1},{1,9},{2,3},{3,11},{4,5},{5,13},{6,7},{7,15},{8,0},{9,17},{1... | collective-permute-start | bytes 344072 | tf_op jit(solution)/shard_map/ppermute | solution.py:312
  52.5 3.9 %collective-permute-start.23 = (bf16[208,4480]{1,0:T(8,128)(2,1)S(1)}, bf16[208,4480]{1,0:T(8,128)(2,1)S(1)}, u32[]{:S(2)}, u32[]{:S(2)}) collective-permute-start(bf16[208,4480]{1,0:T(8,128)(2,1)S(1)} %fusion.27.refs_2_.refs_4_), channel_id=1, source_target_pairs={{0,1},{1,0},{2,3},{3,2},{4,5},{5,4},{6,7},{7,6},{8,9},{9,8},{10,11... | collective-permute-start | bytes 5591048 | tf_op jit(solution)/shard_map/ppermute | solution.py:156
  52.7 3.8 %copy-start = (bf16[2,3,1,32,3584]{4,3,2,1,0:T(8,128)(2,1)S(1)}, bf16[2,3,1,32,3584]{4,3,2,1,0:T(8,128)(2,1)}, u32[]{:S(2)}) copy-start(bf16[2,3,1,32,3584]{4,3,2,1,0:T(8,128)(2,1)} %refs_0_.1) | copy-start | bytes 4128772
  53.5 8.9 %collective-permute-start.22 = (bf16[16,3584]{1,0:T(8,128)(2,1)S(1)}, bf16[16,3584]{1,0:T(8,128)(2,1)S(1)}, u32[]{:S(2)}, u32[]{:S(2)}) collective-permute-start(bf16[16,3584]{1,0:T(8,128)(2,1)S(1)} %get-tuple-element.47), channel_id=1, source_target_pairs={{0,4},{2,6},{4,0},{6,2},{1,5},{3,7},{5,1},{7,3},{8,12},{10,14},{12... | collective-permute-start | bytes 344072 | tf_op jit(solution)/shard_map/ppermute | solution.py:159
  54.4 7.9 %collective-permute-start.21 = (bf16[16,3584]{1,0:T(8,128)(2,1)S(1)}, bf16[16,3584]{1,0:T(8,128)(2,1)S(1)}, u32[]{:S(2)}, u32[]{:S(2)}) collective-permute-start(bf16[16,3584]{1,0:T(8,128)(2,1)S(1)} %get-tuple-element.48), channel_id=1, source_target_pairs={{0,6},{2,0},{4,2},{6,4},{1,7},{3,1},{5,3},{7,5},{8,14},{10,8},{12,... | collective-permute-start | bytes 344072 | tf_op jit(solution)/shard_map/ppermute | solution.py:159
  55.7 7.1 %collective-permute-start.20 = (bf16[16,3584]{1,0:T(8,128)(2,1)S(1)}, bf16[16,3584]{1,0:T(8,128)(2,1)S(1)}, u32[]{:S(2)}, u32[]{:S(2)}) collective-permute-start(bf16[16,3584]{1,0:T(8,128)(2,1)S(1)} %get-tuple-element.49), channel_id=1, source_target_pairs={{0,2},{2,4},{4,6},{6,0},{1,3},{3,5},{5,7},{7,1},{8,10},{10,12},{12... | collective-permute-start | bytes 344072 | tf_op jit(solution)/shard_map/ppermute | solution.py:159
  56.5 6.5 %copy-start.1 = (f32[2,1,8,3584]{3,2,1,0:T(8,128)S(1)}, f32[2,1,8,3584]{3,2,1,0:T(8,128)}, u32[]{:S(2)}) copy-start(f32[2,1,8,3584]{3,2,1,0:T(8,128)} %param.5) | copy-start | bytes 688132
  62.9 1.4 %collective-permute-start.24 = (f32[8,3584]{1,0:T(8,128)S(1)}, f32[8,3584]{1,0:T(8,128)S(1)}, u32[]{:S(2)}, u32[]{:S(2)}) collective-permute-start(f32[8,3584]{1,0:T(8,128)S(1)} %slice.97), channel_id=1, source_target_pairs={{0,1},{1,0},{2,3},{3,2},{4,5},{5,4},{6,7},{7,6},{8,9},{9,8},{10,11... | collective-permute-start | bytes 344072 | tf_op jit(solution)/shard_map/ppermute | solution.py:156
  64.3 0.9 %copy-start.2 = (f32[2,3,1,8,3584]{4,3,2,1,0:T(8,128)}, f32[2,3,1,8,3584]{4,3,2,1,0:T(8,128)S(1)}, u32[]{:S(2)}) copy-start(f32[2,3,1,8,3584]{4,3,2,1,0:T(8,128)S(1)} %bitcast_dynamic-update-slice_fusion) | copy-start | bytes 2064388

commit v7 on v6

--- a/solution.py
+++ b/solution.py
@@ -297,7 +297,7 @@
 
         own_part = part_for(place)
         parts = []
-        for s in [*range(1, tensor_count, 2), *range(2, tensor_count, 2)]:
+        for s in range(1, tensor_count) if k + 1 == steps else [*range(1, tensor_count, 2), *range(2, tensor_count, 2)]:
             parts.append(rotate(part_for(lax.rem(place + s, tensor_count)), s))
         if k + 1 == steps:
             parts, grads = lax.optimization_barrier((parts, weight_grads(held_all)))

time: 65.3 us -> 65.1 us (level)
  no operation moved by 1% of the time
where the time goes in v7:
time: 65.1 us; the launch traced here: 64.9 us
  starting transfers between devices  25.8 us (40%)
  waiting for transfers between devices  21.2 us (33%)
  Pallas kernels  10.5 us (16%)
  matrix products  3.58 us (5%)
  other arithmetic  1.68 us (3%)
  local copies, waits for them, and re-layouts  1.2 us (2%)
  between operations  0.96 us (1%)
    ppermute x12, starting transfers between devices, rotate(): lax.ppermute(x, 'tensor', [(i, (i + shift) % tensor_count) for i in range...  15.2 us
    ppermute x8, waiting for transfers between devices, local(): lax.ppermute(payload, AXES, ring_pairs(sections, tensor_count, replicas, s))  10.7 us
    ppermute x8, starting transfers between devices, local(): lax.ppermute(payload, AXES, ring_pairs(sections, tensor_count, replicas, s))  9.41 us
    ppermute x12, waiting for transfers between devices, rotate(): lax.ppermute(x, 'tensor', [(i, (i + shift) % tensor_count) for i in range...  9.22 us
    pallas_call x1, Pallas kernels, weight_grads(): pl.pallas_call(functools.partial(weight_grads_kernel, steps, replicas, te...  5.86 us
    pallas_call x1, Pallas kernels, local(): pl.pallas_call(functools.partial(factors_kernel, tensor_count), grid_spec...  4.63 us
    dot_general x3, matrix products, local(): jnp.einsum('rc,cd->rd', pre_grad, w_in_dir, preferred_element_type=F32)  2.25 us
    dot_general x3, matrix products, local(): dh = jnp.einsum('rd,dh->rh', dy, w_down_dir, preferred_element_type=F32)  1.33 us
  transfers between devices with their start and end apart: 25, of which 16 were waited for; matrix products, arithmetic and copies ran while one was open for 3% of the time, Pallas kernels for 16%

profile of v7, /device:TPU:0, one launch (start us, length us, event | category | flops | bytes accessed | tf_op | source)
XLA Modules:
  0.0 64.9 jit_solution(11521669251647906027)
XLA Ops:
  0.6 0.5 collective-permute-start
  1.2 0.4 collective-permute-start.4
  1.7 1.0 %select_bitcast_fusion = f32[8,3584]{1,0:T(8,128)S(1)} fusion(f32[2,1,8,3584]{3,2,1,0:T(8,128)} %param.5, pred[]{:T(512)S(6)} %eq.28), kind=kLoop, calls=%fused_computation.56 | loop fusion | flops 28672 | bytes 344065 | tf_op jit(solution)/shard_map/jit(_where)/select_n | solution.py:144
  2.7 3.7 %collective-permute-start.3 = (bf16[16,3584]{1,0:T(8,128)(2,1)S(1)}, bf16[16,3584]{1,0:T(8,128)(2,1)S(1)}, u32[]{:S(2)}, u32[]{:S(2)}) collective-permute-start(bf16[16,3584]{1,0:T(8,128)(2,1)S(1)} %fusion.9._), channel_id=1, source_target_pairs={{0,6},{2,0},{4,2},{6,4},{1,7},{3,1},{5,3},{7,5},{8,14},{10,8},{12,... | collective-permute-start | bytes 344072 | tf_op jit(solution)/shard_map/ppermute | solution.py:159
  6.4 0.5 collective-permute-start.2
  6.9 0.6 collective-permute-start.1
  7.6 4.6 %factors.1 = (f32[3,64,256]{2,1,0:T(8,128)S(1)}, f32[3,64,256]{2,1,0:T(8,128)S(1)}, bf16[3,64,256]{2,1,0:T(8,128)(2,1)S(1)}, bf16[2,16,3584]{2,1,0:T(8,128)(2,1)...) custom-call(s32[2]{0:T(128)S(1)} %pad_add_fusion.at._, bf16[2,3,1,32,3584]{4,3,2,1,0:T(8,128)(2,1)} %refs_0_.1, ...), custom_call_target="tpu_custom_call" | custom-call | tf_op jit(solution)/shard_map/factors/pallas_call | solution.py:180
  12.2 1.7 %collective-permute-done.2 = bf16[16,3584]{1,0:T(8,128)(2,1)S(1)} collective-permute-done((bf16[16,3584]{1,0:T(8,128)(2,1)S(1)}, bf16[16,3584]{1,0:T(8,128)(2,1)S(1)}, u32[]{:S(2)}, u32[]{:S(2)}) %collective-permute-start.2) | collective-permute-done | bytes 114720 | tf_op jit(solution)/shard_map/ppermute | solution.py:159
  14.0 0.4 fusion.25
  14.4 0.8 %convolution_convert_fusion.2 = bf16[64,3584]{1,0:T(8,128)(2,1)S(1)} fusion(bf16[512,3584]{1,0:T(8,128)(2,1)S(1)} %get-tuple-element.31, bf16[64,256]{1,0:T(8,128)(2,1)S(1)} %get-tuple-element.73, bf16[64,256]{1,0:T(8,128)(2,1)S(1)} %get-tuple-element.72), kind=kOutput, calls=%fused_computation.2 | convolution fusion | flops 235241472 | bytes 4194304 | tf_op jit(solution)/shard_map/rc,cd->rd/dot_general | solution.py:292
  15.2 0.7 %collective-permute-start.6 = (bf16[16,3584]{1,0:T(8,128)(2,1)S(1)}, bf16[16,3584]{1,0:T(8,128)(2,1)S(1)}, u32[]{:S(2)}, u32[]{:S(2)}) collective-permute-start(bf16[16,3584]{1,0:T(8,128)(2,1)S(1)} %get-tuple-element.61), channel_id=1, source_target_pairs={{0,2},{2,4},{4,6},{6,0},{1,3},{3,5},{5,7},{7,1},{8,10},{10,12},{12... | collective-permute-start | bytes 344072 | tf_op jit(solution)/shard_map/ppermute | solution.py:159
  16.0 0.5 collective-permute-start.8
  16.5 2.2 %collective-permute-start.7 = (bf16[16,3584]{1,0:T(8,128)(2,1)S(1)}, bf16[16,3584]{1,0:T(8,128)(2,1)S(1)}, u32[]{:S(2)}, u32[]{:S(2)}) collective-permute-start(bf16[16,3584]{1,0:T(8,128)(2,1)S(1)} %get-tuple-element.63), channel_id=1, source_target_pairs={{0,6},{2,0},{4,2},{6,4},{1,7},{3,1},{5,3},{7,5},{8,14},{10,8},{12,... | collective-permute-start | bytes 344072 | tf_op jit(solution)/shard_map/ppermute | solution.py:159
  18.7 0.1 dynamic_update_slice.53
  18.9 2.9 %collective-permute-done.6 = bf16[16,3584]{1,0:T(8,128)(2,1)S(1)} collective-permute-done((bf16[16,3584]{1,0:T(8,128)(2,1)S(1)}, bf16[16,3584]{1,0:T(8,128)(2,1)S(1)}, u32[]{:S(2)}, u32[]{:S(2)}) %collective-permute-start.6) | collective-permute-done | bytes 114720 | tf_op jit(solution)/shard_map/ppermute | solution.py:159
  21.8 0.9 %collective-permute-done.8 = bf16[16,3584]{1,0:T(8,128)(2,1)S(1)} collective-permute-done((bf16[16,3584]{1,0:T(8,128)(2,1)S(1)}, bf16[16,3584]{1,0:T(8,128)(2,1)S(1)}, u32[]{:S(2)}, u32[]{:S(2)}) %collective-permute-start.8) | collective-permute-done | bytes 114720 | tf_op jit(solution)/shard_map/ppermute | solution.py:159
  22.7 0.1 bitcast_select_fusion.1
  22.9 1.0 %collective-permute-start.11 = (bf16[16,3584]{1,0:T(8,128)(2,1)S(1)}, bf16[16,3584]{1,0:T(8,128)(2,1)S(1)}, u32[]{:S(2)}, u32[]{:S(2)}) collective-permute-start(bf16[16,3584]{1,0:T(8,128)(2,1)S(1)} %get-tuple-element.44), channel_id=1, source_target_pairs={{0,5},{1,13},{2,7},{3,15},{4,1},{5,9},{6,3},{7,11},{8,4},{9,21},{1... | collective-permute-start | bytes 344072 | tf_op jit(solution)/shard_map/ppermute | solution.py:312
  23.9 2.1 %collective-permute-start.10 = (bf16[16,3584]{1,0:T(8,128)(2,1)S(1)}, bf16[16,3584]{1,0:T(8,128)(2,1)S(1)}, u32[]{:S(2)}, u32[]{:S(2)}) collective-permute-start(bf16[16,3584]{1,0:T(8,128)(2,1)S(1)} %get-tuple-element.44), channel_id=1, source_target_pairs={{0,7},{1,15},{2,1},{3,9},{4,3},{5,11},{6,5},{7,13},{8,6},{9,23},{1... | collective-permute-start | bytes 344072 | tf_op jit(solution)/shard_map/ppermute | solution.py:312
  26.0 1.1 %collective-permute-start.9 = (bf16[16,3584]{1,0:T(8,128)(2,1)S(1)}, bf16[16,3584]{1,0:T(8,128)(2,1)S(1)}, u32[]{:S(2)}, u32[]{:S(2)}) collective-permute-start(bf16[16,3584]{1,0:T(8,128)(2,1)S(1)} %get-tuple-element.44), channel_id=1, source_target_pairs={{0,1},{1,9},{2,3},{3,11},{4,5},{5,13},{6,7},{7,15},{8,0},{9,17},{1... | collective-permute-start | bytes 344072 | tf_op jit(solution)/shard_map/ppermute | solution.py:312
  27.1 2.7 %collective-permute-done.12 = bf16[16,3584]{1,0:T(8,128)(2,1)S(1)} collective-permute-done((bf16[16,3584]{1,0:T(8,128)(2,1)S(1)}, bf16[16,3584]{1,0:T(8,128)(2,1)S(1)}, u32[]{:S(2)}, u32[]{:S(2)}) %collective-permute-start.12) | collective-permute-done | bytes 114720 | tf_op jit(solution)/shard_map/ppermute | solution.py:312
  29.8 1.0 %collective-permute-done.11 = bf16[16,3584]{1,0:T(8,128)(2,1)S(1)} collective-permute-done((bf16[16,3584]{1,0:T(8,128)(2,1)S(1)}, bf16[16,3584]{1,0:T(8,128)(2,1)S(1)}, u32[]{:S(2)}, u32[]{:S(2)}) %collective-permute-start.11) | collective-permute-done | bytes 114720 | tf_op jit(solution)/shard_map/ppermute | solution.py:312
  30.8 0.5 collective-permute-done.10
  31.3 1.5 %collective-permute-done.9 = bf16[16,3584]{1,0:T(8,128)(2,1)S(1)} collective-permute-done((bf16[16,3584]{1,0:T(8,128)(2,1)S(1)}, bf16[16,3584]{1,0:T(8,128)(2,1)S(1)}, u32[]{:S(2)}, u32[]{:S(2)}) %collective-permute-start.9) | collective-permute-done | bytes 114720 | tf_op jit(solution)/shard_map/ppermute | solution.py:312
  32.8 0.4 fusion.23
  33.3 0.7 %convolution_convert_fusion.1 = bf16[64,3584]{1,0:T(8,128)(2,1)S(1)} fusion(bf16[512,3584]{1,0:T(8,128)(2,1)S(1)} %get-tuple-element.31, bf16[64,256]{1,0:T(8,128)(2,1)S(1)} %get-tuple-element.71, bf16[64,256]{1,0:T(8,128)(2,1)S(1)} %get-tuple-element.70), kind=kOutput, calls=%fused_computation.1 | convolution fusion | flops 235241472 | bytes 4194304 | tf_op jit(solution)/shard_map/rc,cd->rd/dot_general | solution.py:292
  34.1 0.8 %collective-permute-start.13 = (bf16[16,3584]{1,0:T(8,128)(2,1)S(1)}, bf16[16,3584]{1,0:T(8,128)(2,1)S(1)}, u32[]{:S(2)}, u32[]{:S(2)}) collective-permute-start(bf16[16,3584]{1,0:T(8,128)(2,1)S(1)} %get-tuple-element.54), channel_id=1, source_target_pairs={{0,2},{2,4},{4,6},{6,0},{1,3},{3,5},{5,7},{7,1},{8,10},{10,12},{12... | collective-permute-start | bytes 344072 | tf_op jit(solution)/shard_map/ppermute | solution.py:159
  34.9 1.0 %collective-permute-start.15 = (bf16[16,3584]{1,0:T(8,128)(2,1)S(1)}, bf16[16,3584]{1,0:T(8,128)(2,1)S(1)}, u32[]{:S(2)}, u32[]{:S(2)}) collective-permute-start(bf16[16,3584]{1,0:T(8,128)(2,1)S(1)} %get-tuple-element.55), channel_id=1, source_target_pairs={{0,4},{2,6},{4,0},{6,2},{1,5},{3,7},{5,1},{7,3},{8,12},{10,14},{12... | collective-permute-start | bytes 344072 | tf_op jit(solution)/shard_map/ppermute | solution.py:159
  35.9 2.2 %collective-permute-start.14 = (bf16[16,3584]{1,0:T(8,128)(2,1)S(1)}, bf16[16,3584]{1,0:T(8,128)(2,1)S(1)}, u32[]{:S(2)}, u32[]{:S(2)}) collective-permute-start(bf16[16,3584]{1,0:T(8,128)(2,1)S(1)} %get-tuple-element.56), channel_id=1, source_target_pairs={{0,6},{2,0},{4,2},{6,4},{1,7},{3,1},{5,3},{7,5},{8,14},{10,8},{12,... | collective-permute-start | bytes 344072 | tf_op jit(solution)/shard_map/ppermute | solution.py:159
  38.1 2.9 %collective-permute-done.13 = bf16[16,3584]{1,0:T(8,128)(2,1)S(1)} collective-permute-done((bf16[16,3584]{1,0:T(8,128)(2,1)S(1)}, bf16[16,3584]{1,0:T(8,128)(2,1)S(1)}, u32[]{:S(2)}, u32[]{:S(2)}) %collective-permute-start.13) | collective-permute-done | bytes 114720 | tf_op jit(solution)/shard_map/ppermute | solution.py:159
  41.2 0.5 collective-permute-done.14
  41.7 0.1 bitcast_select_fusion
  41.8 1.6 %collective-permute-start.18 = (bf16[16,3584]{1,0:T(8,128)(2,1)S(1)}, bf16[16,3584]{1,0:T(8,128)(2,1)S(1)}, u32[]{:S(2)}, u32[]{:S(2)}) collective-permute-start(bf16[16,3584]{1,0:T(8,128)(2,1)S(1)} %get-tuple-element.41), channel_id=1, source_target_pairs={{0,5},{1,13},{2,7},{3,15},{4,1},{5,9},{6,3},{7,11},{8,4},{9,21},{1... | collective-permute-start | bytes 344072 | tf_op jit(solution)/shard_map/ppermute | solution.py:312
  43.5 1.8 %collective-permute-start.17 = (bf16[16,3584]{1,0:T(8,128)(2,1)S(1)}, bf16[16,3584]{1,0:T(8,128)(2,1)S(1)}, u32[]{:S(2)}, u32[]{:S(2)}) collective-permute-start(bf16[16,3584]{1,0:T(8,128)(2,1)S(1)} %get-tuple-element.41), channel_id=1, source_target_pairs={{0,7},{1,15},{2,1},{3,9},{4,3},{5,11},{6,5},{7,13},{8,6},{9,23},{1... | collective-permute-start | bytes 344072 | tf_op jit(solution)/shard_map/ppermute | solution.py:312
  45.3 1.6 %collective-permute-start.16 = (bf16[16,3584]{1,0:T(8,128)(2,1)S(1)}, bf16[16,3584]{1,0:T(8,128)(2,1)S(1)}, u32[]{:S(2)}, u32[]{:S(2)}) collective-permute-start(bf16[16,3584]{1,0:T(8,128)(2,1)S(1)} %get-tuple-element.41), channel_id=1, source_target_pairs={{0,1},{1,9},{2,3},{3,11},{4,5},{5,13},{6,7},{7,15},{8,0},{9,17},{1... | collective-permute-start | bytes 344072 | tf_op jit(solution)/shard_map/ppermute | solution.py:312
  46.9 1.6 %collective-permute-done.19 = bf16[16,3584]{1,0:T(8,128)(2,1)S(1)} collective-permute-done((bf16[16,3584]{1,0:T(8,128)(2,1)S(1)}, bf16[16,3584]{1,0:T(8,128)(2,1)S(1)}, u32[]{:S(2)}, u32[]{:S(2)}) %collective-permute-start.19) | collective-permute-done | bytes 114720 | tf_op jit(solution)/shard_map/ppermute | solution.py:312
  48.5 1.2 %collective-permute-done.18 = bf16[16,3584]{1,0:T(8,128)(2,1)S(1)} collective-permute-done((bf16[16,3584]{1,0:T(8,128)(2,1)S(1)}, bf16[16,3584]{1,0:T(8,128)(2,1)S(1)}, u32[]{:S(2)}, u32[]{:S(2)}) %collective-permute-start.18) | collective-permute-done | bytes 114720 | tf_op jit(solution)/shard_map/ppermute | solution.py:312
  49.8 0.8 %collective-permute-done.17 = bf16[16,3584]{1,0:T(8,128)(2,1)S(1)} collective-permute-done((bf16[16,3584]{1,0:T(8,128)(2,1)S(1)}, bf16[16,3584]{1,0:T(8,128)(2,1)S(1)}, u32[]{:S(2)}, u32[]{:S(2)}) %collective-permute-start.17) | collective-permute-done | bytes 114720 | tf_op jit(solution)/shard_map/ppermute | solution.py:312
  50.5 1.4 %collective-permute-done.16 = bf16[16,3584]{1,0:T(8,128)(2,1)S(1)} collective-permute-done((bf16[16,3584]{1,0:T(8,128)(2,1)S(1)}, bf16[16,3584]{1,0:T(8,128)(2,1)S(1)}, u32[]{:S(2)}, u32[]{:S(2)}) %collective-permute-start.16) | collective-permute-done | bytes 114720 | tf_op jit(solution)/shard_map/ppermute | solution.py:312
  52.0 0.4 fusion.21
  52.7 0.7 %convolution_convert_fusion = bf16[64,3584]{1,0:T(8,128)(2,1)S(1)} fusion(bf16[512,3584]{1,0:T(8,128)(2,1)S(1)} %get-tuple-element.31, bf16[64,256]{1,0:T(8,128)(2,1)S(1)} %get-tuple-element.69, bf16[64,256]{1,0:T(8,128)(2,1)S(1)} %get-tuple-element.68), kind=kOutput, calls=%fused_computation | convolution fusion | flops 235241472 | bytes 4194304 | tf_op jit(solution)/shard_map/rc,cd->rd/dot_general | solution.py:292
  53.5 1.3 %collective-permute-start.22 = (bf16[16,3584]{1,0:T(8,128)(2,1)S(1)}, bf16[16,3584]{1,0:T(8,128)(2,1)S(1)}, u32[]{:S(2)}, u32[]{:S(2)}) collective-permute-start(bf16[16,3584]{1,0:T(8,128)(2,1)S(1)} %get-tuple-element.47), channel_id=1, source_target_pairs={{0,6},{2,0},{4,2},{6,4},{1,7},{3,1},{5,3},{7,5},{8,14},{10,8},{12,... | collective-permute-start | bytes 344072 | tf_op jit(solution)/shard_map/ppermute | solution.py:159
  54.8 0.9 %collective-permute-start.21 = (bf16[16,3584]{1,0:T(8,128)(2,1)S(1)}, bf16[16,3584]{1,0:T(8,128)(2,1)S(1)}, u32[]{:S(2)}, u32[]{:S(2)}) collective-permute-start(bf16[16,3584]{1,0:T(8,128)(2,1)S(1)} %get-tuple-element.48), channel_id=1, source_target_pairs={{0,4},{2,6},{4,0},{6,2},{1,5},{3,7},{5,1},{7,3},{8,12},{10,14},{12... | collective-permute-start | bytes 344072 | tf_op jit(solution)/shard_map/ppermute | solution.py:159
  55.7 0.8 %collective-permute-start.20 = (bf16[16,3584]{1,0:T(8,128)(2,1)S(1)}, bf16[16,3584]{1,0:T(8,128)(2,1)S(1)}, u32[]{:S(2)}, u32[]{:S(2)}) collective-permute-start(bf16[16,3584]{1,0:T(8,128)(2,1)S(1)} %get-tuple-element.49), channel_id=1, source_target_pairs={{0,2},{2,4},{4,6},{6,0},{1,3},{3,5},{5,7},{7,1},{8,10},{10,12},{12... | collective-permute-start | bytes 344072 | tf_op jit(solution)/shard_map/ppermute | solution.py:159
  56.5 5.9 %weight_grads.1 = (f32[2,1,1792,512]{3,2,1,0:T(8,128)}, f32[2,1,256,1792]{3,2,1,0:T(8,128)}) custom-call(s32[2]{0:T(128)S(1)} %pad_add_fusion.at._, bf16[2,3,1,32,3584]{4,3,2,1,0:T(8,128)(2,1)S(1)} %copy-done, bf16[2,3,1,32,3584]{4,3,2,1,0:T(8,128)(2,1)S(1)} %collective-permute-done.4.peer_ref.refs_1_, bf16[208,4480]{1,0:T(8,128)(2,1)S(1)} %fusion.27.refs_2_.refs_4_, ...), custom_call_target="tpu_custom_call" | custom-call | tf_op jit(solution)/shard_map/weight_grads/pallas_call | solution.py:238
  62.4 0.2 collective-permute-done.21
  62.8 1.2 %collective-permute-done.24 = f32[8,3584]{1,0:T(8,128)S(1)} collective-permute-done((f32[8,3584]{1,0:T(8,128)S(1)}, f32[8,3584]{1,0:T(8,128)S(1)}, u32[]{:S(2)}, u32[]{:S(2)}) %collective-permute-start.24) | collective-permute-done | bytes 114720 | tf_op jit(solution)/shard_map/ppermute | solution.py:156
  64.1 0.8 %copy-done.2 = f32[2,3,1,8,3584]{4,3,2,1,0:T(8,128)} copy-done((f32[2,3,1,8,3584]{4,3,2,1,0:T(8,128)}, f32[2,3,1,8,3584]{4,3,2,1,0:T(8,128)S(1)}, u32[]{:S(2)}) %copy-start.2) | copy-done | bytes 688152
  (46 shorter events, 1.2 us)
Async XLA Ops:
  0.6 2.0 %collective-permute-start = (f32[2,1,8,3584]{3,2,1,0:T(8,128)}, f32[2,1,8,3584]{3,2,1,0:T(8,128)S(1)}, u32[]{:S(2)}, u32[]{:S(2)}) collective-permute-start(f32[2,1,8,3584]{3,2,1,0:T(8,128)} %param.5), channel_id=1, source_target_pairs={{0,1},{1,0},{2,3},{3,2},{4,5},{5,4},{6,7},{7,6},{8,9},{9,8},{10,11... | collective-permute-start | bytes 688136 | tf_op jit(solution)/shard_map/ppermute | solution.py:156
  1.1 6.4 %collective-permute-start.5 = (f32[2,2,8,3584]{3,2,1,0:T(8,128)}, f32[2,2,8,3584]{3,2,1,0:T(8,128)S(1)}, u32[]{:S(2)}, u32[]{:S(2)}) collective-permute-start(f32[2,2,8,3584]{3,2,1,0:T(8,128)} %fresh_ref.1), channel_id=1, source_target_pairs={{0,1},{1,0},{2,3},{3,2},{4,5},{5,4},{6,7},{7,6},{8,9},{9,8},{10,11... | collective-permute-start | bytes 1376264 | tf_op jit(solution)/shard_map/ppermute | solution.py:156
  1.2 6.3 %collective-permute-start.4 = (bf16[2,3,1,32,3584]{4,3,2,1,0:T(8,128)(2,1)}, bf16[2,3,1,32,3584]{4,3,2,1,0:T(8,128)(2,1)S(1)}, u32[]{:S(2)}, u32[]{:S(2)}) collective-permute-start(bf16[2,3,1,32,3584]{4,3,2,1,0:T(8,128)(2,1)} %refs_0_.1), channel_id=1, source_target_pairs={{0,1},{1,0},{2,3},{3,2},{4,5},{5,4},{6,7},{7,6},{8,9},{9,8},{10,11... | collective-permute-start | bytes 4128776 | tf_op jit(solution)/shard_map/ppermute | solution.py:156
  2.7 9.5 %collective-permute-start.3 = (bf16[16,3584]{1,0:T(8,128)(2,1)S(1)}, bf16[16,3584]{1,0:T(8,128)(2,1)S(1)}, u32[]{:S(2)}, u32[]{:S(2)}) collective-permute-start(bf16[16,3584]{1,0:T(8,128)(2,1)S(1)} %fusion.9._), channel_id=1, source_target_pairs={{0,6},{2,0},{4,2},{6,4},{1,7},{3,1},{5,3},{7,5},{8,14},{10,8},{12,... | collective-permute-start | bytes 344072 | tf_op jit(solution)/shard_map/ppermute | solution.py:159
  6.4 7.6 %collective-permute-start.2 = (bf16[16,3584]{1,0:T(8,128)(2,1)S(1)}, bf16[16,3584]{1,0:T(8,128)(2,1)S(1)}, u32[]{:S(2)}, u32[]{:S(2)}) collective-permute-start(bf16[16,3584]{1,0:T(8,128)(2,1)S(1)} %fusion.9._), channel_id=1, source_target_pairs={{0,4},{2,6},{4,0},{6,2},{1,5},{3,7},{5,1},{7,3},{8,12},{10,14},{12... | collective-permute-start | bytes 344072 | tf_op jit(solution)/shard_map/ppermute | solution.py:159
  6.9 7.0 %collective-permute-start.1 = (bf16[16,3584]{1,0:T(8,128)(2,1)S(1)}, bf16[16,3584]{1,0:T(8,128)(2,1)S(1)}, u32[]{:S(2)}, u32[]{:S(2)}) collective-permute-start(bf16[16,3584]{1,0:T(8,128)(2,1)S(1)} %fusion.9._), channel_id=1, source_target_pairs={{0,2},{2,4},{4,6},{6,0},{1,3},{3,5},{5,7},{7,1},{8,10},{10,12},{12... | collective-permute-start | bytes 344072 | tf_op jit(solution)/shard_map/ppermute | solution.py:159
  15.2 6.6 %collective-permute-start.6 = (bf16[16,3584]{1,0:T(8,128)(2,1)S(1)}, bf16[16,3584]{1,0:T(8,128)(2,1)S(1)}, u32[]{:S(2)}, u32[]{:S(2)}) collective-permute-start(bf16[16,3584]{1,0:T(8,128)(2,1)S(1)} %get-tuple-element.61), channel_id=1, source_target_pairs={{0,2},{2,4},{4,6},{6,0},{1,3},{3,5},{5,7},{7,1},{8,10},{10,12},{12... | collective-permute-start | bytes 344072 | tf_op jit(solution)/shard_map/ppermute | solution.py:159
  16.0 6.7 %collective-permute-start.8 = (bf16[16,3584]{1,0:T(8,128)(2,1)S(1)}, bf16[16,3584]{1,0:T(8,128)(2,1)S(1)}, u32[]{:S(2)}, u32[]{:S(2)}) collective-permute-start(bf16[16,3584]{1,0:T(8,128)(2,1)S(1)} %get-tuple-element.62), channel_id=1, source_target_pairs={{0,4},{2,6},{4,0},{6,2},{1,5},{3,7},{5,1},{7,3},{8,12},{10,14},{12... | collective-permute-start | bytes 344072 | tf_op jit(solution)/shard_map/ppermute | solution.py:159
  16.5 6.2 %collective-permute-start.7 = (bf16[16,3584]{1,0:T(8,128)(2,1)S(1)}, bf16[16,3584]{1,0:T(8,128)(2,1)S(1)}, u32[]{:S(2)}, u32[]{:S(2)}) collective-permute-start(bf16[16,3584]{1,0:T(8,128)(2,1)S(1)} %get-tuple-element.63), channel_id=1, source_target_pairs={{0,6},{2,0},{4,2},{6,4},{1,7},{3,1},{5,3},{7,5},{8,14},{10,8},{12,... | collective-permute-start | bytes 344072 | tf_op jit(solution)/shard_map/ppermute | solution.py:159
  22.8 7.0 %collective-permute-start.12 = (bf16[16,3584]{1,0:T(8,128)(2,1)S(1)}, bf16[16,3584]{1,0:T(8,128)(2,1)S(1)}, u32[]{:S(2)}, u32[]{:S(2)}) collective-permute-start(bf16[16,3584]{1,0:T(8,128)(2,1)S(1)} %get-tuple-element.44), channel_id=1, source_target_pairs={{0,3},{1,11},{2,5},{3,13},{4,7},{5,15},{6,1},{7,9},{8,2},{9,19},{1... | collective-permute-start | bytes 344072 | tf_op jit(solution)/shard_map/ppermute | solution.py:312
  22.9 7.9 %collective-permute-start.11 = (bf16[16,3584]{1,0:T(8,128)(2,1)S(1)}, bf16[16,3584]{1,0:T(8,128)(2,1)S(1)}, u32[]{:S(2)}, u32[]{:S(2)}) collective-permute-start(bf16[16,3584]{1,0:T(8,128)(2,1)S(1)} %get-tuple-element.44), channel_id=1, source_target_pairs={{0,5},{1,13},{2,7},{3,15},{4,1},{5,9},{6,3},{7,11},{8,4},{9,21},{1... | collective-permute-start | bytes 344072 | tf_op jit(solution)/shard_map/ppermute | solution.py:312
  23.9 7.4 %collective-permute-start.10 = (bf16[16,3584]{1,0:T(8,128)(2,1)S(1)}, bf16[16,3584]{1,0:T(8,128)(2,1)S(1)}, u32[]{:S(2)}, u32[]{:S(2)}) collective-permute-start(bf16[16,3584]{1,0:T(8,128)(2,1)S(1)} %get-tuple-element.44), channel_id=1, source_target_pairs={{0,7},{1,15},{2,1},{3,9},{4,3},{5,11},{6,5},{7,13},{8,6},{9,23},{1... | collective-permute-start | bytes 344072 | tf_op jit(solution)/shard_map/ppermute | solution.py:312
  26.0 6.8 %collective-permute-start.9 = (bf16[16,3584]{1,0:T(8,128)(2,1)S(1)}, bf16[16,3584]{1,0:T(8,128)(2,1)S(1)}, u32[]{:S(2)}, u32[]{:S(2)}) collective-permute-start(bf16[16,3584]{1,0:T(8,128)(2,1)S(1)} %get-tuple-element.44), channel_id=1, source_target_pairs={{0,1},{1,9},{2,3},{3,11},{4,5},{5,13},{6,7},{7,15},{8,0},{9,17},{1... | collective-permute-start | bytes 344072 | tf_op jit(solution)/shard_map/ppermute | solution.py:312
  34.1 7.0 %collective-permute-start.13 = (bf16[16,3584]{1,0:T(8,128)(2,1)S(1)}, bf16[16,3584]{1,0:T(8,128)(2,1)S(1)}, u32[]{:S(2)}, u32[]{:S(2)}) collective-permute-start(bf16[16,3584]{1,0:T(8,128)(2,1)S(1)} %get-tuple-element.54), channel_id=1, source_target_pairs={{0,2},{2,4},{4,6},{6,0},{1,3},{3,5},{5,7},{7,1},{8,10},{10,12},{12... | collective-permute-start | bytes 344072 | tf_op jit(solution)/shard_map/ppermute | solution.py:159
  34.9 6.3 %collective-permute-start.15 = (bf16[16,3584]{1,0:T(8,128)(2,1)S(1)}, bf16[16,3584]{1,0:T(8,128)(2,1)S(1)}, u32[]{:S(2)}, u32[]{:S(2)}) collective-permute-start(bf16[16,3584]{1,0:T(8,128)(2,1)S(1)} %get-tuple-element.55), channel_id=1, source_target_pairs={{0,4},{2,6},{4,0},{6,2},{1,5},{3,7},{5,1},{7,3},{8,12},{10,14},{12... | collective-permute-start | bytes 344072 | tf_op jit(solution)/shard_map/ppermute | solution.py:159
  35.9 5.7 %collective-permute-start.14 = (bf16[16,3584]{1,0:T(8,128)(2,1)S(1)}, bf16[16,3584]{1,0:T(8,128)(2,1)S(1)}, u32[]{:S(2)}, u32[]{:S(2)}) collective-permute-start(bf16[16,3584]{1,0:T(8,128)(2,1)S(1)} %get-tuple-element.56), channel_id=1, source_target_pairs={{0,6},{2,0},{4,2},{6,4},{1,7},{3,1},{5,3},{7,5},{8,14},{10,8},{12,... | collective-permute-start | bytes 344072 | tf_op jit(solution)/shard_map/ppermute | solution.py:159
  41.8 6.7 %collective-permute-start.19 = (bf16[16,3584]{1,0:T(8,128)(2,1)S(1)}, bf16[16,3584]{1,0:T(8,128)(2,1)S(1)}, u32[]{:S(2)}, u32[]{:S(2)}) collective-permute-start(bf16[16,3584]{1,0:T(8,128)(2,1)S(1)} %get-tuple-element.41), channel_id=1, source_target_pairs={{0,3},{1,11},{2,5},{3,13},{4,7},{5,15},{6,1},{7,9},{8,2},{9,19},{1... | collective-permute-start | bytes 344072 | tf_op jit(solution)/shard_map/ppermute | solution.py:312
  41.8 7.9 %collective-permute-start.18 = (bf16[16,3584]{1,0:T(8,128)(2,1)S(1)}, bf16[16,3584]{1,0:T(8,128)(2,1)S(1)}, u32[]{:S(2)}, u32[]{:S(2)}) collective-permute-start(bf16[16,3584]{1,0:T(8,128)(2,1)S(1)} %get-tuple-element.41), channel_id=1, source_target_pairs={{0,5},{1,13},{2,7},{3,15},{4,1},{5,9},{6,3},{7,11},{8,4},{9,21},{1... | collective-permute-start | bytes 344072 | tf_op jit(solution)/shard_map/ppermute | solution.py:312
  43.5 7.1 %collective-permute-start.17 = (bf16[16,3584]{1,0:T(8,128)(2,1)S(1)}, bf16[16,3584]{1,0:T(8,128)(2,1)S(1)}, u32[]{:S(2)}, u32[]{:S(2)}) collective-permute-start(bf16[16,3584]{1,0:T(8,128)(2,1)S(1)} %get-tuple-element.41), channel_id=1, source_target_pairs={{0,7},{1,15},{2,1},{3,9},{4,3},{5,11},{6,5},{7,13},{8,6},{9,23},{1... | collective-permute-start | bytes 344072 | tf_op jit(solution)/shard_map/ppermute | solution.py:312
  45.3 6.7 %collective-permute-start.16 = (bf16[16,3584]{1,0:T(8,128)(2,1)S(1)}, bf16[16,3584]{1,0:T(8,128)(2,1)S(1)}, u32[]{:S(2)}, u32[]{:S(2)}) collective-permute-start(bf16[16,3584]{1,0:T(8,128)(2,1)S(1)} %get-tuple-element.41), channel_id=1, source_target_pairs={{0,1},{1,9},{2,3},{3,11},{4,5},{5,13},{6,7},{7,15},{8,0},{9,17},{1... | collective-permute-start | bytes 344072 | tf_op jit(solution)/shard_map/ppermute | solution.py:312
  52.5 3.9 %collective-permute-start.23 = (bf16[208,4480]{1,0:T(8,128)(2,1)S(1)}, bf16[208,4480]{1,0:T(8,128)(2,1)S(1)}, u32[]{:S(2)}, u32[]{:S(2)}) collective-permute-start(bf16[208,4480]{1,0:T(8,128)(2,1)S(1)} %fusion.27.refs_2_.refs_4_), channel_id=1, source_target_pairs={{0,1},{1,0},{2,3},{3,2},{4,5},{5,4},{6,7},{7,6},{8,9},{9,8},{10,11... | collective-permute-start | bytes 5591048 | tf_op jit(solution)/shard_map/ppermute | solution.py:156
  52.7 3.8 %copy-start = (bf16[2,3,1,32,3584]{4,3,2,1,0:T(8,128)(2,1)S(1)}, bf16[2,3,1,32,3584]{4,3,2,1,0:T(8,128)(2,1)}, u32[]{:S(2)}) copy-start(bf16[2,3,1,32,3584]{4,3,2,1,0:T(8,128)(2,1)} %refs_0_.1) | copy-start | bytes 4128772
  53.5 8.8 %collective-permute-start.22 = (bf16[16,3584]{1,0:T(8,128)(2,1)S(1)}, bf16[16,3584]{1,0:T(8,128)(2,1)S(1)}, u32[]{:S(2)}, u32[]{:S(2)}) collective-permute-start(bf16[16,3584]{1,0:T(8,128)(2,1)S(1)} %get-tuple-element.47), channel_id=1, source_target_pairs={{0,6},{2,0},{4,2},{6,4},{1,7},{3,1},{5,3},{7,5},{8,14},{10,8},{12,... | collective-permute-start | bytes 344072 | tf_op jit(solution)/shard_map/ppermute | solution.py:159
  54.8 7.7 %collective-permute-start.21 = (bf16[16,3584]{1,0:T(8,128)(2,1)S(1)}, bf16[16,3584]{1,0:T(8,128)(2,1)S(1)}, u32[]{:S(2)}, u32[]{:S(2)}) collective-permute-start(bf16[16,3584]{1,0:T(8,128)(2,1)S(1)} %get-tuple-element.48), channel_id=1, source_target_pairs={{0,4},{2,6},{4,0},{6,2},{1,5},{3,7},{5,1},{7,3},{8,12},{10,14},{12... | collective-permute-start | bytes 344072 | tf_op jit(solution)/shard_map/ppermute | solution.py:159
  55.7 6.9 %collective-permute-start.20 = (bf16[16,3584]{1,0:T(8,128)(2,1)S(1)}, bf16[16,3584]{1,0:T(8,128)(2,1)S(1)}, u32[]{:S(2)}, u32[]{:S(2)}) collective-permute-start(bf16[16,3584]{1,0:T(8,128)(2,1)S(1)} %get-tuple-element.49), channel_id=1, source_target_pairs={{0,2},{2,4},{4,6},{6,0},{1,3},{3,5},{5,7},{7,1},{8,10},{10,12},{12... | collective-permute-start | bytes 344072 | tf_op jit(solution)/shard_map/ppermute | solution.py:159
  56.5 6.3 %copy-start.1 = (f32[2,1,8,3584]{3,2,1,0:T(8,128)S(1)}, f32[2,1,8,3584]{3,2,1,0:T(8,128)}, u32[]{:S(2)}) copy-start(f32[2,1,8,3584]{3,2,1,0:T(8,128)} %param.5) | copy-start | bytes 688132
  62.7 1.4 %collective-permute-start.24 = (f32[8,3584]{1,0:T(8,128)S(1)}, f32[8,3584]{1,0:T(8,128)S(1)}, u32[]{:S(2)}, u32[]{:S(2)}) collective-permute-start(f32[8,3584]{1,0:T(8,128)S(1)} %slice.97), channel_id=1, source_target_pairs={{0,1},{1,0},{2,3},{3,2},{4,5},{5,4},{6,7},{7,6},{8,9},{9,8},{10,11... | collective-permute-start | bytes 344072 | tf_op jit(solution)/shard_map/ppermute | solution.py:156
  64.1 0.9 %copy-start.2 = (f32[2,3,1,8,3584]{4,3,2,1,0:T(8,128)}, f32[2,3,1,8,3584]{4,3,2,1,0:T(8,128)S(1)}, u32[]{:S(2)}) copy-start(f32[2,3,1,8,3584]{4,3,2,1,0:T(8,128)S(1)} %bitcast_dynamic-update-slice_fusion) | copy-start | bytes 2064388
